TPU v7x, 512 devices: a whole 4x8x8 slice. The times are simulated.
512 devices in a mesh: section: 16 (over y, core), tp: 16 (over x_lo, z), rep: 2 (over x_hi).
Axes of the slice: x: 4 (x_hi: 2, x_lo: 2; x = x_hi * 2 + x_lo), y: 8, z: 8, core: 2. Of those that a mesh axis runs over, the one named last changes fastest.
Arguments:
- student_noise: float32 [2, 3072, 64], P('rep', 'section'), may hold values from -10 to 10
- renoise_noise: float32 [2, 3072, 64], P('rep', 'section'), may hold values from -10 to 10
- patch_slot: int32 [2, 3072], P('rep', 'section'), may hold values from 0 to 3071, each once within a row
- renoise_step: int32 [2], P('rep'), may hold values from 20 to 979
- prompt_ids: int32 [2, 256], P('rep'), may hold values from 0 to 31999
- text_table: bfloat16 [32000, 2432], P(('section', 'tp')), may hold values from -48 to 48
- student_in: bfloat16 [64, 2432], replicated, may hold values from -0.75 to 0.75
- student_qkv: bfloat16 [2432, 3, 2048], P('section', None, 'tp'), may hold values from -2 to 2
- student_out: bfloat16 [2432, 2048], P('section', 'tp'), may hold values from -0.375 to 0.375
- student_final: bfloat16 [2432, 64], replicated, may hold values from -0.125 to 0.125
- real_in: bfloat16 [64, 2432], replicated, may hold values from -0.75 to 0.75
- real_qkv: bfloat16 [2432, 3, 2048], P('section', None, 'tp'), may hold values from -2 to 2
- real_out: bfloat16 [2432, 2048], P('section', 'tp'), may hold values from -0.375 to 0.375
- real_final: bfloat16 [2432, 64], replicated, may hold values from -0.125 to 0.125
- fake_in: bfloat16 [64, 2432], replicated, may hold values from -0.75 to 0.75
- fake_qkv: bfloat16 [2432, 3, 2048], P('section', None, 'tp'), may hold values from -2 to 2
- fake_out: bfloat16 [2432, 2048], P('section', 'tp'), may hold values from -0.375 to 0.375
- fake_final: bfloat16 [2432, 64], replicated, may hold values from -0.125 to 0.125
Outputs:
- latent_grad: float32 [2, 3072, 64], P('rep', 'section')
All inputs are finite; a program needn't handle non-finite values. Where the computation divides by a largest or mean magnitude, that divisor is 1e-20 or more.
Results may differ from a plain program's by a relative error of at most 0.03.
Values may be sent and summed in bfloat16 or wider, within the bound.
No kernel may reach another device: no remote copies, remote signals or barrier semaphores. Data moves between devices by JAX's collectives and lax.ppermute only.
A program may use at most 64 MiB of HBM per device.

v0:
```python
import math

import jax
import jax.numpy as jnp
from jax import lax
from jax.sharding import PartitionSpec as P

D = 2432
HD = 64
GRID_W = 64


def time_embed(step_time):
    half_width = D // 2
    frequency = jnp.exp(-math.log(10000.0) * jnp.arange(half_width, dtype=jnp.float32) / half_width)
    angles = 1000.0 * step_time * frequency
    return jnp.concatenate([jnp.cos(angles), jnp.sin(angles)])


def place_embed(slots):
    quarter = D // 4
    frequency = jnp.exp(-math.log(10000.0) * jnp.arange(quarter, dtype=jnp.float32) / quarter)
    row_angle = (slots // GRID_W).astype(jnp.float32)[:, None] * frequency[None, :]
    col_angle = (slots % GRID_W).astype(jnp.float32)[:, None] * frequency[None, :]
    return jnp.concatenate(
        [jnp.sin(row_angle), jnp.cos(row_angle), jnp.sin(col_angle), jnp.cos(col_angle)], axis=1
    )


def rms_norm(values):
    return values * lax.rsqrt(jnp.mean(values * values, axis=-1, keepdims=True) + 1e-06)


def final_layer(after, w_final):
    return jnp.einsum(
        "ntd,ndc->ntc",
        rms_norm(after).astype(jnp.bfloat16),
        w_final,
        preferred_element_type=jnp.float32,
    )


def networks(latents, step_times, condition, w_in, w_qkv, w_out, w_final):
    count = latents.shape[0]
    tok_local = latents.shape[1]
    head_cols = w_out.shape[2]
    local_heads = head_cols // HD
    hidden = jnp.einsum(
        "ntc,ncd->ntd", latents.astype(jnp.bfloat16), w_in, preferred_element_type=jnp.float32
    )
    hidden = hidden + condition[None, :, :] + jax.vmap(time_embed)(step_times)[:, None, :]
    normed = rms_norm(hidden).astype(jnp.bfloat16)
    projected = jnp.einsum(
        "ntd,dnkc->ntkc",
        normed,
        lax.all_gather(w_qkv, "section", axis=0, tiled=True),
        preferred_element_type=jnp.float32,
    )
    projected = projected.astype(jnp.bfloat16)
    queries = projected[:, :, 0].reshape(count, tok_local, local_heads, HD)
    keys_local = projected[:, :, 1]
    values_local = projected[:, :, 2]
    row_max = jnp.full((count, local_heads, tok_local), -1e30, jnp.float32)
    key_block = lax.all_gather(keys_local, "section", axis=1, tiled=True)
    value_block = lax.all_gather(values_local, "section", axis=1, tiled=True)
    key_count = key_block.shape[1]
    key_heads = key_block.reshape(count, key_count, local_heads, HD)
    value_heads = value_block.reshape(count, key_count, local_heads, HD)
    scores = jnp.einsum(
        "nqhd,nkhd->nhqk", queries, key_heads, preferred_element_type=jnp.float32
    ) * HD ** (-0.5)
    new_max = jnp.maximum(row_max, jnp.max(scores, axis=3))
    expo = jnp.exp(scores - new_max[..., None])
    totals = jnp.sum(expo, axis=3)
    running = jnp.einsum(
        "nhqk,nkhd->nhqd",
        expo.astype(jnp.bfloat16),
        value_heads,
        preferred_element_type=jnp.float32,
    )
    row_max, totals, running = (new_max, totals, running)
    mixed = (running / totals[..., None]).astype(jnp.bfloat16)
    mixed = mixed.transpose(0, 2, 1, 3).reshape(count, tok_local, head_cols)
    group_terms = jnp.einsum(
        "ntc,rnc->ntr",
        mixed,
        lax.all_gather(w_out, "section", axis=0, tiled=True),
        preferred_element_type=jnp.float32,
    )
    attended = lax.psum(group_terms.astype(jnp.bfloat16), "tp").astype(jnp.float32)
    return final_layer(hidden + attended, w_final)


def per_device(
    student_noise,
    renoise_noise,
    patch_slot,
    renoise_step,
    prompt_ids,
    text_table,
    student_in,
    student_qkv,
    student_out,
    student_final,
    real_in,
    real_qkv,
    real_out,
    real_final,
    fake_in,
    fake_qkv,
    fake_out,
    fake_final,
):
    vocab_local = text_table.shape[0]
    first_row = lax.axis_index(("section", "tp")) * vocab_local
    prompt_row = prompt_ids[0] - first_row
    matches = (prompt_row[:, None] == jnp.arange(vocab_local, dtype=jnp.int32)[None, :]).astype(
        jnp.bfloat16
    )
    counts = jnp.sum(matches.astype(jnp.float32), axis=0).astype(jnp.bfloat16)
    partial_pool = jnp.dot(counts, text_table, preferred_element_type=jnp.float32)
    pooled = lax.psum(partial_pool, ("section", "tp")) / prompt_ids.shape[1]
    condition = place_embed(patch_slot[0]) + pooled[None, :]
    start_noise = student_noise[0]
    velocity = networks(
        start_noise[None],
        jnp.ones((1,), jnp.float32),
        condition,
        student_in[None],
        student_qkv[:, None],
        student_out[:, None],
        student_final[None],
    )[0]
    clean = start_noise - velocity
    step_time = renoise_step[0].astype(jnp.float32) / 1000.0
    noisy = (1.0 - step_time) * clean + step_time * renoise_noise[0]
    step_row = jnp.full((1,), step_time, jnp.float32)
    real_velocity = networks(
        noisy[None],
        step_row,
        condition,
        real_in[None],
        real_qkv[:, None],
        real_out[:, None],
        real_final[None],
    )[0]
    fake_velocity = networks(
        noisy[None],
        step_row,
        condition,
        fake_in[None],
        fake_qkv[:, None],
        fake_out[:, None],
        fake_final[None],
    )[0]
    pred_real = noisy - step_time * real_velocity
    pred_fake = noisy - step_time * fake_velocity
    local_spread = jnp.sum(jnp.abs(clean - pred_real))
    entries = noisy.shape[0] * lax.axis_size("section") * noisy.shape[1]
    spread = lax.psum(local_spread, "section") / entries + 1e-05
    return ((pred_fake - pred_real) / spread)[None]


def solution(mesh):
    placed = (
        P("rep", "section", None),
        P("rep", "section", None),
        P("rep", "section"),
        P("rep"),
        P("rep", None),
        P(("section", "tp"), None),
        P(),
        P("section", None, "tp"),
        P("section", "tp"),
        P(),
        P(),
        P("section", None, "tp"),
        P("section", "tp"),
        P(),
        P(),
        P("section", None, "tp"),
        P("section", "tp"),
        P(),
    )
    return jax.shard_map(
        per_device, mesh=mesh, in_specs=placed, out_specs=P("rep", "section", None), check_vma=False
    )
```

profile of v0, /device:TPU:1, one launch (start us, length us, event | category | flops | bytes accessed | tf_op | source)
XLA Modules:
  0.0 1666.7 jit_solution(2946937500462225519)
XLA Ops:
  8.0 3.5 multiply_cosine_fusion
  13.9 1085.0 %psum.35 = f32[2432]{0:T(1024)S(1)} all-reduce(f32[2432]{0:T(1024)S(1)} %convolution_reduce_fusion), channel_id=1, replica_groups=mesh['section'=16,'tp'=16,'rep'=2] {'section','tp'}, use_global_device_ids=true, to_apply=%region_1.0 | all-reduce | flops 2432 | bytes 19456 | tf_op jit(solution)/shard_map/psum | solution.py:122
  1101.1 41.5 %all-gather.3 = bf16[2432,128]{1,0:T(8,128)(2,1)} all-gather(bf16[152,128]{1,0:T(8,128)(2,1)S(1)} %copy-done.22), channel_id=5, replica_groups=mesh['section'=16,'tp'=16,'rep'=2] {'section'}, dimensions={0}, use_global_device_ids=true | all-gather | bytes 661504 | tf_op jit(solution)/shard_map/all_gather | solution.py:87
  1144.8 19.5 %all-gather.1 = bf16[1,3072,1,128]{3,1,2,0:T(8,128)(2,1)} all-gather(bf16[1,192,1,128]{3,1,2,0:T(8,128)(2,1)S(1)} %get-tuple-element.13), channel_id=3, replica_groups=mesh['section'=16,'tp'=16,'rep'=2] {'section'}, dimensions={1}, use_global_device_ids=true | all-gather | bytes 835584 | tf_op jit(solution)/shard_map/all_gather | solution.py:64
  1165.8 2.9 fusion.91
  1168.7 18.0 %all-gather.2 = bf16[1,3072,1,128]{3,1,2,0:T(8,128)(2,1)} all-gather(bf16[1,192,1,128]{3,1,2,0:T(8,128)(2,1)S(1)} %get-tuple-element.14), channel_id=4, replica_groups=mesh['section'=16,'tp'=16,'rep'=2] {'section'}, dimensions={1}, use_global_device_ids=true | all-gather | bytes 835584 | tf_op jit(solution)/shard_map/all_gather | solution.py:65
  1188.1 3.3 fusion
  1196.6 18.9 %all-gather.11 = bf16[2432,128]{1,0:T(8,128)(2,1)} all-gather(bf16[152,128]{1,0:T(8,128)(2,1)S(1)} %copy-done.23), channel_id=13, replica_groups=mesh['section'=16,'tp'=16,'rep'=2] {'section'}, dimensions={0}, use_global_device_ids=true | all-gather | bytes 661504 | tf_op jit(solution)/shard_map/all_gather | solution.py:87
  1215.5 17.9 %all-gather.7 = bf16[2432,128]{1,0:T(8,128)(2,1)} all-gather(bf16[152,128]{1,0:T(8,128)(2,1)S(1)} %copy-done.24), channel_id=9, replica_groups=mesh['section'=16,'tp'=16,'rep'=2] {'section'}, dimensions={0}, use_global_device_ids=true | all-gather | bytes 661504 | tf_op jit(solution)/shard_map/all_gather | solution.py:87
  1233.5 86.8 %all-reduce.4.cloned.1.call-done = bf16[1,192,2432]{2,1,0:T(8,128)(2,1)} async-done(((bf16[1,192,2432]{2,1,0:T(8,128)(2,1)}), bf16[1,192,2432]{2,1,0:T(8,128)(2,1)}) %all-reduce.4.cloned.1.call-update) | async-done | bytes 933904 | tf_op jit(solution)/shard_map/psum | solution.py:90
  1324.0 47.4 %all-gather.20.cloned.1.call-done = bf16[2432,3,128]{2,0,1:T(8,128)(2,1)} async-done(((bf16[152,3,128]{2,0,1:T(8,128)(2,1)}), bf16[2432,3,128]{2,0,1:T(8,128)(2,1)}) %all-gather.20.cloned.1.call-update) | async-done | bytes 1867792 | tf_op jit(solution)/shard_map/all_gather | solution.py:56
  1373.7 18.8 %all-gather.9 = bf16[1,3072,1,128]{3,1,2,0:T(8,128)(2,1)S(1)} all-gather(bf16[1,192,1,128]{3,1,2,0:T(8,128)(2,1)S(1)} %get-tuple-element.7), channel_id=11, replica_groups=mesh['section'=16,'tp'=16,'rep'=2] {'section'}, dimensions={1}, use_global_device_ids=true | all-gather | bytes 835584 | tf_op jit(solution)/shard_map/all_gather | solution.py:64
  1393.8 18.7 %all-gather.10 = bf16[1,3072,1,128]{3,1,2,0:T(8,128)(2,1)S(1)} all-gather(bf16[1,192,1,128]{3,1,2,0:T(8,128)(2,1)S(1)} %get-tuple-element.8), channel_id=12, replica_groups=mesh['section'=16,'tp'=16,'rep'=2] {'section'}, dimensions={1}, use_global_device_ids=true | all-gather | bytes 835584 | tf_op jit(solution)/shard_map/all_gather | solution.py:65
  1412.8 2.3 multiply_reduce_fusion.3
  1415.6 2.9 fusion.93
  1422.0 18.4 %all-gather.5 = bf16[1,3072,1,128]{3,1,2,0:T(8,128)(2,1)} all-gather(bf16[1,192,1,128]{3,1,2,0:T(8,128)(2,1)S(1)} %get-tuple-element.10), channel_id=7, replica_groups=mesh['section'=16,'tp'=16,'rep'=2] {'section'}, dimensions={1}, use_global_device_ids=true | all-gather | bytes 835584 | tf_op jit(solution)/shard_map/all_gather | solution.py:64
  1440.5 2.3 copy.41
  1442.9 4.1 fusion.92
  1447.0 19.1 %all-gather.6 = bf16[1,3072,1,128]{3,1,2,0:T(8,128)(2,1)} all-gather(bf16[1,192,1,128]{3,1,2,0:T(8,128)(2,1)S(1)} %copy-done.20), channel_id=8, replica_groups=mesh['section'=16,'tp'=16,'rep'=2] {'section'}, dimensions={1}, use_global_device_ids=true | all-gather | bytes 835584 | tf_op jit(solution)/shard_map/all_gather | solution.py:65
  1468.3 3.1 fusion.4
  1471.5 3.4 fusion.33
  1479.9 136.4 %all-reduce.6.cloned.1.call-done = (bf16[1,192,2432]{2,1,0:T(8,128)(2,1)}, bf16[1,192,2432]{2,1,0:T(8,128)(2,1)}) async-done(((bf16[1,192,2432]{2,1,0:T(8,128)(2,1)}, bf16[1,192,2432]{2,1,0:T(8,128)(2,1)}), (bf16[1,192,2432]{2,1,0:T(8,128)(2,1)}, bf16[1,192,2432]{2,1,0:T(8,128)(2,1)})) %all-reduce.6.cloned.1.call-update) | async-done | bytes 1867792 | tf_op jit(solution)/shard_map/psum | solution.py:90
  1619.0 2.8 fusion.70
  1621.8 34.6 %psum.39 = f32[]{:T(128)} all-reduce(f32[]{:T(128)} %get-tuple-element.38), channel_id=1, replica_groups=mesh['section'=16,'tp'=16,'rep'=2] {'section'}, use_global_device_ids=true, to_apply=%region_18.19 | all-reduce | flops 1 | bytes 8 | tf_op jit(solution)/shard_map/psum | solution.py:160
  (113 shorter events, 40.2 us)
Async XLA Ops:
  6.5 7.1 copy-start
  6.5 1136.0 %all-gather.16.cloned.1.call-start = ((), (), s32[]{:S(2)}) async-start(), calls=%async_computation.1 | async-start | bytes 1984512 | tf_op jit(solution)/shard_map/all_gather | solution.py:56
  7.3 1313.0 %all-reduce.4.cloned.1.call-start = ((), (), s32[]{:S(2)}) async-start(), calls=%async_computation | async-start | bytes 1867776 | tf_op jit(solution)/shard_map/psum | solution.py:90
  11.5 1087.4 %copy-start.14 = (f32[1,192,64]{1,2,0:T(8,128)S(1)}, f32[1,192,64]{1,2,0:T(8,128)}, u32[]{:S(2)}) copy-start(f32[1,192,64]{1,2,0:T(8,128)} %param.18) | copy-start | bytes 147460
  11.5 1087.4 %copy-start.15 = (bf16[64,2432]{1,0:T(8,128)(2,1)S(1)}, bf16[64,2432]{1,0:T(8,128)(2,1)}, u32[]{:S(2)}) copy-start(bf16[64,2432]{1,0:T(8,128)(2,1)} %param.24) | copy-start | bytes 933892
  1188.1 3.8 copy-start.2
  1192.9 3.7 copy-start.23
  1192.9 22.6 %copy-start.24 = (bf16[152,128]{1,0:T(8,128)(2,1)S(1)}, bf16[152,128]{1,0:T(8,128)(2,1)}, u32[]{:S(2)}) copy-start(bf16[152,128]{1,0:T(8,128)(2,1)} %param.34) | copy-start | bytes 116740
  1194.4 177.1 %all-gather.20.cloned.1.call-start = ((), (), s32[]{:S(2)}) async-start(), calls=%async_computation.3 | async-start | bytes 1984512 | tf_op jit(solution)/shard_map/all_gather | solution.py:56
  1195.1 224.0 %all-gather.18.cloned.1.call-start = ((), (), s32[]{:S(2)}) async-start(), calls=%async_computation.2 | async-start | bytes 1984512 | tf_op jit(solution)/shard_map/all_gather | solution.py:56
  1195.7 420.7 %all-reduce.6.cloned.1.call-start = ((), (), s32[]{:S(2)}) async-start(), calls=%async_computation.4 | async-start | bytes 3735552 | tf_op jit(solution)/shard_map/psum | solution.py:90
  1215.5 106.4 %copy-start.17 = (bf16[2432,64]{0,1:T(8,128)(2,1)S(1)}, bf16[2432,64]{0,1:T(8,128)(2,1)}, u32[]{:S(2)}) copy-start(bf16[2432,64]{0,1:T(8,128)(2,1)} %param.27) | copy-start | bytes 933892
  1215.5 106.4 %copy-start.18 = (f32[1,192,64]{1,2,0:T(8,128)S(1)}, f32[1,192,64]{1,2,0:T(8,128)}, u32[]{:S(2)}) copy-start(f32[1,192,64]{1,2,0:T(8,128)} %param.19) | copy-start | bytes 147460
  1324.0 49.7 %copy-start.4 = (f32[192,2432]{1,0:T(8,128)}, f32[192,2432]{1,0:T(8,128)S(1)}, u32[]{:S(2)}) copy-start(f32[192,2432]{1,0:T(8,128)S(1)} %get-tuple-element.33) | copy-start | bytes 5603332
  1412.8 2.8 copy-start.9
  1422.0 20.7 %copy-start.21 = (bf16[1,192,1,128]{3,1,2,0:T(8,128)(2,1)S(1)}, bf16[1,192,1,128]{3,1,2,0:T(8,128)(2,1)}, u32[]{:S(2)}) copy-start(bf16[1,192,1,128]{3,1,2,0:T(8,128)(2,1)} %get-tuple-element.12) | copy-start | bytes 147460
  1442.8 4.1 copy-start.20
  1447.0 21.4 %copy-start.25 = (f32[2,192]{1,0:T(2,128)S(1)}, f32[2,192]{1,0:T(2,128)}, u32[]{:S(2)}) copy-start(f32[2,192]{1,0:T(2,128)} %broadcast_maximum_fusion) | copy-start | bytes 4612
  1471.4 3.5 copy-start.12
  1471.5 4.9 copy-start.1
  1616.4 2.4 copy-start.5
  1616.4 2.6 copy-start.8
  1618.6 37.8 %copy-start.7 = (bf16[1,192,2432]{2,1,0:T(8,128)(2,1)S(1)}, bf16[1,192,2432]{2,1,0:T(8,128)(2,1)}, u32[]{:S(2)}) copy-start(bf16[1,192,2432]{2,1,0:T(8,128)(2,1)} %get-tuple-element.5) | copy-start | bytes 2801668
  1621.8 36.3 %copy-start.19 = (f32[192,64]{0,1:T(8,128)S(1)}, f32[192,64]{0,1:T(8,128)}, u32[]{:S(2)}) copy-start(f32[192,64]{0,1:T(8,128)} %get-tuple-element.39) | copy-start | bytes 147460
  (8 other events, 12.2 us)
Sparse Core Ops, SparseCore 0:
  9.4 47.5 all-gather.15
  1194.5 125.6 all-reduce.3
  1322.5 48.8 all-gather.19
  1373.6 40.7 all-gather.17
  1480.1 136.2 all-reduce.5
where the time goes:
time: 1670 us
  blocking collectives  1310 us (78%)
  waiting for transfers between devices  273 us (16%)
  matrix products  37.6 us (2%)
  other arithmetic  17.9 us (1%)
    psum x1, blocking collectives, per_device(): pooled = lax.psum(partial_pool, ('section', 'tp')) / prompt_ids.shape[1]  1090 us
    psum x2, waiting for transfers between devices, networks(): lax.psum(group_terms.astype(jnp.bfloat16), 'tp').astype(jnp.float32)  223 us
    all_gather x3, blocking collectives, networks(): lax.all_gather(w_out, 'section', axis=0, tiled=True)  78.2 us
    all_gather x3, blocking collectives, networks(): key_block = lax.all_gather(keys_local, 'section', axis=1, tiled=True)  56.7 us
    all_gather x3, blocking collectives, networks(): value_block = lax.all_gather(values_local, 'section', axis=1, tiled=True)  55.8 us
    all_gather x3, waiting for transfers between devices, networks(): lax.all_gather(w_qkv, 'section', axis=0, tiled=True)  47.4 us
    psum x1, blocking collectives, per_device(): spread = lax.psum(local_spread, 'section') / entries + 1e-05  34.6 us
  transfers between devices with their start and end apart: 5, of which 3 were waited for; matrix products, arithmetic and copies ran while one was open for 1% of the time, Pallas kernels for 0%

commit v1 on v0

v1 whole, which is shorter than its diff:
```python
import math

import jax
import jax.numpy as jnp
import numpy as np
from jax import lax
from jax.experimental import pallas as pl
from jax.experimental.pallas import tpu as pltpu
from jax.sharding import Mesh, PartitionSpec as P

D = 2432
HD = 64
GRID_W = 64
GRID_H = 48
CH = 64
BASIS = 192
ROW0, ONE, COL0 = 64, 112, 128
EPS = 1e-06
SEC = ("y", "core")
TP = ("xl", "zh", "zp")
N_SEC = 16
PROMPT = 256
N_TP = 16
LOCAL = 192
OWN = 12
TOKENS = 3072
KEYS = 1536
QUART = D // 4
SLOTS, SHARES, MESSAGE = 96, 104, 144
VMEM = 60 * 2**20
bf16 = jnp.bfloat16
f32 = jnp.float32


def nn(a, b):
    return jnp.dot(a, b, preferred_element_type=f32)


def nt(a, b):
    return lax.dot_general(a, b, (((1,), (1,)), ((), ())), preferred_element_type=f32)


def split2(values):
    high = values.astype(bf16)
    return high, (values - high.astype(f32)).astype(bf16)


def features(message):
    z = message[:SLOTS]
    z = jnp.concatenate([z, jnp.concatenate([z[:, CH:], z[:, :CH]], axis=1)], axis=0)
    slots = message[SLOTS:SHARES].astype(f32).T
    row = jnp.concatenate([slots[:, 0:1], slots[:64, 1:2]], axis=0)
    col = jnp.concatenate([slots[:, 2:3], slots[:64, 3:4]], axis=0)
    lane = lax.broadcasted_iota(jnp.int32, (LOCAL, 128), 1).astype(f32)
    rest = ((lane == row + ROW0) | (lane == ONE)).astype(f32).astype(bf16)
    hot = (lane[:, :GRID_W] == col).astype(f32).astype(bf16)
    return z, rest, hot


def own_tokens(g):
    row = lax.broadcasted_iota(jnp.int32, (OWN, LOCAL), 0)
    col = lax.broadcasted_iota(jnp.int32, (OWN, LOCAL), 1)
    return (col == row * N_TP + g).astype(f32)


def prepare_kernel(high_ref, low_ref, w1_ref, w2_ref, w3_ref, time_ref, shares_ref, hid_high_ref, hid_low_ref, gram_ref):
    pooled = shares_ref[0]
    for g in range(1, N_TP):
        pooled = pooled + shares_ref[g]
    pooled = pooled / PROMPT
    pooled = jnp.concatenate([pooled[k : k + 1] for k in range(D // 128)], axis=1)
    is_one = lax.broadcasted_iota(jnp.int32, (16, D), 0) == 0
    for net, w_ref in enumerate((w1_ref, w2_ref, w3_ref)):
        bias = jnp.broadcast_to(time_ref[net : net + 1, :] + pooled, (16, D))
        bias = jnp.where(is_one, bias, 0.0)
        for ref, table_ref, part in zip((hid_high_ref, hid_low_ref), (high_ref, low_ref), split2(bias)):
            ref[net, :CH, :] = w_ref[...] if ref is hid_high_ref else jnp.zeros((CH, D), bf16)
            ref[net, ROW0:ONE, :] = table_ref[:GRID_H]
            ref[net, ONE:COL0, :] = part
            ref[net, COL0:, :] = table_ref[GRID_H:]
        high, low = hid_high_ref[net], hid_low_ref[net]
        cross = nt(high, low)
        gram_ref[net] = nt(high, high) + cross + nt(low, high)


def project_kernel(pick_ref, hid_ref, w_ref, out_ref):
    out_ref[0] = nn(hid_ref[0], w_ref[0]).astype(bf16)


def project(pick, hid, w):
    return pl.pallas_call(
        project_kernel,
        grid_spec=pltpu.PrefetchScalarGridSpec(
            num_scalar_prefetch=1,
            grid=(3,),
            in_specs=[
                pl.BlockSpec((1, BASIS, D), lambda k, pick: (pick[1], 0, 0)),
                pl.BlockSpec((1, D, 128), lambda k, pick: (pick[0] + k, 0, 0)),
            ],
            out_specs=pl.BlockSpec((1, BASIS, 128), lambda k, pick: (k, 0, 0)),
        ),
        out_shape=jax.ShapeDtypeStruct((3, BASIS, 128), bf16),
        compiler_params=pltpu.CompilerParams(vmem_limit_bytes=VMEM),
        cost_estimate=pl.CostEstimate(flops=2 * BASIS * D * 384, bytes_accessed=3 * 10**6, transcendentals=0),
        name="project",
    )(pick, hid, w)


def attend_kernel(nets, members, packed, wout_at, place_ref, base_ref, *refs):
    if packed:
        z_ref, *refs = refs
    gram_ref, *refs = refs
    proj_refs = refs[:-9]
    wout_hbm, out_ref, x_ref, qp_ref, s_ref, sc_ref, wout_ref, z32_ref, sem = refs[-9:]
    s, xl, zh, core = place_ref[0], place_ref[2], place_ref[3], place_ref[4]
    shares = N_TP // members
    count = shares * OWN
    load = pltpu.make_async_copy(wout_hbm.at[pl.ds(wout_at, members * nets)], wout_ref, sem)
    load.start()
    if packed:
        z32_ref[...] = z_ref[...].astype(f32)
        for sec in range(N_SEC):
            unused, rest, hot = features(base_ref[sec])
            for j in range(OWN):
                at = (j * N_SEC + sec) * 16
                x_ref[at : at + 16, :128] = rest[j * 16 : (j + 1) * 16]
                x_ref[at : at + 16, COL0:] = hot[j * 16 : (j + 1) * 16]
        lane = lax.broadcasted_iota(jnp.int32, (256, 128), 1)
        for j in range(OWN):
            chunk = z32_ref[pl.ds(j // 2, 256, stride=8), :].astype(bf16)
            if j % 2:
                chunk = jnp.concatenate([chunk[:, 64:], chunk[:, :64]], axis=1)
            at = slice(j * 256, (j + 1) * 256)
            x_ref[at, :128] = jnp.where(lane < CH, chunk, x_ref[at, :128])
        own = jnp.concatenate(
            [x_ref[pl.ds(pl.multiple_of((j * N_SEC + s) * 16, 16), 16), :] for j in range(OWN)], axis=0
        )
        scales = z32_ref[pl.ds(6, 256, stride=8), :].T
        for net in range(nets):
            for j in range(OWN):
                line = net * 32 + j
                line = scales[line : line + 1] + scales[line + 16 : line + 17]
                at = j * 256
                sc_ref[net, at // KEYS, :, at % KEYS : at % KEYS + 256] = jnp.broadcast_to(line, (8, 256))
    else:
        for sec in range(N_SEC):
            z, rest, hot = features(base_ref[sec])
            lane = lax.broadcasted_iota(jnp.int32, z.shape, 1)
            x_ref[sec * LOCAL : (sec + 1) * LOCAL, :128] = jnp.where(lane < CH, z, rest)
            x_ref[sec * LOCAL : (sec + 1) * LOCAL, COL0:] = hot
        own = x_ref[pl.ds(pl.multiple_of(s * LOCAL, LOCAL), LOCAL), :]
    row = lax.broadcasted_iota(jnp.int32, (count, LOCAL), 0)
    col = lax.broadcasted_iota(jnp.int32, (count, LOCAL), 1)
    share = lax.shift_right_logical(row * 171, 11)
    if members == 2:
        owner = xl * 8 + share
    else:
        owner = lax.shift_right_logical(share, 1) * 8 + zh * 2 + lax.bitwise_and(share, 1)
    order = (col == (row - share * OWN) * N_TP + owner).astype(bf16)
    queries = nn(order, own).astype(bf16)
    eye = (
        lax.broadcasted_iota(jnp.int32, (BASIS, BASIS), 0) == lax.broadcasted_iota(jnp.int32, (BASIS, BASIS), 1)
    ).astype(bf16)
    heads = [(member, slice(half * HD, (half + 1) * HD)) for member in range(members) for half in range(2)]
    rows = len(heads) * count
    for turn in range(nets):
        net = lax.bitwise_xor(core, turn) if nets == 2 else 0
        gram_high, gram_low = split2(gram_ref[net])
        energy = jnp.sum(
            (nn(queries, gram_high) + nn(queries, gram_low)) * queries.astype(f32), axis=1, keepdims=True
        )
        scale = lax.rsqrt(energy / D + EPS)

        def proj(member, kind):
            if nets == 2:
                return proj_refs[turn][member, kind]
            return proj_refs[member][kind]

        for h, (member, part) in enumerate(heads):
            if part.start == 0:
                q = (nn(queries, proj(member, 0)) * scale).astype(bf16)
            qp_ref[h * count : (h + 1) * count, :] = (
                nt(q[:, part], proj(member, 1)[:, part]) * HD ** (-0.5)
            ).astype(bf16)

        def score(block, top):
            keys = x_ref[pl.ds(pl.multiple_of(block * KEYS, KEYS), KEYS), :]
            if not packed:
                energy = (nt(gram_high, keys) + nt(gram_low, keys)) * nt(eye, keys)
                scale = lax.rsqrt(jnp.sum(energy, axis=0, keepdims=True) / D + EPS)
                sc_ref[net, block] = jnp.broadcast_to(scale, (8, KEYS))
            scores = nt(qp_ref[...], keys) * sc_ref[net, block][:1]
            s_ref[block] = scores
            for part in range(KEYS // 128):
                top = jnp.maximum(top, scores[:, part * 128 : (part + 1) * 128])
            return top

        top = lax.fori_loop(0, TOKENS // KEYS, score, jnp.full((rows, 128), -1e30, f32))
        top = jnp.max(top, axis=1, keepdims=True)

        def mix(block, carry):
            total, mixed = carry
            expo = jnp.exp(s_ref[block] - top)
            for part in range(KEYS // 128):
                total = total + expo[:, part * 128 : (part + 1) * 128]
            weights = (expo * sc_ref[net, block][:1]).astype(bf16)
            keys = x_ref[pl.ds(pl.multiple_of(block * KEYS, KEYS), KEYS), :]
            return total, mixed + nn(weights, keys)

        total, mixed = lax.fori_loop(
            0, TOKENS // KEYS, mix, (jnp.zeros((rows, 128), f32), jnp.zeros((rows, BASIS), f32))
        )
        mixed = (mixed / jnp.sum(total, axis=1, keepdims=True)).astype(bf16)
        if turn == 0:
            load.wait()
        values = [
            nn(mixed[h * count : (h + 1) * count], proj(member, 2)[:, part]) for h, (member, part) in enumerate(heads)
        ]
        values = jnp.concatenate(values, axis=1).astype(bf16)
        term = []
        for part in range(4):
            at = slice(part * QUART, (part + 1) * QUART)
            term.append(nt(values, jnp.concatenate([wout_ref[m * nets + net, at, :] for m in range(members)], axis=1)))
        for d in range(shares):
            block = jnp.concatenate([t[d * OWN : (d + 1) * OWN] for t in term], axis=0).astype(bf16)
            if nets == 2:
                out_ref[d, pl.ds(pl.multiple_of(net * 48, 16), 48), :] = block
            else:
                out_ref[d] = block


def attend(place, base, z, gram_at, gram, proj, wout_at, wout):
    nets = 1 if z is None else 2
    members = 2 if z is None else 4
    packed = z is not None
    args = (base, z) if packed else (base,)
    rows = 2 * members * OWN * (N_TP // members)
    whole = lambda a: pl.BlockSpec(a.shape, lambda i: (0,) * a.ndim)
    out = jax.ShapeDtypeStruct((N_TP // members, nets * 4 * OWN, QUART), bf16)
    return pl.pallas_call(
        lambda *refs: attend_kernel(nets, members, packed, wout_at, *refs),
        out_shape=out,
        grid=(1,),
        in_specs=[pl.BlockSpec(memory_space=pltpu.SMEM)]
        + [whole(a) for a in args]
        + [pl.BlockSpec((nets, BASIS, BASIS), lambda i: (gram_at, 0, 0))]
        + [whole(a) for a in proj]
        + [pl.BlockSpec(memory_space=pl.ANY)],
        out_specs=whole(out),
        scratch_shapes=[
            pltpu.VMEM((TOKENS, BASIS), bf16),
            pltpu.VMEM((rows, BASIS), bf16),
            pltpu.VMEM((TOKENS // KEYS, rows, KEYS), f32),
            pltpu.VMEM((nets, TOKENS // KEYS, 8, KEYS), f32),
            pltpu.VMEM((members * nets, D, 128), bf16),
            pltpu.VMEM((N_SEC * N_TP * 8, 128), f32),
            pltpu.SemaphoreType.DMA,
        ],
        compiler_params=pltpu.CompilerParams(vmem_limit_bytes=VMEM),
        cost_estimate=pl.CostEstimate(flops=nets * 4 * 10**9, bytes_accessed=10**7, transcendentals=nets * 1200000),
        name="attend",
    )(place, *args, gram, *proj, wout)


def finish(recv_ref, net, hidden, w_final):
    rows = slice(net * 4 * OWN, (net + 1) * 4 * OWN)
    terms = recv_ref[0, rows].astype(f32)
    for d in range(1, recv_ref.shape[0]):
        terms = terms + recv_ref[d, rows].astype(f32)
    afters = []
    energy = jnp.zeros((OWN, 1), f32)
    for part in range(4):
        after = hidden[:, part * QUART : (part + 1) * QUART] + terms[part * OWN : (part + 1) * OWN]
        energy = energy + jnp.sum(after * after, axis=1, keepdims=True)
        afters.append(after)
    scale = lax.rsqrt(energy / D + EPS)
    normed = jnp.concatenate([after * scale for after in afters], axis=1).astype(bf16)
    return nt(normed, w_final[...])


def own_kernel(place_ref, message_ref, high_ref, low_ref, x12_ref, hidden_ref):
    z, rest, hot = features(message_ref[...])
    lane = lax.broadcasted_iota(jnp.int32, z.shape, 1)
    full = jnp.concatenate([jnp.where(lane < CH, z, rest), hot], axis=1)
    x12 = nn(own_tokens(place_ref[1]).astype(bf16), full).astype(bf16)
    x12_ref[...] = x12
    hidden_ref[...] = nn(x12, high_ref[0]) + nn(x12, low_ref[0])


def scores_own_kernel(after_ref, x12_ref, high_ref, low_ref, hidden_ref):
    for net in range(2):
        hidden_ref[net] = nn(x12_ref[...], high_ref[net]) + nn(x12_ref[...], low_ref[net])


def student_kernel(
    place_ref, time_ref, recv_ref, hidden_ref, own12_ref, noise_ref, renoise_ref, wf_ref, gram_ref,
    x0_ref, noisy_ref, x12_ref, send_ref,
):
    pick = own_tokens(place_ref[1])
    x12 = own12_ref[...]
    velocity = finish(recv_ref, 0, hidden_ref[...], wf_ref)
    exact = lax.Precision.HIGHEST
    noise = jnp.dot(pick, noise_ref[...], precision=exact, preferred_element_type=f32)
    renoise = jnp.dot(pick, renoise_ref[...], precision=exact, preferred_element_type=f32)
    x0 = noise - velocity
    t = time_ref[0]
    noisy = (1.0 - t) * x0 + t * renoise
    x12 = jnp.concatenate([noisy.astype(bf16), x12[:, CH:]], axis=1)
    x0_ref[...] = x0
    noisy_ref[...] = noisy
    x12_ref[...] = x12
    row = lax.broadcasted_iota(jnp.int32, (OWN, 128), 0)
    lane = lax.broadcasted_iota(jnp.int32, (OWN, 128), 1)
    scales = jnp.zeros((OWN, 128), f32)
    for net in range(2):
        high, low = split2(gram_ref[net])
        energy = jnp.sum((nn(x12, high) + nn(x12, low)) * x12.astype(f32), axis=1, keepdims=True)
        for part, value in enumerate(split2(lax.rsqrt(energy / D + EPS))):
            scales = jnp.where(lane == row + (net * 32 + part * 16), value.astype(f32), scales)
    scales = jnp.sum(scales, axis=0, keepdims=True)
    pairs = [jnp.concatenate([noisy[j : j + 1], noisy[j + 1 : j + 2]], axis=1) for j in range(0, OWN, 2)]
    send_ref[...] = jnp.concatenate(pairs + [scales, jnp.zeros((1, 128), f32)], axis=0).astype(bf16)


def score_kernel(
    time_ref, recv_ref, x0_ref, noisy_ref, hidden_ref, wr_ref, wf_ref, send_ref
):
    noisy = noisy_ref[...]
    real = finish(recv_ref, 0, hidden_ref[0], wr_ref)
    fake = finish(recv_ref, 1, hidden_ref[1], wf_ref)
    t = time_ref[0]
    gap = jnp.abs(x0_ref[...] - (noisy - t * real))
    gap = jnp.sum(jnp.sum(gap, axis=1, keepdims=True), axis=0, keepdims=True)
    grad = t * (real - fake)
    packed = [jnp.concatenate([grad[j : j + 1], grad[j + 1 : j + 2]], axis=1) for j in range(0, OWN, 2)]
    packed = jnp.concatenate([*packed, jnp.broadcast_to(gap, (1, 128)), jnp.zeros((1, 128), f32)], axis=0)
    send_ref[...] = jnp.broadcast_to(packed[None], send_ref.shape)


def call(kernel, shapes, smem, *args):
    def spec(arg):
        if isinstance(arg, tuple):
            array, n, at = arg
            return pl.BlockSpec((n, *array.shape[1:]), lambda i: (at,) + (0,) * (array.ndim - 1))
        return pl.BlockSpec(arg.shape, lambda i: (0,) * len(arg.shape))

    return pl.pallas_call(
        kernel,
        out_shape=shapes,
        grid=(1,),
        in_specs=[pl.BlockSpec(memory_space=pltpu.SMEM)] * smem + [spec(arg) for arg in args[smem:]],
        out_specs=jax.tree.map(spec, shapes),
        compiler_params=pltpu.CompilerParams(vmem_limit_bytes=VMEM),
        cost_estimate=pl.CostEstimate(flops=10**9, bytes_accessed=10**7, transcendentals=0),
        name=kernel.__name__,
    )(*[arg[0] if isinstance(arg, tuple) else arg for arg in args])


def swap(values, axes):
    return lax.all_to_all(values, axes, 0, 0, tiled=False)


def spread_to(values, axes, count):
    return swap(jnp.broadcast_to(values[None], (count, *values.shape)), axes)


def shift(values, axis, count, step):
    return lax.ppermute(values, axis, [((i + step) % count, i) for i in range(count)])


def place_tables():
    quarter = D // 4
    frequency = np.exp(-math.log(10000.0) * np.arange(quarter, dtype=np.float64) / quarter)
    table = np.zeros((GRID_H + GRID_W, D), np.float32)
    row = np.arange(GRID_H)[:, None] * frequency[None, :]
    col = np.arange(GRID_W)[:, None] * frequency[None, :]
    table[:GRID_H, : D // 2] = np.concatenate([np.sin(row), np.cos(row)], axis=1)
    table[GRID_H:, D // 2 :] = np.concatenate([np.sin(col), np.cos(col)], axis=1)
    high = table.astype(bf16)
    return jnp.asarray(high), jnp.asarray((table - high.astype(np.float32)).astype(bf16))


def time_embed(step_time):
    half_width = D // 2
    frequency = jnp.exp(-math.log(10000.0) * jnp.arange(half_width, dtype=f32) / half_width)
    angles = 1000.0 * step_time * frequency
    return jnp.concatenate([jnp.cos(angles), jnp.sin(angles)])


def per_device(
    student_noise,
    renoise_noise,
    patch_slot,
    renoise_step,
    prompt_ids,
    text_table,
    student_in,
    student_qkv,
    student_out,
    student_final,
    real_in,
    real_qkv,
    real_out,
    real_final,
    fake_in,
    fake_qkv,
    fake_out,
    fake_final,
):
    s = lax.axis_index(SEC)
    g = lax.axis_index(TP)
    core = lax.axis_index("core")
    place = jnp.stack([s, g, lax.axis_index("xl"), lax.axis_index("zh"), core]).astype(jnp.int32)
    step_time = renoise_step[0].astype(f32) / 1000.0

    vocab_local = text_table.shape[0]
    first_row = (s * N_TP + g) * vocab_local
    prompt_row = prompt_ids[0] - first_row
    matches = (prompt_row[:, None] == jnp.arange(vocab_local, dtype=jnp.int32)[None, :]).astype(f32)
    counts = jnp.sum(matches, axis=0).astype(bf16)
    partial_pool = nn(counts[None], text_table).reshape(D // 128, 128)
    noise = student_noise[0]
    packed = noise.astype(bf16)
    packed = jnp.concatenate([packed[:SLOTS], packed[SLOTS:]], axis=1)
    slot = patch_slot[0]
    lines = jnp.stack([slot // GRID_W, slot % GRID_W]).astype(bf16)
    lines = jnp.pad(jnp.pad(lines, ((0, 0), (0, 64))).reshape(4, 128), ((0, 4), (0, 0)))
    own = jnp.concatenate([packed, lines, *split2(partial_pool), jnp.zeros((2, 128), bf16)], axis=0)
    out_peer = shift(student_out, "xl", 2, 1)[None]
    out_peer, own = lax.optimization_barrier((out_peer, own))
    base = spread_to(own, SEC, N_SEC)
    out2 = jnp.stack([real_out, fake_out])
    out2, own = lax.optimization_barrier((out2, own))
    out2 = lax.all_gather(out2, "zh", axis=0, tiled=True)
    shares = base[:, SHARES : SHARES + 38].astype(f32).reshape(N_SEC * 2, D // 128, 128)
    shares = jnp.sum(shares, axis=0)
    shares, out2 = lax.optimization_barrier((shares, out2))
    shares = spread_to(shares, TP, N_TP)

    def columns(qkv):
        return jnp.transpose(qkv, (1, 0, 2))

    def gather(*parts):
        return lax.all_gather(jnp.concatenate(parts, axis=0), SEC, axis=1, tiled=True)

    first = gather(columns(student_qkv), columns(real_qkv), columns(fake_qkv), student_out[None], out_peer)

    one = jax.ShapeDtypeStruct
    times = jnp.stack([time_embed(t) for t in (step_time, step_time, jnp.float32(1.0))])
    high, low, gram = call(
        prepare_kernel,
        (one((3, BASIS, D), bf16), one((3, BASIS, D), bf16), one((3, BASIS, BASIS), f32)),
        0,
        *place_tables(),
        real_in,
        fake_in,
        student_in,
        times,
        shares,
    )
    first, gram = lax.optimization_barrier((first, gram))
    out2, first = lax.optimization_barrier((out2, first))
    wout2 = gather(out2)
    zero = jnp.int32(0)
    proj1 = project(jnp.stack([zero, zero + 2]), high, first)
    peer1 = shift(proj1, "xl", 2, 1)
    pick = jnp.stack([3 + 3 * core, core])
    pick, place, proj1 = lax.optimization_barrier((pick, place, proj1))
    proj2 = project(pick, high, first)
    x12, hidden = call(
        own_kernel, (one((OWN, BASIS), bf16), one((OWN, D), f32)), 1, place, own, (high, 1, 2), (low, 1, 2)
    )
    proj2, hidden, place = lax.optimization_barrier((proj2, hidden, place))
    terms = attend(place, base, None, 2, gram, (proj1, peer1), 9, first)
    terms = swap(terms, ("zh", "zp"))
    x0, noisy, x12, message = call(
        student_kernel,
        (one((OWN, CH), f32), one((OWN, CH), f32), one((OWN, BASIS), bf16), one((8, 128), bf16)),
        2,
        place,
        step_time[None],
        terms,
        hidden,
        x12,
        noise,
        renoise_noise[0],
        student_final.T,
        (gram, 2, 0),
    )
    proj2, message = lax.optimization_barrier((proj2, message))
    proj2 = lax.all_gather(proj2, "zh", axis=0, tiled=False)
    everyone = spread_to(message, SEC + TP, N_SEC * N_TP).reshape(N_SEC * N_TP * 8, 128)
    proj2 = (proj2, shift(proj2, "core", 2, 1))
    terms = attend(place, base, everyone, 0, gram, proj2, 0, wout2)
    x12, terms = lax.optimization_barrier((x12, terms))
    hidden = call(
        scores_own_kernel, one((2, OWN, D), f32), 1, place, x12, (high, 2, 0), (low, 2, 0)
    )
    terms = swap(terms, ("xl", "zp"))
    message = call(
        score_kernel,
        one((N_TP, 8, 128), f32),
        1,
        step_time[None],
        terms,
        x0,
        noisy,
        hidden,
        real_final.T,
        fake_final.T,
    )
    near = swap(message, TP)
    gap = spread_to(jnp.sum(near[:, 6:7], axis=0), SEC, N_SEC)
    spread = jnp.sum(gap[:, 0, 0]) / (TOKENS * CH) + 1e-05
    grad = jnp.transpose(near[:, :6].reshape(N_TP, 6, 2, CH), (1, 2, 0, 3))
    return (grad.reshape(LOCAL, CH) / spread)[None]


def solution(mesh):
    fine = Mesh(mesh.devices.reshape(8, 2, 2, 4, 2, 2), ("y", "core", "xl", "zh", "zp", "rep"))
    qkv = P(SEC, None, TP)
    out = P(SEC, TP)
    net = (P(), qkv, out, P())
    placed = (
        P("rep", SEC, None),
        P("rep", SEC, None),
        P("rep", SEC),
        P("rep"),
        P("rep", None),
        P(SEC + TP, None),
    ) + net * 3
    return jax.shard_map(
        per_device, mesh=fine, in_specs=placed, out_specs=P("rep", SEC, None), check_vma=False
    )
```

time: 1670 us -> 245 us (0.15)
  blocking collectives: 1310 us -> 73.2 us
  waiting for transfers between devices: 273 us -> 33.5 us
  starting transfers between devices: 0.16 us -> 51.6 us
  Pallas kernels: 0 us -> 49.3 us
  matrix products: 37.6 us -> 0.26 us
    psum x2 -> x0, blocking collectives: 1120 us -> none  [the longest x1 1090 us: per_device(): pooled = lax.psum(partial_pool, ('section', 'tp')) / prompt_ids.shape[1]]
    psum x2 -> x0, waiting for transfers between devices: 223 us -> none  [networks(): lax.psum(group_terms.astype(jnp.bfloat16), 'tp').astype(jnp.float32)]
    all_gather x9 -> x2, blocking collectives: 191 us -> 45.6 us  [the longest x1 27.3 us: per_device(): proj2 = lax.all_gather(proj2, 'zh', axis=0, tiled=False)]
    pallas_call x0 -> x9, Pallas kernels: none -> 49.3 us  [the longest x2 22.7 us: attend(): pl.pallas_call(lambda *refs: attend_kernel(nets, members, packed, wout_at...]
    all_gather x3 -> x2, waiting for transfers between devices: 47.4 us -> 3.73 us  [gather(): lax.all_gather(jnp.concatenate(parts, axis=0), SEC, axis=1, tiled=True)]
    all_to_all x0 -> x5, starting transfers between devices: none -> 41.1 us  [swap(): return lax.all_to_all(values, axes, 0, 0, tiled=False)]
    dot_general x19 -> x1, matrix products: 37.6 us -> 0.26 us  [nn(): return jnp.dot(a, b, preferred_element_type=f32)]
    all_to_all x0 -> x5, waiting for transfers between devices: none -> 28.2 us  [swap(): return lax.all_to_all(values, axes, 0, 0, tiled=False)]
  transfers between devices with their start and end apart: 5 -> 10, of which waited for: 3 -> 6; matrix products, arithmetic and copies ran while one was open for 1% -> 6% of each run, Pallas kernels for 0% -> 14%
where the time goes in v1:
time: 245 us; the launch traced here: 244 us
  blocking collectives  73.2 us (30%)
  starting transfers between devices  51.6 us (21%)
  Pallas kernels  49.3 us (20%)
  waiting for transfers between devices  33.5 us (14%)
  local copies, waits for them, and re-layouts  16.4 us (7%)
  between operations  15 us (6%)
  other arithmetic  4.38 us (2%)
    all_to_all x5, starting transfers between devices, swap(): return lax.all_to_all(values, axes, 0, 0, tiled=False)  41.1 us
    all_to_all x5, waiting for transfers between devices, swap(): return lax.all_to_all(values, axes, 0, 0, tiled=False)  28.2 us
    all_to_all x2, blocking collectives, swap(): return lax.all_to_all(values, axes, 0, 0, tiled=False)  27.6 us
    all_gather x1, blocking collectives, per_device(): proj2 = lax.all_gather(proj2, 'zh', axis=0, tiled=False)  27.3 us
    pallas_call x2, Pallas kernels, attend(): pl.pallas_call(lambda *refs: attend_kernel(nets, members, packed, wout_at...  22.7 us
    all_gather x1, blocking collectives, per_device(): out2 = lax.all_gather(out2, 'zh', axis=0, tiled=True)  18.3 us
    pallas_call x5, Pallas kernels, call(): pl.pallas_call(kernel, out_shape=shapes, grid=(1,), in_specs=[pl.BlockSpe...  17.4 us
    unnamed x37, local copies, waits for them, and re-layouts  11.4 us
  transfers between devices with their start and end apart: 10, of which 6 were waited for; matrix products, arithmetic and copies ran while one was open for 6% of the time, Pallas kernels for 14%

profile of v1, /device:TPU:1, one launch (start us, length us, event | category | flops | bytes accessed | tf_op | source)
XLA Modules:
  0.0 243.7 jit_solution(564548318117674175)
XLA Ops:
  6.5 4.1 %collective-permute-start = (bf16[152,128]{1,0:T(8,128)(2,1)}, bf16[152,128]{1,0:T(8,128)(2,1)S(1)}, u32[]{:S(2)}, u32[]{:S(2)}) collective-permute-start(bf16[152,128]{1,0:T(8,128)(2,1)} %param.28), channel_id=1, source_target_pairs={{16,0},{0,16},{17,1},{1,17},{18,2},{2,18},{19,3},{3,19},{20,4},{4,... | collective-permute-start | bytes 116744 | tf_op jit(solution)/shard_map/ppermute | solution.py:368
  20.4 8.2 %all-to-all-start = ((bf16[16,144,128]{2,1,0:T(8,128)(2,1)}), bf16[16,144,128]{2,1,0:T(8,128)(2,1)S(1)}, u32[]{:S(2)}, u32[]{:S(2)}) async-start(bf16[16,144,128]{2,1,0:T(8,128)(2,1)} %broadcast_in_dim.19), calls=%async_computation | async-start | bytes 1179648 | tf_op jit(solution)/shard_map/all_to_all | solution.py:360
  29.7 18.3 %all_gather.15 = bf16[8,152,128]{2,1,0:T(8,128)(2,1)} all-gather(bf16[2,152,128]{2,1,0:T(8,128)(2,1)S(1)} %pad_maximum_fusion), channel_id=1, replica_groups=mesh['y'=8,'core'=2,'xl'=2,'zh'=4,'zp'=2,'rep'=2] {'zh'}, dimensions={0}, use_global_device_ids=true | all-gather | bytes 389120 | tf_op jit(solution)/shard_map/all_gather | solution.py:434
  49.4 11.9 %all-to-all-start.1 = ((f32[16,19,128]{2,1,0:T(8,128)}), f32[16,19,128]{2,1,0:T(8,128)S(1)}, u32[]{:S(2)}, u32[]{:S(2)}) async-start(f32[16,19,128]{2,1,0:T(8,128)} %broadcast_in_dim.20), calls=%async_computation.1 | async-start | bytes 393216 | tf_op jit(solution)/shard_map/all_to_all | solution.py:360
  62.1 7.3 %all-to-all-done.1.shares_ref = f32[16,19,128]{2,1,0:T(8,128)S(1)} async-done(((f32[16,19,128]{2,1,0:T(8,128)}), f32[16,19,128]{2,1,0:T(8,128)S(1)}, u32[]{:S(2)}, u32[]{:S(2)}) %all-to-all-start.1) | async-done | bytes 155680 | tf_op jit(solution)/shard_map/all_to_all | solution.py:360
  70.1 5.6 %prepare_kernel.1 = (bf16[3,192,2432]{2,1,0:T(8,128)(2,1)}, bf16[3,192,2432]{2,1,0:T(8,128)(2,1)}, f32[3,192,192]{2,1,0:T(8,128)}) custom-call(bf16[112,2432]{1,0:T(8,128)(2,1)} %constant.89.clone.high_ref, bf16[112,2432]{1,0:T(8,128)(2,1)} %constant.90.clone.low_ref, bf16[64,2432]{1,0:T(8,128)(2,1)} %w1_ref.1, bf16[64,2432]{1,0:T(8,128)(2,1)} %w2_ref.1, ...), custom_call_target="tpu_custom_call" | custom-call | flops 1000000000 | bytes 10000000 | tf_op jit(solution)/shard_map/prepare_kernel/pallas_call | solution.py:347
  75.6 3.7 %all-gather.4.cloned.1.call-done.w_ref.refs_5_ = bf16[11,2432,128]{2,1,0:T(8,128)(2,1)} async-done(((bf16[11,152,128]{2,1,0:T(8,128)(2,1)}), bf16[11,2432,128]{2,1,0:T(8,128)(2,1)}) %all-gather.4.cloned.1.call-update) | async-done | bytes 6848528 | tf_op jit(solution)/shard_map/all_gather | solution.py:444
  79.9 4.6 %project.2.refs_3_ = bf16[3,192,128]{2,1,0:T(8,128)(2,1)} custom-call(s32[2]{0:T(128)} %iota_multiply_fusion.pick_ref, bf16[3,192,2432]{2,1,0:T(8,128)(2,1)} %get-tuple-element.37.hid_ref.high_ref, bf16[11,2432,128]{2,1,0:T(8,128)(2,1)} %all-gather.4.cloned.1.call-done.w_ref.refs_5_), custom_call_target="tpu_custom_call" | custom-call | flops 358612992 | bytes 3000000 | tf_op jit(solution)/shard_map/project/pallas_call | solution.py:91
  84.5 3.6 %collective-permute-start.1 = (bf16[3,192,128]{2,1,0:T(8,128)(2,1)}, bf16[3,192,128]{2,1,0:T(8,128)(2,1)S(1)}, u32[]{:S(2)}, u32[]{:S(2)}) collective-permute-start(bf16[3,192,128]{2,1,0:T(8,128)(2,1)} %project.2.refs_3_), channel_id=1, source_target_pairs={{16,0},{0,16},{17,1},{1,17},{18,2},{2,18},{19,3},{3,19},{20,4},{4,... | collective-permute-start | bytes 442376 | tf_op jit(solution)/shard_map/ppermute | solution.py:368
  89.4 4.6 %project.3 = bf16[3,192,128]{2,1,0:T(8,128)(2,1)} custom-call(s32[2]{0:T(128)} %pad_add_fusion.pick_ref, bf16[3,192,2432]{2,1,0:T(8,128)(2,1)} %get-tuple-element.37.hid_ref.high_ref, bf16[11,2432,128]{2,1,0:T(8,128)(2,1)} %all-gather.4.cloned.1.call-done.w_ref.refs_5_), custom_call_target="tpu_custom_call" | custom-call | flops 358612992 | bytes 3000000 | tf_op jit(solution)/shard_map/project/pallas_call | solution.py:91
  94.0 2.9 %own_kernel.1 = (bf16[12,192]{1,0:T(8,128)(2,1)}, f32[12,2432]{1,0:T(8,128)}) custom-call(s32[5]{0:T(128)} %stack.57.place_ref.refs_0_.after_ref, bf16[144,128]{1,0:T(8,128)(2,1)} %copy-done.8, bf16[3,192,2432]{2,1,0:T(8,128)(2,1)} %get-tuple-element.37.hid_ref.high_ref, bf16[3,192,2432]{2,1,0:T(8,128)(2,1)} %get-tuple-element.46.low_ref), custom_call_target="tpu_custom_call" | custom-call | flops 1000000000 | bytes 10000000 | tf_op jit(solution)/shard_map/own_kernel/pallas_call | solution.py:347
  97.5 9.3 %attend.2 = bf16[8,48,608]{2,1,0:T(8,128)(2,1)} custom-call(s32[5]{0:T(128)} %stack.57.place_ref.refs_0_.after_ref, bf16[16,144,128]{2,1,0:T(8,128)(2,1)} %copy-done, f32[3,192,192]{2,1,0:T(8,128)} %get-tuple-element.49.refs_2_.gram_ref.refs_3_, bf16[3,192,128]{2,1,0:T(8,128)(2,1)} %project.2.refs_3_, bf16[3,192,128]{2,1,0:T(8,128)(2,1)} %copy-done.14, ...), custom_call_target="tpu_custom_call" | custom-call | flops 4000000000 | bytes 10000000 | tf_op jit(solution)/shard_map/attend/pallas_call | solution.py:240
  106.8 8.6 %all-to-all-start.2 = ((bf16[8,48,608]{2,1,0:T(8,128)(2,1)}), bf16[8,48,608]{2,1,0:T(8,128)(2,1)S(1)}, u32[]{:S(2)}, u32[]{:S(2)}) async-start(bf16[8,48,608]{2,1,0:T(8,128)(2,1)} %attend.2), calls=%async_computation.2 | async-start | bytes 983040 | tf_op jit(solution)/shard_map/all_to_all | solution.py:360
  116.2 16.5 %all-to-all-done.2.recv_ref = bf16[8,48,608]{2,1,0:T(8,128)(2,1)S(1)} async-done(((bf16[8,48,608]{2,1,0:T(8,128)(2,1)}), bf16[8,48,608]{2,1,0:T(8,128)(2,1)S(1)}, u32[]{:S(2)}, u32[]{:S(2)}) %all-to-all-start.2) | async-done | bytes 466976 | tf_op jit(solution)/shard_map/all_to_all | solution.py:360
  133.5 2.9 %student_kernel.1 = (f32[12,64]{1,0:T(8,128)}, f32[12,64]{1,0:T(8,128)}, bf16[12,192]{1,0:T(8,128)(2,1)}, bf16[8,128]{1,0:T(8,128)(2,1)}) custom-call(s32[5]{0:T(128)} %stack.57.place_ref.refs_0_.after_ref, f32[1]{0:T(128)} %bitcast.1.time_ref, bf16[8,48,608]{2,1,0:T(8,128)(2,1)} %copy-done.5, f32[12,2432]{1,0:T(8,128)} %get-tuple-element.51.hidden_ref, ...), custom_call_target="tpu_custom_call" | custom-call | flops 1000000000 | bytes 10000000 | tf_op jit(solution)/shard_map/student_kernel/pallas_call | solution.py:347
  138.0 8.9 %all-to-all-start.3 = ((bf16[256,8,128]{2,1,0:T(8,128)(2,1)}), bf16[256,8,128]{2,1,0:T(8,128)(2,1)S(1)}, u32[]{:S(2)}, u32[]{:S(2)}) async-start(bf16[256,8,128]{2,1,0:T(8,128)(2,1)} %broadcast_in_dim.22), calls=%async_computation.3 | async-start | bytes 1048576 | tf_op jit(solution)/shard_map/all_to_all | solution.py:360
  146.8 27.3 %all-gather = bf16[12,192,128]{2,1,0:T(8,128)(2,1)S(1)} all-gather(bf16[3,192,128]{2,1,0:T(8,128)(2,1)S(1)} %copy-done.3), channel_id=2, replica_groups=mesh['y'=8,'core'=2,'xl'=2,'zh'=4,'zp'=2,'rep'=2] {'zh'}, dimensions={0}, use_global_device_ids=true | all-gather | bytes 737280 | tf_op jit(solution)/shard_map/all_gather | solution.py:491
  174.1 2.7 %collective-permute-start.2 = (bf16[4,3,192,128]{3,2,1,0:T(8,128)(2,1)S(1)}, bf16[4,3,192,128]{3,2,1,0:T(8,128)(2,1)S(1)}, u32[]{:S(2)}, u32[]{:S(2)}) collective-permute-start(bf16[4,3,192,128]{3,2,1,0:T(8,128)(2,1)S(1)} %bitcast.46), channel_id=1, source_target_pairs={{32,0},{0,32},{33,1},{1,33},{34,2},{2,34},{35,3},{3,35},{36,4},{4,... | collective-permute-start | bytes 1769480 | tf_op jit(solution)/shard_map/ppermute | solution.py:368
  179.5 13.4 %attend.3 = bf16[4,96,608]{2,1,0:T(8,128)(2,1)} custom-call(s32[5]{0:T(128)} %stack.57.place_ref.refs_0_.after_ref, bf16[16,144,128]{2,1,0:T(8,128)(2,1)} %copy-done, bf16[2048,128]{1,0:T(8,128)(2,1)} %bitcast.48, f32[3,192,192]{2,1,0:T(8,128)} %get-tuple-element.49.refs_2_.gram_ref.refs_3_, bf16[4,3,192,128]{3,2,1,0:T(8,128)(2,1)} %bitcast.47, ...), custom_call_target="tpu_custom_call" | custom-call | flops 8000000000 | bytes 10000000 | tf_op jit(solution)/shard_map/attend/pallas_call | solution.py:240
  192.9 3.5 %all-to-all-start.4 = ((bf16[4,96,608]{2,1,0:T(8,128)(2,1)}), bf16[4,96,608]{2,1,0:T(8,128)(2,1)S(1)}, u32[]{:S(2)}, u32[]{:S(2)}) async-start(bf16[4,96,608]{2,1,0:T(8,128)(2,1)} %attend.3), calls=%async_computation.4 | async-start | bytes 983040 | tf_op jit(solution)/shard_map/all_to_all | solution.py:360
  196.4 3.5 %scores_own_kernel.1.hidden_ref = f32[2,12,2432]{2,1,0:T(8,128)} custom-call(s32[5]{0:T(128)} %stack.57.place_ref.refs_0_.after_ref, bf16[12,192]{1,0:T(8,128)(2,1)} %get-tuple-element.62.x12_ref, bf16[3,192,2432]{2,1,0:T(8,128)(2,1)} %get-tuple-element.37.hid_ref.high_ref, bf16[3,192,2432]{2,1,0:T(8,128)(2,1)} %get-tuple-element.46.low_ref), custom_call_target="tpu_custom_call" | custom-call | flops 1000000000 | bytes 10000000 | tf_op jit(solution)/shard_map/scores_own_kernel/pallas_call | solution.py:347
  199.8 3.8 %all-to-all-done.4.recv_ref = bf16[4,96,608]{2,1,0:T(8,128)(2,1)S(1)} async-done(((bf16[4,96,608]{2,1,0:T(8,128)(2,1)}), bf16[4,96,608]{2,1,0:T(8,128)(2,1)S(1)}, u32[]{:S(2)}, u32[]{:S(2)}) %all-to-all-start.4) | async-done | bytes 466976 | tf_op jit(solution)/shard_map/all_to_all | solution.py:360
  207.0 11.6 %all_to_all.35 = f32[16,8,128]{2,1,0:T(8,128)S(1)} all-to-all(f32[16,8,128]{2,1,0:T(8,128)} %score_kernel.1), channel_id=1, replica_groups=mesh['y'=8,'core'=2,'xl'=2,'zh'=4,'zp'=2,'rep'=2] {'xl','zh','zp'}, dimensions={0} | all-to-all | bytes 131072 | tf_op jit(solution)/shard_map/all_to_all | solution.py:360
  218.7 16.0 %all_to_all.36 = f32[16,1,128]{2,1,0:T(1,128)S(1)} all-to-all(f32[16,1,128]{2,1,0:T(1,128)S(1)} %broadcast_in_dim.23), channel_id=1, replica_groups=mesh['y'=8,'core'=2,'xl'=2,'zh'=4,'zp'=2,'rep'=2] {'y','core'}, dimensions={0} | all-to-all | bytes 16384 | tf_op jit(solution)/shard_map/all_to_all | solution.py:360
  (88 shorter events, 26.0 us)
Async XLA Ops:
  6.5 23.1 %copy-start.12 = (bf16[152,128]{1,0:T(8,128)(2,1)S(1)}, bf16[152,128]{1,0:T(8,128)(2,1)}, u32[]{:S(2)}) copy-start(bf16[152,128]{1,0:T(8,128)(2,1)} %param.32) | copy-start | bytes 116740
  6.5 23.1 %copy-start.11 = (bf16[152,128]{1,0:T(8,128)(2,1)S(1)}, bf16[152,128]{1,0:T(8,128)(2,1)}, u32[]{:S(2)}) copy-start(bf16[152,128]{1,0:T(8,128)(2,1)} %param.36) | copy-start | bytes 116740
  6.5 72.8 %all-gather.4.cloned.1.call-start = ((), (), s32[]{:S(2)}) async-start(), calls=%async_computation.7 | async-start | bytes 7276544 | tf_op jit(solution)/shard_map/all_gather | solution.py:444
  6.5 12.2 %collective-permute-start = (bf16[152,128]{1,0:T(8,128)(2,1)}, bf16[152,128]{1,0:T(8,128)(2,1)S(1)}, u32[]{:S(2)}, u32[]{:S(2)}) collective-permute-start(bf16[152,128]{1,0:T(8,128)(2,1)} %param.28), channel_id=1, source_target_pairs={{16,0},{0,16},{17,1},{1,17},{18,2},{2,18},{19,3},{3,19},{20,4},{4,... | collective-permute-start | bytes 116744 | tf_op jit(solution)/shard_map/ppermute | solution.py:368
  14.1 61.5 %copy-start.7 = (f32[1,192,64]{2,1,0:T(8,128)}, f32[1,192,64]{2,1,0:T(8,128)S(1)}, u32[]{:S(2)}) copy-start(f32[1,192,64]{2,1,0:T(8,128)S(1)} %copy.49) | copy-start | bytes 147460
  18.7 65.8 %copy-start.8 = (bf16[144,128]{1,0:T(8,128)(2,1)}, bf16[144,128]{1,0:T(8,128)(2,1)S(1)}, u32[]{:S(2)}) copy-start(bf16[144,128]{1,0:T(8,128)(2,1)S(1)} %concatenate.19.message_ref) | copy-start | bytes 110596
  18.7 0.8 copy-start.1
  20.4 28.1 %all-to-all-start = ((bf16[16,144,128]{2,1,0:T(8,128)(2,1)}), bf16[16,144,128]{2,1,0:T(8,128)(2,1)S(1)}, u32[]{:S(2)}, u32[]{:S(2)}) async-start(bf16[16,144,128]{2,1,0:T(8,128)(2,1)} %broadcast_in_dim.19), calls=%async_computation | async-start | bytes 1179648 | tf_op jit(solution)/shard_map/all_to_all | solution.py:360
  48.5 36.0 %copy-start = (bf16[16,144,128]{2,1,0:T(8,128)(2,1)}, bf16[16,144,128]{2,1,0:T(8,128)(2,1)S(1)}, u32[]{:S(2)}) copy-start(bf16[16,144,128]{2,1,0:T(8,128)(2,1)S(1)} %all-to-all-done.refs_1_) | copy-start | bytes 1769476
  49.4 19.9 %all-to-all-start.1 = ((f32[16,19,128]{2,1,0:T(8,128)}), f32[16,19,128]{2,1,0:T(8,128)S(1)}, u32[]{:S(2)}, u32[]{:S(2)}) async-start(f32[16,19,128]{2,1,0:T(8,128)} %broadcast_in_dim.20), calls=%async_computation.1 | async-start | bytes 393216 | tf_op jit(solution)/shard_map/all_to_all | solution.py:360
  61.4 117.1 %all-gather.6.cloned.1.call-start = ((), (), s32[]{:S(2)}) async-start(), calls=%async_computation.8 | async-start | bytes 5292032 | tf_op jit(solution)/shard_map/all_gather | solution.py:444
  69.4 0.7 copy-start.9
  84.5 12.4 %collective-permute-start.1 = (bf16[3,192,128]{2,1,0:T(8,128)(2,1)}, bf16[3,192,128]{2,1,0:T(8,128)(2,1)S(1)}, u32[]{:S(2)}, u32[]{:S(2)}) collective-permute-start(bf16[3,192,128]{2,1,0:T(8,128)(2,1)} %project.2.refs_3_), channel_id=1, source_target_pairs={{16,0},{0,16},{17,1},{1,17},{18,2},{2,18},{19,3},{3,19},{20,4},{4,... | collective-permute-start | bytes 442376 | tf_op jit(solution)/shard_map/ppermute | solution.py:368
  96.8 18.6 %copy-start.10 = (f32[1,192,64]{1,2,0:T(8,128)S(1)}, f32[1,192,64]{1,2,0:T(8,128)}, u32[]{:S(2)}) copy-start(f32[1,192,64]{1,2,0:T(8,128)} %param.21) | copy-start | bytes 147460
  106.8 40.0 %copy-start.3 = (bf16[3,192,128]{2,1,0:T(8,128)(2,1)S(1)}, bf16[3,192,128]{2,1,0:T(8,128)(2,1)}, u32[]{:S(2)}) copy-start(bf16[3,192,128]{2,1,0:T(8,128)(2,1)} %project.3) | copy-start | bytes 442372
  106.8 25.9 %all-to-all-start.2 = ((bf16[8,48,608]{2,1,0:T(8,128)(2,1)}), bf16[8,48,608]{2,1,0:T(8,128)(2,1)S(1)}, u32[]{:S(2)}, u32[]{:S(2)}) async-start(bf16[8,48,608]{2,1,0:T(8,128)(2,1)} %attend.2), calls=%async_computation.2 | async-start | bytes 983040 | tf_op jit(solution)/shard_map/all_to_all | solution.py:360
  132.7 0.8 copy-start.5
  138.0 40.5 %all-to-all-start.3 = ((bf16[256,8,128]{2,1,0:T(8,128)(2,1)}), bf16[256,8,128]{2,1,0:T(8,128)(2,1)S(1)}, u32[]{:S(2)}, u32[]{:S(2)}) async-start(bf16[256,8,128]{2,1,0:T(8,128)(2,1)} %broadcast_in_dim.22), calls=%async_computation.3 | async-start | bytes 1048576 | tf_op jit(solution)/shard_map/all_to_all | solution.py:360
  174.1 4.3 %copy-start.2 = (bf16[12,192,128]{2,1,0:T(8,128)(2,1)}, bf16[12,192,128]{2,1,0:T(8,128)(2,1)S(1)}, u32[]{:S(2)}) copy-start(bf16[12,192,128]{2,1,0:T(8,128)(2,1)S(1)} %all-gather) | copy-start | bytes 1769476
  174.1 4.3 %collective-permute-start.2 = (bf16[4,3,192,128]{3,2,1,0:T(8,128)(2,1)S(1)}, bf16[4,3,192,128]{3,2,1,0:T(8,128)(2,1)S(1)}, u32[]{:S(2)}, u32[]{:S(2)}) collective-permute-start(bf16[4,3,192,128]{3,2,1,0:T(8,128)(2,1)S(1)} %bitcast.46), channel_id=1, source_target_pairs={{32,0},{0,32},{33,1},{1,33},{34,2},{2,34},{35,3},{3,35},{36,4},{4,... | collective-permute-start | bytes 1769480 | tf_op jit(solution)/shard_map/ppermute | solution.py:368
  178.4 0.8 copy-start.13
  178.4 1.1 copy-start.4
  192.9 10.7 %all-to-all-start.4 = ((bf16[4,96,608]{2,1,0:T(8,128)(2,1)}), bf16[4,96,608]{2,1,0:T(8,128)(2,1)S(1)}, u32[]{:S(2)}, u32[]{:S(2)}) async-start(bf16[4,96,608]{2,1,0:T(8,128)(2,1)} %attend.3), calls=%async_computation.4 | async-start | bytes 983040 | tf_op jit(solution)/shard_map/all_to_all | solution.py:360
  203.6 0.8 copy-start.6
  (1 other events, 0.7 us)
Sparse Core Ops, SparseCore 0:
  19.7 59.6 all-gather.3
  81.4 47.1 all-gather.5

commit v2 on v1

--- a/solution.py
+++ b/solution.py
@@ -63,14 +63,15 @@
     return (col == row * N_TP + g).astype(f32)
 
 
-def prepare_kernel(high_ref, low_ref, w1_ref, w2_ref, w3_ref, time_ref, shares_ref, hid_high_ref, hid_low_ref, gram_ref):
+def prepare_kernel(high_ref, low_ref, time_ref, shares_ref, *refs):
+    *w_refs, hid_high_ref, hid_low_ref, gram_ref = refs
     pooled = shares_ref[0]
     for g in range(1, N_TP):
         pooled = pooled + shares_ref[g]
     pooled = pooled / PROMPT
     pooled = jnp.concatenate([pooled[k : k + 1] for k in range(D // 128)], axis=1)
     is_one = lax.broadcasted_iota(jnp.int32, (16, D), 0) == 0
-    for net, w_ref in enumerate((w1_ref, w2_ref, w3_ref)):
+    for net, w_ref in enumerate(w_refs):
         bias = jnp.broadcast_to(time_ref[net : net + 1, :] + pooled, (16, D))
         bias = jnp.where(is_one, bias, 0.0)
         for ref, table_ref, part in zip((hid_high_ref, hid_low_ref), (high_ref, low_ref), split2(bias)):
@@ -443,36 +444,33 @@
     def gather(*parts):
         return lax.all_gather(jnp.concatenate(parts, axis=0), SEC, axis=1, tiled=True)
 
-    first = gather(columns(student_qkv), columns(real_qkv), columns(fake_qkv), student_out[None], out_peer)
+    first = gather(columns(student_qkv), student_out[None], out_peer)
 
     one = jax.ShapeDtypeStruct
-    times = jnp.stack([time_embed(t) for t in (step_time, step_time, jnp.float32(1.0))])
-    high, low, gram = call(
-        prepare_kernel,
-        (one((3, BASIS, D), bf16), one((3, BASIS, D), bf16), one((3, BASIS, BASIS), f32)),
-        0,
-        *place_tables(),
-        real_in,
-        fake_in,
-        student_in,
-        times,
-        shares,
+    tables = place_tables()
+
+    def prepare(shares, times, *w_in):
+        n = len(w_in)
+        shapes = (one((n, BASIS, D), bf16), one((n, BASIS, D), bf16), one((n, BASIS, BASIS), f32))
+        return call(prepare_kernel, shapes, 0, *tables, jnp.stack([time_embed(t) for t in times]), shares, *w_in)
+
+    high1, low1, gram1 = prepare(shares, (jnp.float32(1.0),), student_in)
+    first, gram1 = lax.optimization_barrier((first, gram1))
+    real_qkv, fake_qkv, out2, first = lax.optimization_barrier((real_qkv, fake_qkv, out2, first))
+    second = gather(columns(real_qkv), columns(fake_qkv), out2)
+    zero = jnp.int32(0)
+    proj1 = project(jnp.stack([zero, zero]), high1, first)
+    peer1 = shift(proj1, "xl", 2, 1)
+    place, proj1 = lax.optimization_barrier((place, proj1))
+    x12, hidden = call(
+        own_kernel, (one((OWN, BASIS), bf16), one((OWN, D), f32)), 1, place, own, (high1, 1, 0), (low1, 1, 0)
     )
-    first, gram = lax.optimization_barrier((first, gram))
-    out2, first = lax.optimization_barrier((out2, first))
-    wout2 = gather(out2)
-    zero = jnp.int32(0)
-    proj1 = project(jnp.stack([zero, zero + 2]), high, first)
-    peer1 = shift(proj1, "xl", 2, 1)
-    pick = jnp.stack([3 + 3 * core, core])
-    pick, place, proj1 = lax.optimization_barrier((pick, place, proj1))
-    proj2 = project(pick, high, first)
-    x12, hidden = call(
-        own_kernel, (one((OWN, BASIS), bf16), one((OWN, D), f32)), 1, place, own, (high, 1, 2), (low, 1, 2)
-    )
-    proj2, hidden, place = lax.optimization_barrier((proj2, hidden, place))
-    terms = attend(place, base, None, 2, gram, (proj1, peer1), 9, first)
+    place, hidden = lax.optimization_barrier((place, hidden))
+    terms = attend(place, base, None, 0, gram1, (proj1, peer1), 3, first)
+    shares, terms = lax.optimization_barrier((shares, terms))
+    high, low, gram = prepare(shares, (step_time, step_time), real_in, fake_in)
     terms = swap(terms, ("zh", "zp"))
+    terms, gram = lax.optimization_barrier((terms, gram))
     x0, noisy, x12, message = call(
         student_kernel,
         (one((OWN, CH), f32), one((OWN, CH), f32), one((OWN, BASIS), bf16), one((8, 128), bf16)),
@@ -487,11 +485,15 @@
         student_final.T,
         (gram, 2, 0),
     )
-    proj2, message = lax.optimization_barrier((proj2, message))
+    pick = jnp.stack([3 * core, core])
+    pick, message, second = lax.optimization_barrier((pick, message, second))
+    proj2 = project(pick, high, second)
+    near = spread_to(message, TP, N_TP).reshape(N_TP * 8, 128)
+    near, proj2 = lax.optimization_barrier((near, proj2))
     proj2 = lax.all_gather(proj2, "zh", axis=0, tiled=False)
-    everyone = spread_to(message, SEC + TP, N_SEC * N_TP).reshape(N_SEC * N_TP * 8, 128)
+    everyone = spread_to(near, SEC, N_SEC).reshape(N_SEC * N_TP * 8, 128)
     proj2 = (proj2, shift(proj2, "core", 2, 1))
-    terms = attend(place, base, everyone, 0, gram, proj2, 0, wout2)
+    terms = attend(place, base, everyone, 0, gram, proj2, 6, second)
     x12, terms = lax.optimization_barrier((x12, terms))
     hidden = call(
         scores_own_kernel, one((2, OWN, D), f32), 1, place, x12, (high, 2, 0), (low, 2, 0)

time: 245 us -> 245 us (level)
  blocking collectives: 73.2 us -> 62.8 us
  starting transfers between devices: 51.6 us -> 56.8 us
  waiting for transfers between devices: 33.5 us -> 37.4 us
  local copies, waits for them, and re-layouts: 16.4 us -> 13.8 us
    all_gather x1, blocking collectives: 27.3 us -> 14.6 us  [per_device(): proj2 = lax.all_gather(proj2, 'zh', axis=0, tiled=False)]
    all_gather x2, waiting for transfers between devices: 3.73 us -> 10.6 us  [gather(): lax.all_gather(jnp.concatenate(parts, axis=0), SEC, axis=1, tiled=True)]
    all_to_all x5 -> x6, starting transfers between devices: 41.1 us -> 45.4 us  [swap(): return lax.all_to_all(values, axes, 0, 0, tiled=False)]
    unnamed x37 -> x33, local copies, waits for them, and re-layouts: 11.4 us -> 7.11 us
    all_to_all x5 -> x6, waiting for transfers between devices: 28.2 us -> 24.8 us  [swap(): return lax.all_to_all(values, axes, 0, 0, tiled=False)]
    concatenate x0 -> x2, other arithmetic: none -> 2.5 us  [gather(): jnp.concatenate(parts, axis=0)]
    pallas_call x5 -> x6, Pallas kernels: 17.4 us -> 19 us  [call(): pl.pallas_call(kernel, out_shape=shapes, grid=(1,), in_specs=[pl.BlockSpe...]
  transfers between devices with their start and end apart: 10 -> 11, of which waited for: 6 -> 8; matrix products, arithmetic and copies ran while one was open for 6% -> 4% of each run, Pallas kernels for 14% -> 14%
where the time goes in v2:
time: 245 us; the launch traced here: 243 us
  blocking collectives  62.8 us (26%)
  starting transfers between devices  56.8 us (23%)
  Pallas kernels  50.9 us (21%)
  waiting for transfers between devices  37.4 us (15%)
  between operations  15 us (6%)
  local copies, waits for them, and re-layouts  13.8 us (6%)
  other arithmetic  6.41 us (3%)
    all_to_all x6, starting transfers between devices, swap(): return lax.all_to_all(values, axes, 0, 0, tiled=False)  45.4 us
    all_to_all x2, blocking collectives, swap(): return lax.all_to_all(values, axes, 0, 0, tiled=False)  30.1 us
    all_to_all x6, waiting for transfers between devices, swap(): return lax.all_to_all(values, axes, 0, 0, tiled=False)  24.8 us
    pallas_call x2, Pallas kernels, attend(): pl.pallas_call(lambda *refs: attend_kernel(nets, members, packed, wout_at...  22.7 us
    pallas_call x6, Pallas kernels, call(): pl.pallas_call(kernel, out_shape=shapes, grid=(1,), in_specs=[pl.BlockSpe...  19 us
    all_gather x1, blocking collectives, per_device(): out2 = lax.all_gather(out2, 'zh', axis=0, tiled=True)  18.1 us
    all_gather x1, blocking collectives, per_device(): proj2 = lax.all_gather(proj2, 'zh', axis=0, tiled=False)  14.6 us
    ppermute x3, starting transfers between devices, shift(): lax.ppermute(values, axis, [((i + step) % count, i) for i in range(count)])  11.3 us
  transfers between devices with their start and end apart: 11, of which 8 were waited for; matrix products, arithmetic and copies ran while one was open for 4% of the time, Pallas kernels for 14%

profile of v2, /device:TPU:1, one launch (start us, length us, event | category | flops | bytes accessed | tf_op | source)
XLA Modules:
  0.0 243.3 jit_solution(13795371814191761548)
XLA Ops:
  6.5 4.1 %collective-permute-start = (bf16[152,128]{1,0:T(8,128)(2,1)}, bf16[152,128]{1,0:T(8,128)(2,1)S(1)}, u32[]{:S(2)}, u32[]{:S(2)}) collective-permute-start(bf16[152,128]{1,0:T(8,128)(2,1)} %param.28), channel_id=1, source_target_pairs={{16,0},{0,16},{17,1},{1,17},{18,2},{2,18},{19,3},{3,19},{20,4},{4,... | collective-permute-start | bytes 116744 | tf_op jit(solution)/shard_map/ppermute | solution.py:369
  17.8 8.2 %all-to-all-start = ((bf16[16,144,128]{2,1,0:T(8,128)(2,1)}), bf16[16,144,128]{2,1,0:T(8,128)(2,1)S(1)}, u32[]{:S(2)}, u32[]{:S(2)}) async-start(bf16[16,144,128]{2,1,0:T(8,128)(2,1)} %broadcast_in_dim.21), calls=%async_computation | async-start | bytes 1179648 | tf_op jit(solution)/shard_map/all_to_all | solution.py:361
  26.1 18.1 %all_gather.15 = bf16[8,152,128]{2,1,0:T(8,128)(2,1)S(1)} all-gather(bf16[2,152,128]{2,1,0:T(8,128)(2,1)S(1)} %pad_maximum_fusion.2), channel_id=1, replica_groups=mesh['y'=8,'core'=2,'xl'=2,'zh'=4,'zp'=2,'rep'=2] {'zh'}, dimensions={0}, use_global_device_ids=true | all-gather | bytes 389120 | tf_op jit(solution)/shard_map/all_gather | solution.py:435
  46.8 11.9 %all-to-all-start.1 = ((f32[16,19,128]{2,1,0:T(8,128)}), f32[16,19,128]{2,1,0:T(8,128)S(1)}, u32[]{:S(2)}, u32[]{:S(2)}) async-start(f32[16,19,128]{2,1,0:T(8,128)} %broadcast_in_dim.22), calls=%async_computation.1 | async-start | bytes 393216 | tf_op jit(solution)/shard_map/all_to_all | solution.py:361
  59.5 7.2 %all-to-all-done.1.shares_ref = f32[16,19,128]{2,1,0:T(8,128)S(1)} async-done(((f32[16,19,128]{2,1,0:T(8,128)}), f32[16,19,128]{2,1,0:T(8,128)S(1)}, u32[]{:S(2)}, u32[]{:S(2)}) %all-to-all-start.1) | async-done | bytes 155680 | tf_op jit(solution)/shard_map/all_to_all | solution.py:361
  67.4 3.1 %prepare_kernel.2 = (bf16[1,192,2432]{2,1,0:T(8,128)(2,1)}, bf16[1,192,2432]{2,1,0:T(8,128)(2,1)}, f32[1,192,192]{2,1,0:T(8,128)}) custom-call(bf16[112,2432]{1,0:T(8,128)(2,1)} %constant.88.clone.high_ref, bf16[112,2432]{1,0:T(8,128)(2,1)} %constant.89.clone.low_ref, f32[1,2432]{1,0:T(1,128)} %stack.56.time_ref, f32[16,19,128]{2,1,0:T(8,128)} %copy-done.6, ...), custom_call_target="tpu_custom_call" | custom-call | flops 1000000000 | bytes 10000000 | tf_op jit(solution)/shard_map/prepare_kernel/pallas_call | solution.py:348
  71.9 4.6 %project.2.refs_3_ = bf16[3,192,128]{2,1,0:T(8,128)(2,1)} custom-call(s32[2]{0:T(128)} %broadcast_5_pick_ref.2.pick_ref, bf16[1,192,2432]{2,1,0:T(8,128)(2,1)} %get-tuple-element.47.hid_ref.high_ref, bf16[5,2432,128]{2,1,0:T(8,128)(2,1)} %all-gather.4.cloned.1.call-done.w_ref.refs_5_), custom_call_target="tpu_custom_call" | custom-call | flops 358612992 | bytes 3000000 | tf_op jit(solution)/shard_map/project/pallas_call | solution.py:92
  84.1 9.3 %attend.2 = bf16[8,48,608]{2,1,0:T(8,128)(2,1)} custom-call(s32[5]{0:T(128)} %stack.55.place_ref.refs_0_.after_ref, bf16[16,144,128]{2,1,0:T(8,128)(2,1)} %copy-done, f32[1,192,192]{2,1,0:T(8,128)} %get-tuple-element.58.refs_2_, bf16[3,192,128]{2,1,0:T(8,128)(2,1)} %project.2.refs_3_, bf16[3,192,128]{2,1,0:T(8,128)(2,1)} %copy-done.14, ...), custom_call_target="tpu_custom_call" | custom-call | flops 4000000000 | bytes 10000000 | tf_op jit(solution)/shard_map/attend/pallas_call | solution.py:241
  93.5 7.5 %all-to-all-start.2 = ((bf16[8,48,608]{2,1,0:T(8,128)(2,1)}), bf16[8,48,608]{2,1,0:T(8,128)(2,1)S(1)}, u32[]{:S(2)}, u32[]{:S(2)}) async-start(bf16[8,48,608]{2,1,0:T(8,128)(2,1)} %attend.2), calls=%async_computation.2 | async-start | bytes 983040 | tf_op jit(solution)/shard_map/all_to_all | solution.py:361
  103.8 4.0 %prepare_kernel.3 = (bf16[2,192,2432]{2,1,0:T(8,128)(2,1)}, bf16[2,192,2432]{2,1,0:T(8,128)(2,1)}, f32[2,192,192]{2,1,0:T(8,128)}) custom-call(bf16[112,2432]{1,0:T(8,128)(2,1)} %constant.88.clone.high_ref, bf16[112,2432]{1,0:T(8,128)(2,1)} %constant.89.clone.low_ref, f32[2,2432]{1,0:T(2,128)} %pad_maximum_fusion.4.time_ref, f32[16,19,128]{2,1,0:T(8,128)} %copy-done.6, ...), custom_call_target="tpu_custom_call" | custom-call | flops 1000000000 | bytes 10000000 | tf_op jit(solution)/shard_map/prepare_kernel/pallas_call | solution.py:348
  107.9 9.2 %all-to-all-done.2.recv_ref = bf16[8,48,608]{2,1,0:T(8,128)(2,1)S(1)} async-done(((bf16[8,48,608]{2,1,0:T(8,128)(2,1)}), bf16[8,48,608]{2,1,0:T(8,128)(2,1)S(1)}, u32[]{:S(2)}, u32[]{:S(2)}) %all-to-all-start.2) | async-done | bytes 466976 | tf_op jit(solution)/shard_map/all_to_all | solution.py:361
  117.9 3.0 %student_kernel.1 = (f32[12,64]{1,0:T(8,128)}, f32[12,64]{1,0:T(8,128)}, bf16[12,192]{1,0:T(8,128)(2,1)}, bf16[8,128]{1,0:T(8,128)(2,1)}) custom-call(s32[5]{0:T(128)} %stack.55.place_ref.refs_0_.after_ref, f32[1]{0:T(128)} %bitcast.1.time_ref, bf16[8,48,608]{2,1,0:T(8,128)(2,1)} %copy-done.3, f32[12,2432]{1,0:T(8,128)} %get-tuple-element.64.hidden_ref, ...), custom_call_target="tpu_custom_call" | custom-call | flops 1000000000 | bytes 10000000 | tf_op jit(solution)/shard_map/student_kernel/pallas_call | solution.py:348
  120.8 10.6 %all-gather.6.cloned.1.call-done.w_ref.refs_6_ = bf16[14,2432,128]{2,1,0:T(8,128)(2,1)} async-done(((bf16[14,152,128]{2,1,0:T(8,128)(2,1)}), bf16[14,2432,128]{2,1,0:T(8,128)(2,1)}) %all-gather.6.cloned.1.call-update) | async-done | bytes 8716304 | tf_op jit(solution)/shard_map/all_gather | solution.py:445
  132.7 8.1 %all-to-all-start.3 = ((bf16[16,8,128]{2,1,0:T(8,128)(2,1)}), bf16[16,8,128]{2,1,0:T(8,128)(2,1)S(1)}, u32[]{:S(2)}, u32[]{:S(2)}) async-start(bf16[16,8,128]{2,1,0:T(8,128)(2,1)} %broadcast_in_dim.24), calls=%async_computation.3 | async-start | bytes 65536 | tf_op jit(solution)/shard_map/all_to_all | solution.py:361
  140.8 4.6 %project.3 = bf16[3,192,128]{2,1,0:T(8,128)(2,1)} custom-call(s32[2]{0:T(128)} %pad_add_fusion.pick_ref, bf16[2,192,2432]{2,1,0:T(8,128)(2,1)} %get-tuple-element.74.hid_ref.high_ref, bf16[14,2432,128]{2,1,0:T(8,128)(2,1)} %all-gather.6.cloned.1.call-done.w_ref.refs_6_), custom_call_target="tpu_custom_call" | custom-call | flops 358612992 | bytes 3000000 | tf_op jit(solution)/shard_map/project/pallas_call | solution.py:92
  149.1 6.2 %all-to-all-start.4 = ((bf16[16,128,128]{2,1,0:T(8,128)(2,1)}), bf16[16,128,128]{2,1,0:T(8,128)(2,1)S(1)}, u32[]{:S(2)}, u32[]{:S(2)}) async-start(bf16[16,128,128]{2,1,0:T(8,128)(2,1)} %broadcast_in_dim.25), calls=%async_computation.4 | async-start | bytes 1048576 | tf_op jit(solution)/shard_map/all_to_all | solution.py:361
  155.3 14.6 %all-gather = bf16[12,192,128]{2,1,0:T(8,128)(2,1)S(1)} all-gather(bf16[3,192,128]{2,1,0:T(8,128)(2,1)} %project.3), channel_id=2, replica_groups=mesh['y'=8,'core'=2,'xl'=2,'zh'=4,'zp'=2,'rep'=2] {'zh'}, dimensions={0}, use_global_device_ids=true | all-gather | bytes 737280 | tf_op jit(solution)/shard_map/all_gather | solution.py:493
  169.8 4.3 %collective-permute-start.2 = (bf16[4,3,192,128]{3,2,1,0:T(8,128)(2,1)S(1)}, bf16[4,3,192,128]{3,2,1,0:T(8,128)(2,1)S(1)}, u32[]{:S(2)}, u32[]{:S(2)}) collective-permute-start(bf16[4,3,192,128]{3,2,1,0:T(8,128)(2,1)S(1)} %bitcast.43), channel_id=1, source_target_pairs={{32,0},{0,32},{33,1},{1,33},{34,2},{2,34},{35,3},{3,35},{36,4},{4,... | collective-permute-start | bytes 1769480 | tf_op jit(solution)/shard_map/ppermute | solution.py:369
  176.6 13.4 %attend.3 = bf16[4,96,608]{2,1,0:T(8,128)(2,1)} custom-call(s32[5]{0:T(128)} %stack.55.place_ref.refs_0_.after_ref, bf16[16,144,128]{2,1,0:T(8,128)(2,1)} %copy-done, bf16[2048,128]{1,0:T(8,128)(2,1)} %bitcast.45, f32[2,192,192]{2,1,0:T(8,128)} %get-tuple-element.66.gram_ref.refs_3_, bf16[4,3,192,128]{3,2,1,0:T(8,128)(2,1)} %bitcast.44, ...), custom_call_target="tpu_custom_call" | custom-call | flops 8000000000 | bytes 10000000 | tf_op jit(solution)/shard_map/attend/pallas_call | solution.py:241
  190.0 3.5 %all-to-all-start.5 = ((bf16[4,96,608]{2,1,0:T(8,128)(2,1)}), bf16[4,96,608]{2,1,0:T(8,128)(2,1)S(1)}, u32[]{:S(2)}, u32[]{:S(2)}) async-start(bf16[4,96,608]{2,1,0:T(8,128)(2,1)} %attend.3), calls=%async_computation.5 | async-start | bytes 983040 | tf_op jit(solution)/shard_map/all_to_all | solution.py:361
  193.4 3.5 %scores_own_kernel.1.hidden_ref = f32[2,12,2432]{2,1,0:T(8,128)} custom-call(s32[5]{0:T(128)} %stack.55.place_ref.refs_0_.after_ref, bf16[12,192]{1,0:T(8,128)(2,1)} %get-tuple-element.81.x12_ref, bf16[2,192,2432]{2,1,0:T(8,128)(2,1)} %get-tuple-element.74.hid_ref.high_ref, bf16[2,192,2432]{2,1,0:T(8,128)(2,1)} %get-tuple-element.82.low_ref), custom_call_target="tpu_custom_call" | custom-call | flops 1000000000 | bytes 10000000 | tf_op jit(solution)/shard_map/scores_own_kernel/pallas_call | solution.py:348
  196.9 3.9 %all-to-all-done.5.recv_ref = bf16[4,96,608]{2,1,0:T(8,128)(2,1)S(1)} async-done(((bf16[4,96,608]{2,1,0:T(8,128)(2,1)}), bf16[4,96,608]{2,1,0:T(8,128)(2,1)S(1)}, u32[]{:S(2)}, u32[]{:S(2)}) %all-to-all-start.5) | async-done | bytes 466976 | tf_op jit(solution)/shard_map/all_to_all | solution.py:361
  204.2 12.3 %all_to_all.40 = f32[16,8,128]{2,1,0:T(8,128)S(1)} all-to-all(f32[16,8,128]{2,1,0:T(8,128)} %score_kernel.1), channel_id=1, replica_groups=mesh['y'=8,'core'=2,'xl'=2,'zh'=4,'zp'=2,'rep'=2] {'xl','zh','zp'}, dimensions={0} | all-to-all | bytes 131072 | tf_op jit(solution)/shard_map/all_to_all | solution.py:361
  216.6 17.7 %all_to_all.41 = f32[16,1,128]{2,1,0:T(1,128)S(1)} all-to-all(f32[16,1,128]{2,1,0:T(1,128)S(1)} %broadcast_in_dim.26), channel_id=1, replica_groups=mesh['y'=8,'core'=2,'xl'=2,'zh'=4,'zp'=2,'rep'=2] {'y','core'}, dimensions={0} | all-to-all | bytes 16384 | tf_op jit(solution)/shard_map/all_to_all | solution.py:361
  (89 shorter events, 35.5 us)
Async XLA Ops:
  6.5 19.5 %copy-start.11 = (bf16[152,128]{1,0:T(8,128)(2,1)S(1)}, bf16[152,128]{1,0:T(8,128)(2,1)}, u32[]{:S(2)}) copy-start(bf16[152,128]{1,0:T(8,128)(2,1)} %param.36) | copy-start | bytes 116740
  6.5 19.5 %copy-start.12 = (bf16[152,128]{1,0:T(8,128)(2,1)S(1)}, bf16[152,128]{1,0:T(8,128)(2,1)}, u32[]{:S(2)}) copy-start(bf16[152,128]{1,0:T(8,128)(2,1)} %param.32) | copy-start | bytes 116740
  6.5 63.9 %all-gather.4.cloned.1.call-start = ((), (), s32[]{:S(2)}) async-start(), calls=%async_computation.8 | async-start | bytes 3307520 | tf_op jit(solution)/shard_map/all_gather | solution.py:445
  6.5 8.7 %collective-permute-start = (bf16[152,128]{1,0:T(8,128)(2,1)}, bf16[152,128]{1,0:T(8,128)(2,1)S(1)}, u32[]{:S(2)}, u32[]{:S(2)}) collective-permute-start(bf16[152,128]{1,0:T(8,128)(2,1)} %param.28), channel_id=1, source_target_pairs={{16,0},{0,16},{17,1},{1,17},{18,2},{2,18},{19,3},{3,19},{20,4},{4,... | collective-permute-start | bytes 116744 | tf_op jit(solution)/shard_map/ppermute | solution.py:369
  13.1 32.9 %copy-start.5 = (f32[1,192,64]{2,1,0:T(8,128)}, f32[1,192,64]{2,1,0:T(8,128)S(1)}, u32[]{:S(2)}) copy-start(f32[1,192,64]{2,1,0:T(8,128)S(1)} %copy.49) | copy-start | bytes 147460
  15.2 55.2 %copy-start.7 = (bf16[144,128]{1,0:T(8,128)(2,1)}, bf16[144,128]{1,0:T(8,128)(2,1)S(1)}, u32[]{:S(2)}) copy-start(bf16[144,128]{1,0:T(8,128)(2,1)S(1)} %concatenate.21.message_ref) | copy-start | bytes 110596
  17.8 28.1 %all-to-all-start = ((bf16[16,144,128]{2,1,0:T(8,128)(2,1)}), bf16[16,144,128]{2,1,0:T(8,128)(2,1)S(1)}, u32[]{:S(2)}, u32[]{:S(2)}) async-start(bf16[16,144,128]{2,1,0:T(8,128)(2,1)} %broadcast_in_dim.21), calls=%async_computation | async-start | bytes 1179648 | tf_op jit(solution)/shard_map/all_to_all | solution.py:361
  26.1 44.4 %copy-start.8 = (bf16[152,3,128]{2,0,1:T(8,128)(2,1)S(1)}, bf16[152,3,128]{2,0,1:T(8,128)(2,1)}, u32[]{:S(2)}) copy-start(bf16[152,3,128]{2,0,1:T(8,128)(2,1)} %param.35) | copy-start | bytes 350212
  26.1 44.4 %copy-start.9 = (bf16[152,3,128]{2,0,1:T(8,128)(2,1)S(1)}, bf16[152,3,128]{2,0,1:T(8,128)(2,1)}, u32[]{:S(2)}) copy-start(bf16[152,3,128]{2,0,1:T(8,128)(2,1)} %param.31) | copy-start | bytes 350212
  45.9 25.4 %copy-start = (bf16[16,144,128]{2,1,0:T(8,128)(2,1)}, bf16[16,144,128]{2,1,0:T(8,128)(2,1)S(1)}, u32[]{:S(2)}) copy-start(bf16[16,144,128]{2,1,0:T(8,128)(2,1)S(1)} %all-to-all-done.refs_1_) | copy-start | bytes 1769476
  46.8 19.9 %all-to-all-start.1 = ((f32[16,19,128]{2,1,0:T(8,128)}), f32[16,19,128]{2,1,0:T(8,128)S(1)}, u32[]{:S(2)}, u32[]{:S(2)}) async-start(f32[16,19,128]{2,1,0:T(8,128)} %broadcast_in_dim.22), calls=%async_computation.1 | async-start | bytes 393216 | tf_op jit(solution)/shard_map/all_to_all | solution.py:361
  58.7 72.7 %all-gather.6.cloned.1.call-start = ((), (), s32[]{:S(2)}) async-start(), calls=%async_computation.9 | async-start | bytes 9261056 | tf_op jit(solution)/shard_map/all_gather | solution.py:445
  76.5 7.0 %collective-permute-start.1 = (bf16[3,192,128]{2,1,0:T(8,128)(2,1)}, bf16[3,192,128]{2,1,0:T(8,128)(2,1)S(1)}, u32[]{:S(2)}, u32[]{:S(2)}) collective-permute-start(bf16[3,192,128]{2,1,0:T(8,128)(2,1)} %project.2.refs_3_), channel_id=1, source_target_pairs={{16,0},{0,16},{17,1},{1,17},{18,2},{2,18},{19,3},{3,19},{20,4},{4,... | collective-permute-start | bytes 442376 | tf_op jit(solution)/shard_map/ppermute | solution.py:369
  82.9 18.9 %copy-start.10 = (f32[1,192,64]{1,2,0:T(8,128)S(1)}, f32[1,192,64]{1,2,0:T(8,128)}, u32[]{:S(2)}) copy-start(f32[1,192,64]{1,2,0:T(8,128)} %param.21) | copy-start | bytes 147460
  93.5 23.5 %all-to-all-start.2 = ((bf16[8,48,608]{2,1,0:T(8,128)(2,1)}), bf16[8,48,608]{2,1,0:T(8,128)(2,1)S(1)}, u32[]{:S(2)}, u32[]{:S(2)}) async-start(bf16[8,48,608]{2,1,0:T(8,128)(2,1)} %attend.2), calls=%async_computation.2 | async-start | bytes 983040 | tf_op jit(solution)/shard_map/all_to_all | solution.py:361
  117.0 0.8 copy-start.3
  132.7 15.5 %all-to-all-start.3 = ((bf16[16,8,128]{2,1,0:T(8,128)(2,1)}), bf16[16,8,128]{2,1,0:T(8,128)(2,1)S(1)}, u32[]{:S(2)}, u32[]{:S(2)}) async-start(bf16[16,8,128]{2,1,0:T(8,128)(2,1)} %broadcast_in_dim.24), calls=%async_computation.3 | async-start | bytes 65536 | tf_op jit(solution)/shard_map/all_to_all | solution.py:361
  149.1 26.5 %all-to-all-start.4 = ((bf16[16,128,128]{2,1,0:T(8,128)(2,1)}), bf16[16,128,128]{2,1,0:T(8,128)(2,1)S(1)}, u32[]{:S(2)}, u32[]{:S(2)}) async-start(bf16[16,128,128]{2,1,0:T(8,128)(2,1)} %broadcast_in_dim.25), calls=%async_computation.4 | async-start | bytes 1048576 | tf_op jit(solution)/shard_map/all_to_all | solution.py:361
  169.8 5.7 %copy-start.1 = (bf16[12,192,128]{2,1,0:T(8,128)(2,1)}, bf16[12,192,128]{2,1,0:T(8,128)(2,1)S(1)}, u32[]{:S(2)}) copy-start(bf16[12,192,128]{2,1,0:T(8,128)(2,1)S(1)} %all-gather) | copy-start | bytes 1769476
  169.8 5.7 %collective-permute-start.2 = (bf16[4,3,192,128]{3,2,1,0:T(8,128)(2,1)S(1)}, bf16[4,3,192,128]{3,2,1,0:T(8,128)(2,1)S(1)}, u32[]{:S(2)}, u32[]{:S(2)}) collective-permute-start(bf16[4,3,192,128]{3,2,1,0:T(8,128)(2,1)S(1)} %bitcast.43), channel_id=1, source_target_pairs={{32,0},{0,32},{33,1},{1,33},{34,2},{2,34},{35,3},{3,35},{36,4},{4,... | collective-permute-start | bytes 1769480 | tf_op jit(solution)/shard_map/ppermute | solution.py:369
  175.6 0.8 copy-start.13
  175.6 1.0 copy-start.2
  190.0 10.9 %all-to-all-start.5 = ((bf16[4,96,608]{2,1,0:T(8,128)(2,1)}), bf16[4,96,608]{2,1,0:T(8,128)(2,1)S(1)}, u32[]{:S(2)}, u32[]{:S(2)}) async-start(bf16[4,96,608]{2,1,0:T(8,128)(2,1)} %attend.3), calls=%async_computation.5 | async-start | bytes 983040 | tf_op jit(solution)/shard_map/all_to_all | solution.py:361
  200.8 0.8 copy-start.4
  (2 other events, 1.3 us)
Sparse Core Ops, SparseCore 0:
  17.0 51.2 all-gather.3
  71.5 59.8 all-gather.5

commit v3 on v2

--- a/solution.py
+++ b/solution.py
@@ -23,6 +23,7 @@
 N_TP = 16
 LOCAL = 192
 OWN = 12
+DESTS = 8
 TOKENS = 3072
 KEYS = 1536
 QUART = D // 4
@@ -85,7 +86,9 @@
 
 
 def project_kernel(pick_ref, hid_ref, w_ref, out_ref):
-    out_ref[0] = nn(hid_ref[0], w_ref[0]).astype(bf16)
+    out = nn(hid_ref[0], jnp.concatenate([w_ref[k] for k in range(3)], axis=1)).astype(bf16)
+    for k in range(3):
+        out_ref[k] = out[:, k * 128 : (k + 1) * 128]
 
 
 def project(pick, hid, w):
@@ -93,12 +96,12 @@
         project_kernel,
         grid_spec=pltpu.PrefetchScalarGridSpec(
             num_scalar_prefetch=1,
-            grid=(3,),
+            grid=(1,),
             in_specs=[
-                pl.BlockSpec((1, BASIS, D), lambda k, pick: (pick[1], 0, 0)),
-                pl.BlockSpec((1, D, 128), lambda k, pick: (pick[0] + k, 0, 0)),
+                pl.BlockSpec((1, BASIS, D), lambda i, pick: (pick[0], 0, 0)),
+                pl.BlockSpec((3, D, 128), lambda i, pick: (pick[0], 0, 0)),
             ],
-            out_specs=pl.BlockSpec((1, BASIS, 128), lambda k, pick: (k, 0, 0)),
+            out_specs=pl.BlockSpec((3, BASIS, 128), lambda i, pick: (0, 0, 0)),
         ),
         out_shape=jax.ShapeDtypeStruct((3, BASIS, 128), bf16),
         compiler_params=pltpu.CompilerParams(vmem_limit_bytes=VMEM),
@@ -107,17 +110,21 @@
     )(pick, hid, w)
 
 
-def attend_kernel(nets, members, packed, wout_at, place_ref, base_ref, *refs):
+def attend_kernel(members, packed, wout_at, place_ref, base_ref, *refs):
     if packed:
         z_ref, *refs = refs
     gram_ref, *refs = refs
     proj_refs = refs[:-9]
     wout_hbm, out_ref, x_ref, qp_ref, s_ref, sc_ref, wout_ref, z32_ref, sem = refs[-9:]
     s, xl, zh, core = place_ref[0], place_ref[2], place_ref[3], place_ref[4]
-    shares = N_TP // members
-    count = shares * OWN
-    load = pltpu.make_async_copy(wout_hbm.at[pl.ds(wout_at, members * nets)], wout_ref, sem)
-    load.start()
+    count = DESTS * OWN
+    net = core if packed else 0
+    loads = [
+        pltpu.make_async_copy(wout_hbm.at[wout_at + (2 * m + net if packed else m)], wout_ref.at[m], sem.at[m])
+        for m in range(members)
+    ]
+    for load in loads:
+        load.start()
     if packed:
         z32_ref[...] = z_ref[...].astype(f32)
         for sec in range(N_SEC):
@@ -134,15 +141,19 @@
             at = slice(j * 256, (j + 1) * 256)
             x_ref[at, :128] = jnp.where(lane < CH, chunk, x_ref[at, :128])
         own = jnp.concatenate(
-            [x_ref[pl.ds(pl.multiple_of((j * N_SEC + s) * 16, 16), 16), :] for j in range(OWN)], axis=0
+            [
+                x_ref[pl.ds(pl.multiple_of((j * N_SEC + s - core + other) * 16, 16), 16), :]
+                for other in range(2)
+                for j in range(OWN)
+            ],
+            axis=0,
         )
         scales = z32_ref[pl.ds(6, 256, stride=8), :].T
-        for net in range(nets):
-            for j in range(OWN):
-                line = net * 32 + j
-                line = scales[line : line + 1] + scales[line + 16 : line + 17]
-                at = j * 256
-                sc_ref[net, at // KEYS, :, at % KEYS : at % KEYS + 256] = jnp.broadcast_to(line, (8, 256))
+        scales = jnp.where(core == 0, scales[:32], scales[32:64])
+        for j in range(OWN):
+            line = scales[j : j + 1] + scales[j + 16 : j + 17]
+            at = j * 256
+            sc_ref[at // KEYS, :, at % KEYS : at % KEYS + 256] = jnp.broadcast_to(line, (8, 256))
     else:
         for sec in range(N_SEC):
             z, rest, hot = features(base_ref[sec])
@@ -150,124 +161,114 @@
             x_ref[sec * LOCAL : (sec + 1) * LOCAL, :128] = jnp.where(lane < CH, z, rest)
             x_ref[sec * LOCAL : (sec + 1) * LOCAL, COL0:] = hot
         own = x_ref[pl.ds(pl.multiple_of(s * LOCAL, LOCAL), LOCAL), :]
-    row = lax.broadcasted_iota(jnp.int32, (count, LOCAL), 0)
-    col = lax.broadcasted_iota(jnp.int32, (count, LOCAL), 1)
+    row = lax.broadcasted_iota(jnp.int32, (count, own.shape[0]), 0)
+    col = lax.broadcasted_iota(jnp.int32, (count, own.shape[0]), 1)
     share = lax.shift_right_logical(row * 171, 11)
-    if members == 2:
-        owner = xl * 8 + share
+    token = row - share * OWN
+    if packed:
+        half = lax.shift_right_logical(share, 2)
+        owner = lax.bitwise_and(lax.shift_right_logical(share, 1), 1) * 8 + zh * 2 + lax.bitwise_and(share, 1)
+        order = (col == half * LOCAL + token * N_TP + owner).astype(bf16)
     else:
-        owner = lax.shift_right_logical(share, 1) * 8 + zh * 2 + lax.bitwise_and(share, 1)
-    order = (col == (row - share * OWN) * N_TP + owner).astype(bf16)
+        order = (col == token * N_TP + xl * 8 + share).astype(bf16)
     queries = nn(order, own).astype(bf16)
     eye = (
         lax.broadcasted_iota(jnp.int32, (BASIS, BASIS), 0) == lax.broadcasted_iota(jnp.int32, (BASIS, BASIS), 1)
     ).astype(bf16)
     heads = [(member, slice(half * HD, (half + 1) * HD)) for member in range(members) for half in range(2)]
     rows = len(heads) * count
-    for turn in range(nets):
-        net = lax.bitwise_xor(core, turn) if nets == 2 else 0
-        gram_high, gram_low = split2(gram_ref[net])
-        energy = jnp.sum(
-            (nn(queries, gram_high) + nn(queries, gram_low)) * queries.astype(f32), axis=1, keepdims=True
-        )
-        scale = lax.rsqrt(energy / D + EPS)
-
-        def proj(member, kind):
-            if nets == 2:
-                return proj_refs[turn][member, kind]
-            return proj_refs[member][kind]
-
-        for h, (member, part) in enumerate(heads):
-            if part.start == 0:
-                q = (nn(queries, proj(member, 0)) * scale).astype(bf16)
-            qp_ref[h * count : (h + 1) * count, :] = (
-                nt(q[:, part], proj(member, 1)[:, part]) * HD ** (-0.5)
-            ).astype(bf16)
-
-        def score(block, top):
-            keys = x_ref[pl.ds(pl.multiple_of(block * KEYS, KEYS), KEYS), :]
-            if not packed:
-                energy = (nt(gram_high, keys) + nt(gram_low, keys)) * nt(eye, keys)
-                scale = lax.rsqrt(jnp.sum(energy, axis=0, keepdims=True) / D + EPS)
-                sc_ref[net, block] = jnp.broadcast_to(scale, (8, KEYS))
-            scores = nt(qp_ref[...], keys) * sc_ref[net, block][:1]
-            s_ref[block] = scores
-            for part in range(KEYS // 128):
-                top = jnp.maximum(top, scores[:, part * 128 : (part + 1) * 128])
-            return top
-
-        top = lax.fori_loop(0, TOKENS // KEYS, score, jnp.full((rows, 128), -1e30, f32))
-        top = jnp.max(top, axis=1, keepdims=True)
-
-        def mix(block, carry):
-            total, mixed = carry
-            expo = jnp.exp(s_ref[block] - top)
-            for part in range(KEYS // 128):
-                total = total + expo[:, part * 128 : (part + 1) * 128]
-            weights = (expo * sc_ref[net, block][:1]).astype(bf16)
-            keys = x_ref[pl.ds(pl.multiple_of(block * KEYS, KEYS), KEYS), :]
-            return total, mixed + nn(weights, keys)
-
-        total, mixed = lax.fori_loop(
-            0, TOKENS // KEYS, mix, (jnp.zeros((rows, 128), f32), jnp.zeros((rows, BASIS), f32))
-        )
-        mixed = (mixed / jnp.sum(total, axis=1, keepdims=True)).astype(bf16)
-        if turn == 0:
-            load.wait()
-        values = [
-            nn(mixed[h * count : (h + 1) * count], proj(member, 2)[:, part]) for h, (member, part) in enumerate(heads)
-        ]
-        values = jnp.concatenate(values, axis=1).astype(bf16)
-        term = []
-        for part in range(4):
-            at = slice(part * QUART, (part + 1) * QUART)
-            term.append(nt(values, jnp.concatenate([wout_ref[m * nets + net, at, :] for m in range(members)], axis=1)))
-        for d in range(shares):
-            block = jnp.concatenate([t[d * OWN : (d + 1) * OWN] for t in term], axis=0).astype(bf16)
-            if nets == 2:
-                out_ref[d, pl.ds(pl.multiple_of(net * 48, 16), 48), :] = block
-            else:
-                out_ref[d] = block
-
-
-def attend(place, base, z, gram_at, gram, proj, wout_at, wout):
-    nets = 1 if z is None else 2
-    members = 2 if z is None else 4
+    gram_high, gram_low = split2(gram_ref[net])
+    energy = jnp.sum(
+        (nn(queries, gram_high) + nn(queries, gram_low)) * queries.astype(f32), axis=1, keepdims=True
+    )
+    scale = lax.rsqrt(energy / D + EPS)
+
+    def proj(member, kind):
+        return proj_refs[0][member, kind] if packed else proj_refs[member][kind]
+
+    for h, (member, part) in enumerate(heads):
+        if part.start == 0:
+            q = (nn(queries, proj(member, 0)) * scale).astype(bf16)
+        qp_ref[h * count : (h + 1) * count, :] = (
+            nt(q[:, part], proj(member, 1)[:, part]) * HD ** (-0.5)
+        ).astype(bf16)
+
+    def score(block, top):
+        keys = x_ref[pl.ds(pl.multiple_of(block * KEYS, KEYS), KEYS), :]
+        if not packed:
+            energy = (nt(gram_high, keys) + nt(gram_low, keys)) * nt(eye, keys)
+            scale = lax.rsqrt(jnp.sum(energy, axis=0, keepdims=True) / D + EPS)
+            sc_ref[block] = jnp.broadcast_to(scale, (8, KEYS))
+        scores = nt(qp_ref[...], keys) * sc_ref[block][:1]
+        s_ref[block] = scores
+        for part in range(KEYS // 128):
+            top = jnp.maximum(top, scores[:, part * 128 : (part + 1) * 128])
+        return top
+
+    top = lax.fori_loop(0, TOKENS // KEYS, score, jnp.full((rows, 128), -1e30, f32))
+    top = jnp.max(top, axis=1, keepdims=True)
+
+    def mix(block, carry):
+        total, mixed = carry
+        expo = jnp.exp(s_ref[block] - top)
+        for part in range(KEYS // 128):
+            total = total + expo[:, part * 128 : (part + 1) * 128]
+        weights = (expo * sc_ref[block][:1]).astype(bf16)
+        keys = x_ref[pl.ds(pl.multiple_of(block * KEYS, KEYS), KEYS), :]
+        return total, mixed + nn(weights, keys)
+
+    total, mixed = lax.fori_loop(
+        0, TOKENS // KEYS, mix, (jnp.zeros((rows, 128), f32), jnp.zeros((rows, BASIS), f32))
+    )
+    mixed = (mixed / jnp.sum(total, axis=1, keepdims=True)).astype(bf16)
+    for load in loads:
+        load.wait()
+    values = [
+        nn(mixed[h * count : (h + 1) * count], proj(member, 2)[:, part]) for h, (member, part) in enumerate(heads)
+    ]
+    values = jnp.concatenate(values, axis=1).astype(bf16)
+    term = []
+    for part in range(4):
+        at = slice(part * QUART, (part + 1) * QUART)
+        term.append(nt(values, jnp.concatenate([wout_ref[m, at, :] for m in range(members)], axis=1)))
+    for d in range(DESTS):
+        out_ref[d] = jnp.concatenate([t[d * OWN : (d + 1) * OWN] for t in term], axis=0).astype(bf16)
+
+
+def attend(place, base, z, gram, proj, wout_at, wout):
     packed = z is not None
+    members = 4 if packed else 2
     args = (base, z) if packed else (base,)
-    rows = 2 * members * OWN * (N_TP // members)
+    rows = 2 * members * DESTS * OWN
     whole = lambda a: pl.BlockSpec(a.shape, lambda i: (0,) * a.ndim)
-    out = jax.ShapeDtypeStruct((N_TP // members, nets * 4 * OWN, QUART), bf16)
+    out = jax.ShapeDtypeStruct((DESTS, 4 * OWN, QUART), bf16)
     return pl.pallas_call(
-        lambda *refs: attend_kernel(nets, members, packed, wout_at, *refs),
+        lambda *refs: attend_kernel(members, packed, wout_at, *refs),
         out_shape=out,
         grid=(1,),
         in_specs=[pl.BlockSpec(memory_space=pltpu.SMEM)]
-        + [whole(a) for a in args]
-        + [pl.BlockSpec((nets, BASIS, BASIS), lambda i: (gram_at, 0, 0))]
-        + [whole(a) for a in proj]
+        + [whole(a) for a in (*args, gram, *proj)]
         + [pl.BlockSpec(memory_space=pl.ANY)],
         out_specs=whole(out),
         scratch_shapes=[
             pltpu.VMEM((TOKENS, BASIS), bf16),
             pltpu.VMEM((rows, BASIS), bf16),
             pltpu.VMEM((TOKENS // KEYS, rows, KEYS), f32),
-            pltpu.VMEM((nets, TOKENS // KEYS, 8, KEYS), f32),
-            pltpu.VMEM((members * nets, D, 128), bf16),
+            pltpu.VMEM((TOKENS // KEYS, 8, KEYS), f32),
+            pltpu.VMEM((members, D, 128), bf16),
             pltpu.VMEM((N_SEC * N_TP * 8, 128), f32),
-            pltpu.SemaphoreType.DMA,
+            pltpu.SemaphoreType.DMA((members,)),
         ],
         compiler_params=pltpu.CompilerParams(vmem_limit_bytes=VMEM),
-        cost_estimate=pl.CostEstimate(flops=nets * 4 * 10**9, bytes_accessed=10**7, transcendentals=nets * 1200000),
+        cost_estimate=pl.CostEstimate(flops=members * 2 * 10**9, bytes_accessed=10**7, transcendentals=rows * TOKENS),
         name="attend",
     )(place, *args, gram, *proj, wout)
 
 
-def finish(recv_ref, net, hidden, w_final):
-    rows = slice(net * 4 * OWN, (net + 1) * 4 * OWN)
-    terms = recv_ref[0, rows].astype(f32)
-    for d in range(1, recv_ref.shape[0]):
-        terms = terms + recv_ref[d, rows].astype(f32)
+def finish(recv_ref, senders, hidden, w_final):
+    terms = recv_ref[senders[0]].astype(f32)
+    for d in senders[1:]:
+        terms = terms + recv_ref[d].astype(f32)
     afters = []
     energy = jnp.zeros((OWN, 1), f32)
     for part in range(4):
@@ -299,7 +300,7 @@
 ):
     pick = own_tokens(place_ref[1])
     x12 = own12_ref[...]
-    velocity = finish(recv_ref, 0, hidden_ref[...], wf_ref)
+    velocity = finish(recv_ref, range(DESTS), hidden_ref[...], wf_ref)
     exact = lax.Precision.HIGHEST
     noise = jnp.dot(pick, noise_ref[...], precision=exact, preferred_element_type=f32)
     renoise = jnp.dot(pick, renoise_ref[...], precision=exact, preferred_element_type=f32)
@@ -327,8 +328,8 @@
     time_ref, recv_ref, x0_ref, noisy_ref, hidden_ref, wr_ref, wf_ref, send_ref
 ):
     noisy = noisy_ref[...]
-    real = finish(recv_ref, 0, hidden_ref[0], wr_ref)
-    fake = finish(recv_ref, 1, hidden_ref[1], wf_ref)
+    real = finish(recv_ref, range(4), hidden_ref[0], wr_ref)
+    fake = finish(recv_ref, range(4, DESTS), hidden_ref[1], wf_ref)
     t = time_ref[0]
     gap = jnp.abs(x0_ref[...] - (noisy - t * real))
     gap = jnp.sum(jnp.sum(gap, axis=1, keepdims=True), axis=0, keepdims=True)
@@ -410,7 +411,7 @@
 ):
     s = lax.axis_index(SEC)
     g = lax.axis_index(TP)
-    core = lax.axis_index("core")
+    core = lax.axis_index("core").astype(jnp.int32)
     place = jnp.stack([s, g, lax.axis_index("xl"), lax.axis_index("zh"), core]).astype(jnp.int32)
     step_time = renoise_step[0].astype(f32) / 1000.0
 
@@ -458,15 +459,14 @@
     first, gram1 = lax.optimization_barrier((first, gram1))
     real_qkv, fake_qkv, out2, first = lax.optimization_barrier((real_qkv, fake_qkv, out2, first))
     second = gather(columns(real_qkv), columns(fake_qkv), out2)
-    zero = jnp.int32(0)
-    proj1 = project(jnp.stack([zero, zero]), high1, first)
+    proj1 = project(jnp.zeros((1,), jnp.int32), high1, first)
     peer1 = shift(proj1, "xl", 2, 1)
     place, proj1 = lax.optimization_barrier((place, proj1))
     x12, hidden = call(
         own_kernel, (one((OWN, BASIS), bf16), one((OWN, D), f32)), 1, place, own, (high1, 1, 0), (low1, 1, 0)
     )
     place, hidden = lax.optimization_barrier((place, hidden))
-    terms = attend(place, base, None, 0, gram1, (proj1, peer1), 3, first)
+    terms = attend(place, base, None, gram1, (proj1, peer1), 3, first)
     shares, terms = lax.optimization_barrier((shares, terms))
     high, low, gram = prepare(shares, (step_time, step_time), real_in, fake_in)
     terms = swap(terms, ("zh", "zp"))
@@ -485,20 +485,18 @@
         student_final.T,
         (gram, 2, 0),
     )
-    pick = jnp.stack([3 * core, core])
-    pick, message, second = lax.optimization_barrier((pick, message, second))
+    pick, second, unused = lax.optimization_barrier((core[None], second, message))
     proj2 = project(pick, high, second)
     near = spread_to(message, TP, N_TP).reshape(N_TP * 8, 128)
     near, proj2 = lax.optimization_barrier((near, proj2))
     proj2 = lax.all_gather(proj2, "zh", axis=0, tiled=False)
     everyone = spread_to(near, SEC, N_SEC).reshape(N_SEC * N_TP * 8, 128)
-    proj2 = (proj2, shift(proj2, "core", 2, 1))
-    terms = attend(place, base, everyone, 0, gram, proj2, 6, second)
+    terms = attend(place, base, everyone, gram, (proj2,), 6, second)
     x12, terms = lax.optimization_barrier((x12, terms))
     hidden = call(
         scores_own_kernel, one((2, OWN, D), f32), 1, place, x12, (high, 2, 0), (low, 2, 0)
     )
-    terms = swap(terms, ("xl", "zp"))
+    terms = swap(terms, ("core", "xl", "zp"))
     message = call(
         score_kernel,
         one((N_TP, 8, 128), f32),

time: 245 us -> 226 us (0.922)
  starting transfers between devices: 56.8 us -> 48.3 us
  Pallas kernels: 50.9 us -> 45.2 us
  waiting for transfers between devices: 37.4 us -> 33 us
    all_gather x1, blocking collectives: 14.6 us -> 19.1 us  [per_device(): proj2 = lax.all_gather(proj2, 'zh', axis=0, tiled=False)]
    ppermute x3 -> x2, starting transfers between devices: 11.3 us -> 7.01 us  [shift(): lax.ppermute(values, axis, [((i + step) % count, i) for i in range(count)])]
    all_to_all x6, starting transfers between devices: 45.4 us -> 41.2 us  [swap(): return lax.all_to_all(values, axes, 0, 0, tiled=False)]
    pallas_call x2, Pallas kernels: 9.19 us -> 6.23 us  [project(): pl.pallas_call(project_kernel, grid_spec=pltpu.PrefetchScalarGridSpec(num...]
    pallas_call x2, Pallas kernels: 22.7 us -> 19.9 us  [attend(): pl.pallas_call(lambda *refs: attend_kernel(members, packed, wout_at, *ref...]
    all_to_all x2, blocking collectives: 30.1 us -> 27.3 us  [swap(): return lax.all_to_all(values, axes, 0, 0, tiled=False)]
    unnamed x33 -> x29, local copies, waits for them, and re-layouts: 7.11 us -> 6.9 us
  transfers between devices with their start and end apart: 11 -> 10, of which waited for: 8 -> 6; matrix products, arithmetic and copies ran while one was open for 4% -> 5% of each run, Pallas kernels for 14% -> 14%
where the time goes in v3:
time: 226 us; the launch traced here: 225 us
  blocking collectives  64.5 us (29%)
  starting transfers between devices  48.3 us (21%)
  Pallas kernels  45.2 us (20%)
  waiting for transfers between devices  33 us (15%)
  between operations  15 us (7%)
  local copies, waits for them, and re-layouts  13.1 us (6%)
  other arithmetic  5.77 us (3%)
    all_to_all x6, starting transfers between devices, swap(): return lax.all_to_all(values, axes, 0, 0, tiled=False)  41.2 us
    all_to_all x2, blocking collectives, swap(): return lax.all_to_all(values, axes, 0, 0, tiled=False)  27.3 us
    all_to_all x6, waiting for transfers between devices, swap(): return lax.all_to_all(values, axes, 0, 0, tiled=False)  23.8 us
    pallas_call x2, Pallas kernels, attend(): pl.pallas_call(lambda *refs: attend_kernel(members, packed, wout_at, *ref...  19.9 us
    all_gather x1, blocking collectives, per_device(): proj2 = lax.all_gather(proj2, 'zh', axis=0, tiled=False)  19.1 us
    pallas_call x6, Pallas kernels, call(): pl.pallas_call(kernel, out_shape=shapes, grid=(1,), in_specs=[pl.BlockSpe...  19 us
    all_gather x1, blocking collectives, per_device(): out2 = lax.all_gather(out2, 'zh', axis=0, tiled=True)  18.1 us
    all_gather x2, waiting for transfers between devices, gather(): lax.all_gather(jnp.concatenate(parts, axis=0), SEC, axis=1, tiled=True)  8.57 us
  transfers between devices with their start and end apart: 10, of which 6 were waited for; matrix products, arithmetic and copies ran while one was open for 5% of the time, Pallas kernels for 14%

profile of v3, /device:TPU:1, one launch (start us, length us, event | category | flops | bytes accessed | tf_op | source)
XLA Modules:
  0.0 225.0 jit_solution(2673224226879985456)
XLA Ops:
  6.5 4.1 %collective-permute-start = (bf16[152,128]{1,0:T(8,128)(2,1)}, bf16[152,128]{1,0:T(8,128)(2,1)S(1)}, u32[]{:S(2)}, u32[]{:S(2)}) collective-permute-start(bf16[152,128]{1,0:T(8,128)(2,1)} %param.28), channel_id=1, source_target_pairs={{16,0},{0,16},{17,1},{1,17},{18,2},{2,18},{19,3},{3,19},{20,4},{4,... | collective-permute-start | bytes 116744 | tf_op jit(solution)/shard_map/ppermute | solution.py:370
  17.8 8.2 %all-to-all-start = ((bf16[16,144,128]{2,1,0:T(8,128)(2,1)}), bf16[16,144,128]{2,1,0:T(8,128)(2,1)S(1)}, u32[]{:S(2)}, u32[]{:S(2)}) async-start(bf16[16,144,128]{2,1,0:T(8,128)(2,1)} %broadcast_in_dim.21), calls=%async_computation | async-start | bytes 1179648 | tf_op jit(solution)/shard_map/all_to_all | solution.py:362
  26.1 18.1 %all_gather.15 = bf16[8,152,128]{2,1,0:T(8,128)(2,1)S(1)} all-gather(bf16[2,152,128]{2,1,0:T(8,128)(2,1)S(1)} %pad_maximum_fusion.2), channel_id=1, replica_groups=mesh['y'=8,'core'=2,'xl'=2,'zh'=4,'zp'=2,'rep'=2] {'zh'}, dimensions={0}, use_global_device_ids=true | all-gather | bytes 389120 | tf_op jit(solution)/shard_map/all_gather | solution.py:436
  46.8 11.9 %all-to-all-start.1 = ((f32[16,19,128]{2,1,0:T(8,128)}), f32[16,19,128]{2,1,0:T(8,128)S(1)}, u32[]{:S(2)}, u32[]{:S(2)}) async-start(f32[16,19,128]{2,1,0:T(8,128)} %broadcast_in_dim.22), calls=%async_computation.1 | async-start | bytes 393216 | tf_op jit(solution)/shard_map/all_to_all | solution.py:362
  59.5 7.2 %all-to-all-done.1.shares_ref = f32[16,19,128]{2,1,0:T(8,128)S(1)} async-done(((f32[16,19,128]{2,1,0:T(8,128)}), f32[16,19,128]{2,1,0:T(8,128)S(1)}, u32[]{:S(2)}, u32[]{:S(2)}) %all-to-all-start.1) | async-done | bytes 155680 | tf_op jit(solution)/shard_map/all_to_all | solution.py:362
  67.4 3.0 %prepare_kernel.2 = (bf16[1,192,2432]{2,1,0:T(8,128)(2,1)}, bf16[1,192,2432]{2,1,0:T(8,128)(2,1)}, f32[1,192,192]{2,1,0:T(8,128)}) custom-call(bf16[112,2432]{1,0:T(8,128)(2,1)} %constant.87.clone.high_ref, bf16[112,2432]{1,0:T(8,128)(2,1)} %constant.88.clone.low_ref, f32[1,2432]{1,0:T(1,128)} %stack.49.time_ref, f32[16,19,128]{2,1,0:T(8,128)} %copy-done.5, ...), custom_call_target="tpu_custom_call" | custom-call | flops 1000000000 | bytes 10000000 | tf_op jit(solution)/shard_map/prepare_kernel/pallas_call | solution.py:349
  71.4 3.1 %project.2.refs_3_ = bf16[3,192,128]{2,1,0:T(8,128)(2,1)} custom-call(s32[1]{0:T(128)} %constant.72.clone.1.pick_ref, bf16[1,192,2432]{2,1,0:T(8,128)(2,1)} %get-tuple-element.46.hid_ref.high_ref, bf16[5,2432,128]{2,1,0:T(8,128)(2,1)} %all-gather.4.cloned.1.call-done.w_ref.refs_5_), custom_call_target="tpu_custom_call" | custom-call | flops 358612992 | bytes 3000000 | tf_op jit(solution)/shard_map/project/pallas_call | solution.py:95
  74.5 2.9 %collective-permute-start.1 = (bf16[3,192,128]{2,1,0:T(8,128)(2,1)}, bf16[3,192,128]{2,1,0:T(8,128)(2,1)S(1)}, u32[]{:S(2)}, u32[]{:S(2)}) collective-permute-start(bf16[3,192,128]{2,1,0:T(8,128)(2,1)} %project.2.refs_3_), channel_id=1, source_target_pairs={{16,0},{0,16},{17,1},{1,17},{18,2},{2,18},{19,3},{3,19},{20,4},{4,... | collective-permute-start | bytes 442376 | tf_op jit(solution)/shard_map/ppermute | solution.py:370
  82.1 9.3 %attend.2 = bf16[8,48,608]{2,1,0:T(8,128)(2,1)} custom-call(s32[5]{0:T(128)} %stack.48.place_ref.refs_0_.after_ref, bf16[16,144,128]{2,1,0:T(8,128)(2,1)} %copy-done, f32[1,192,192]{2,1,0:T(8,128)} %get-tuple-element.57.refs_2_, bf16[3,192,128]{2,1,0:T(8,128)(2,1)} %project.2.refs_3_, bf16[3,192,128]{2,1,0:T(8,128)(2,1)} %copy-done.12, ...), custom_call_target="tpu_custom_call" | custom-call | flops 4000000000 | bytes 10000000 | tf_op jit(solution)/shard_map/attend/pallas_call | solution.py:245
  91.5 7.2 %all-to-all-start.2 = ((bf16[8,48,608]{2,1,0:T(8,128)(2,1)}), bf16[8,48,608]{2,1,0:T(8,128)(2,1)S(1)}, u32[]{:S(2)}, u32[]{:S(2)}) async-start(bf16[8,48,608]{2,1,0:T(8,128)(2,1)} %attend.2), calls=%async_computation.2 | async-start | bytes 983040 | tf_op jit(solution)/shard_map/all_to_all | solution.py:362
  100.8 4.0 %prepare_kernel.3 = (bf16[2,192,2432]{2,1,0:T(8,128)(2,1)}, bf16[2,192,2432]{2,1,0:T(8,128)(2,1)}, f32[2,192,192]{2,1,0:T(8,128)}) custom-call(bf16[112,2432]{1,0:T(8,128)(2,1)} %constant.87.clone.high_ref, bf16[112,2432]{1,0:T(8,128)(2,1)} %constant.88.clone.low_ref, f32[2,2432]{1,0:T(2,128)} %pad_maximum_fusion.4.time_ref, f32[16,19,128]{2,1,0:T(8,128)} %copy-done.5, ...), custom_call_target="tpu_custom_call" | custom-call | flops 1000000000 | bytes 10000000 | tf_op jit(solution)/shard_map/prepare_kernel/pallas_call | solution.py:349
  104.8 9.6 %all-to-all-done.2.recv_ref = bf16[8,48,608]{2,1,0:T(8,128)(2,1)S(1)} async-done(((bf16[8,48,608]{2,1,0:T(8,128)(2,1)}), bf16[8,48,608]{2,1,0:T(8,128)(2,1)S(1)}, u32[]{:S(2)}, u32[]{:S(2)}) %all-to-all-start.2) | async-done | bytes 466976 | tf_op jit(solution)/shard_map/all_to_all | solution.py:362
  115.2 3.0 %student_kernel.1 = (f32[12,64]{1,0:T(8,128)}, f32[12,64]{1,0:T(8,128)}, bf16[12,192]{1,0:T(8,128)(2,1)}, bf16[8,128]{1,0:T(8,128)(2,1)}) custom-call(s32[5]{0:T(128)} %stack.48.place_ref.refs_0_.after_ref, f32[1]{0:T(128)} %bitcast.1.time_ref, bf16[8,48,608]{2,1,0:T(8,128)(2,1)} %copy-done.2, f32[12,2432]{1,0:T(8,128)} %get-tuple-element.63.hidden_ref, ...), custom_call_target="tpu_custom_call" | custom-call | flops 1000000000 | bytes 10000000 | tf_op jit(solution)/shard_map/student_kernel/pallas_call | solution.py:349
  119.5 3.5 %all-to-all-start.3 = ((bf16[16,8,128]{2,1,0:T(8,128)(2,1)}), bf16[16,8,128]{2,1,0:T(8,128)(2,1)S(1)}, u32[]{:S(2)}, u32[]{:S(2)}) async-start(bf16[16,8,128]{2,1,0:T(8,128)(2,1)} %broadcast_in_dim.24), calls=%async_computation.3 | async-start | bytes 65536 | tf_op jit(solution)/shard_map/all_to_all | solution.py:362
  123.0 8.6 %all-gather.6.cloned.1.call-done.w_ref.refs_5_ = bf16[14,2432,128]{2,1,0:T(8,128)(2,1)} async-done(((bf16[14,152,128]{2,1,0:T(8,128)(2,1)}), bf16[14,2432,128]{2,1,0:T(8,128)(2,1)}) %all-gather.6.cloned.1.call-update) | async-done | bytes 8716304 | tf_op jit(solution)/shard_map/all_gather | solution.py:446
  131.6 3.1 %project.3 = bf16[3,192,128]{2,1,0:T(8,128)(2,1)} custom-call(s32[1]{0:T(128)} %bitcast.6.pick_ref, bf16[2,192,2432]{2,1,0:T(8,128)(2,1)} %get-tuple-element.72.hid_ref.high_ref, bf16[14,2432,128]{2,1,0:T(8,128)(2,1)} %all-gather.6.cloned.1.call-done.w_ref.refs_5_), custom_call_target="tpu_custom_call" | custom-call | flops 358612992 | bytes 3000000 | tf_op jit(solution)/shard_map/project/pallas_call | solution.py:95
  135.6 4.7 %all-to-all-start.4 = ((bf16[16,128,128]{2,1,0:T(8,128)(2,1)}), bf16[16,128,128]{2,1,0:T(8,128)(2,1)S(1)}, u32[]{:S(2)}, u32[]{:S(2)}) async-start(bf16[16,128,128]{2,1,0:T(8,128)(2,1)} %broadcast_in_dim.25), calls=%async_computation.4 | async-start | bytes 1048576 | tf_op jit(solution)/shard_map/all_to_all | solution.py:362
  140.3 19.1 %all-gather = bf16[12,192,128]{2,1,0:T(8,128)(2,1)} all-gather(bf16[3,192,128]{2,1,0:T(8,128)(2,1)} %project.3), channel_id=2, replica_groups=mesh['y'=8,'core'=2,'xl'=2,'zh'=4,'zp'=2,'rep'=2] {'zh'}, dimensions={0}, use_global_device_ids=true | all-gather | bytes 737280 | tf_op jit(solution)/shard_map/all_gather | solution.py:492
  160.3 10.6 %attend.3 = bf16[8,48,608]{2,1,0:T(8,128)(2,1)} custom-call(s32[5]{0:T(128)} %stack.48.place_ref.refs_0_.after_ref, bf16[16,144,128]{2,1,0:T(8,128)(2,1)} %copy-done, bf16[2048,128]{1,0:T(8,128)(2,1)} %bitcast.43, f32[2,192,192]{2,1,0:T(8,128)} %get-tuple-element.65.gram_ref.refs_3_, bf16[4,3,192,128]{3,2,1,0:T(8,128)(2,1)} %bitcast.42, ...), custom_call_target="tpu_custom_call" | custom-call | flops 8000000000 | bytes 10000000 | tf_op jit(solution)/shard_map/attend/pallas_call | solution.py:245
  170.9 5.7 %all-to-all-start.5 = ((bf16[8,48,608]{2,1,0:T(8,128)(2,1)}), bf16[8,48,608]{2,1,0:T(8,128)(2,1)S(1)}, u32[]{:S(2)}, u32[]{:S(2)}) async-start(bf16[8,48,608]{2,1,0:T(8,128)(2,1)} %attend.3), calls=%async_computation.5 | async-start | bytes 983040 | tf_op jit(solution)/shard_map/all_to_all | solution.py:362
  176.6 3.5 %scores_own_kernel.1.hidden_ref = f32[2,12,2432]{2,1,0:T(8,128)} custom-call(s32[5]{0:T(128)} %stack.48.place_ref.refs_0_.after_ref, bf16[12,192]{1,0:T(8,128)(2,1)} %get-tuple-element.79.x12_ref, bf16[2,192,2432]{2,1,0:T(8,128)(2,1)} %get-tuple-element.72.hid_ref.high_ref, bf16[2,192,2432]{2,1,0:T(8,128)(2,1)} %get-tuple-element.80.low_ref), custom_call_target="tpu_custom_call" | custom-call | flops 1000000000 | bytes 10000000 | tf_op jit(solution)/shard_map/scores_own_kernel/pallas_call | solution.py:349
  180.1 5.2 %all-to-all-done.5.recv_ref = bf16[8,48,608]{2,1,0:T(8,128)(2,1)S(1)} async-done(((bf16[8,48,608]{2,1,0:T(8,128)(2,1)}), bf16[8,48,608]{2,1,0:T(8,128)(2,1)S(1)}, u32[]{:S(2)}, u32[]{:S(2)}) %all-to-all-start.5) | async-done | bytes 466976 | tf_op jit(solution)/shard_map/all_to_all | solution.py:362
  188.7 11.4 %all_to_all.40 = f32[16,8,128]{2,1,0:T(8,128)S(1)} all-to-all(f32[16,8,128]{2,1,0:T(8,128)} %score_kernel.1), channel_id=1, replica_groups=mesh['y'=8,'core'=2,'xl'=2,'zh'=4,'zp'=2,'rep'=2] {'xl','zh','zp'}, dimensions={0} | all-to-all | bytes 131072 | tf_op jit(solution)/shard_map/all_to_all | solution.py:362
  200.2 15.9 %all_to_all.41 = f32[16,1,128]{2,1,0:T(1,128)S(1)} all-to-all(f32[16,1,128]{2,1,0:T(1,128)S(1)} %broadcast_in_dim.26), channel_id=1, replica_groups=mesh['y'=8,'core'=2,'xl'=2,'zh'=4,'zp'=2,'rep'=2] {'y','core'}, dimensions={0} | all-to-all | bytes 16384 | tf_op jit(solution)/shard_map/all_to_all | solution.py:362
  (81 shorter events, 27.0 us)
Async XLA Ops:
  6.5 19.5 %copy-start.10 = (bf16[152,128]{1,0:T(8,128)(2,1)S(1)}, bf16[152,128]{1,0:T(8,128)(2,1)}, u32[]{:S(2)}) copy-start(bf16[152,128]{1,0:T(8,128)(2,1)} %param.36) | copy-start | bytes 116740
  6.5 19.5 %copy-start.11 = (bf16[152,128]{1,0:T(8,128)(2,1)S(1)}, bf16[152,128]{1,0:T(8,128)(2,1)}, u32[]{:S(2)}) copy-start(bf16[152,128]{1,0:T(8,128)(2,1)} %param.32) | copy-start | bytes 116740
  6.5 63.9 %all-gather.4.cloned.1.call-start = ((), (), s32[]{:S(2)}) async-start(), calls=%async_computation.8 | async-start | bytes 3307520 | tf_op jit(solution)/shard_map/all_gather | solution.py:446
  6.5 8.7 %collective-permute-start = (bf16[152,128]{1,0:T(8,128)(2,1)}, bf16[152,128]{1,0:T(8,128)(2,1)S(1)}, u32[]{:S(2)}, u32[]{:S(2)}) collective-permute-start(bf16[152,128]{1,0:T(8,128)(2,1)} %param.28), channel_id=1, source_target_pairs={{16,0},{0,16},{17,1},{1,17},{18,2},{2,18},{19,3},{3,19},{20,4},{4,... | collective-permute-start | bytes 116744 | tf_op jit(solution)/shard_map/ppermute | solution.py:370
  13.1 32.9 %copy-start.4 = (f32[1,192,64]{2,1,0:T(8,128)}, f32[1,192,64]{2,1,0:T(8,128)S(1)}, u32[]{:S(2)}) copy-start(f32[1,192,64]{2,1,0:T(8,128)S(1)} %copy.49) | copy-start | bytes 147460
  15.2 55.2 %copy-start.6 = (bf16[144,128]{1,0:T(8,128)(2,1)}, bf16[144,128]{1,0:T(8,128)(2,1)S(1)}, u32[]{:S(2)}) copy-start(bf16[144,128]{1,0:T(8,128)(2,1)S(1)} %concatenate.21.message_ref) | copy-start | bytes 110596
  17.8 28.1 %all-to-all-start = ((bf16[16,144,128]{2,1,0:T(8,128)(2,1)}), bf16[16,144,128]{2,1,0:T(8,128)(2,1)S(1)}, u32[]{:S(2)}, u32[]{:S(2)}) async-start(bf16[16,144,128]{2,1,0:T(8,128)(2,1)} %broadcast_in_dim.21), calls=%async_computation | async-start | bytes 1179648 | tf_op jit(solution)/shard_map/all_to_all | solution.py:362
  26.1 44.4 %copy-start.7 = (bf16[152,3,128]{2,0,1:T(8,128)(2,1)S(1)}, bf16[152,3,128]{2,0,1:T(8,128)(2,1)}, u32[]{:S(2)}) copy-start(bf16[152,3,128]{2,0,1:T(8,128)(2,1)} %param.35) | copy-start | bytes 350212
  26.1 44.4 %copy-start.8 = (bf16[152,3,128]{2,0,1:T(8,128)(2,1)S(1)}, bf16[152,3,128]{2,0,1:T(8,128)(2,1)}, u32[]{:S(2)}) copy-start(bf16[152,3,128]{2,0,1:T(8,128)(2,1)} %param.31) | copy-start | bytes 350212
  45.9 25.4 %copy-start = (bf16[16,144,128]{2,1,0:T(8,128)(2,1)}, bf16[16,144,128]{2,1,0:T(8,128)(2,1)S(1)}, u32[]{:S(2)}) copy-start(bf16[16,144,128]{2,1,0:T(8,128)(2,1)S(1)} %all-to-all-done.refs_1_) | copy-start | bytes 1769476
  46.8 19.9 %all-to-all-start.1 = ((f32[16,19,128]{2,1,0:T(8,128)}), f32[16,19,128]{2,1,0:T(8,128)S(1)}, u32[]{:S(2)}, u32[]{:S(2)}) async-start(f32[16,19,128]{2,1,0:T(8,128)} %broadcast_in_dim.22), calls=%async_computation.1 | async-start | bytes 393216 | tf_op jit(solution)/shard_map/all_to_all | solution.py:362
  58.7 72.9 %all-gather.6.cloned.1.call-start = ((), (), s32[]{:S(2)}) async-start(), calls=%async_computation.9 | async-start | bytes 9261056 | tf_op jit(solution)/shard_map/all_gather | solution.py:446
  66.7 0.7 copy-start.5
  74.5 7.0 %collective-permute-start.1 = (bf16[3,192,128]{2,1,0:T(8,128)(2,1)}, bf16[3,192,128]{2,1,0:T(8,128)(2,1)S(1)}, u32[]{:S(2)}, u32[]{:S(2)}) collective-permute-start(bf16[3,192,128]{2,1,0:T(8,128)(2,1)} %project.2.refs_3_), channel_id=1, source_target_pairs={{16,0},{0,16},{17,1},{1,17},{18,2},{2,18},{19,3},{3,19},{20,4},{4,... | collective-permute-start | bytes 442376 | tf_op jit(solution)/shard_map/ppermute | solution.py:370
  80.9 18.5 %copy-start.9 = (f32[1,192,64]{1,2,0:T(8,128)S(1)}, f32[1,192,64]{1,2,0:T(8,128)}, u32[]{:S(2)}) copy-start(f32[1,192,64]{1,2,0:T(8,128)} %param.21) | copy-start | bytes 147460
  81.5 0.6 copy-start.12
  91.5 23.0 %all-to-all-start.2 = ((bf16[8,48,608]{2,1,0:T(8,128)(2,1)}), bf16[8,48,608]{2,1,0:T(8,128)(2,1)S(1)}, u32[]{:S(2)}, u32[]{:S(2)}) async-start(bf16[8,48,608]{2,1,0:T(8,128)(2,1)} %attend.2), calls=%async_computation.2 | async-start | bytes 983040 | tf_op jit(solution)/shard_map/all_to_all | solution.py:362
  114.4 0.8 copy-start.2
  119.5 15.2 %all-to-all-start.3 = ((bf16[16,8,128]{2,1,0:T(8,128)(2,1)}), bf16[16,8,128]{2,1,0:T(8,128)(2,1)S(1)}, u32[]{:S(2)}, u32[]{:S(2)}) async-start(bf16[16,8,128]{2,1,0:T(8,128)(2,1)} %broadcast_in_dim.24), calls=%async_computation.3 | async-start | bytes 65536 | tf_op jit(solution)/shard_map/all_to_all | solution.py:362
  135.6 23.9 %all-to-all-start.4 = ((bf16[16,128,128]{2,1,0:T(8,128)(2,1)}), bf16[16,128,128]{2,1,0:T(8,128)(2,1)S(1)}, u32[]{:S(2)}, u32[]{:S(2)}) async-start(bf16[16,128,128]{2,1,0:T(8,128)(2,1)} %broadcast_in_dim.25), calls=%async_computation.4 | async-start | bytes 1048576 | tf_op jit(solution)/shard_map/all_to_all | solution.py:362
  159.5 0.8 copy-start.1
  170.9 14.4 %all-to-all-start.5 = ((bf16[8,48,608]{2,1,0:T(8,128)(2,1)}), bf16[8,48,608]{2,1,0:T(8,128)(2,1)S(1)}, u32[]{:S(2)}, u32[]{:S(2)}) async-start(bf16[8,48,608]{2,1,0:T(8,128)(2,1)} %attend.3), calls=%async_computation.5 | async-start | bytes 983040 | tf_op jit(solution)/shard_map/all_to_all | solution.py:362
  185.3 0.8 copy-start.3
Sparse Core Ops, SparseCore 0:
  17.0 51.0 all-gather.3
  71.5 60.0 all-gather.5

commit v4 on v3

--- a/solution.py
+++ b/solution.py
@@ -99,7 +99,7 @@
             grid=(1,),
             in_specs=[
                 pl.BlockSpec((1, BASIS, D), lambda i, pick: (pick[0], 0, 0)),
-                pl.BlockSpec((3, D, 128), lambda i, pick: (pick[0], 0, 0)),
+                pl.BlockSpec((3, D, 128), lambda i, pick: (pick[1], 0, 0)),
             ],
             out_specs=pl.BlockSpec((3, BASIS, 128), lambda i, pick: (0, 0, 0)),
         ),
@@ -120,7 +120,7 @@
     count = DESTS * OWN
     net = core if packed else 0
     loads = [
-        pltpu.make_async_copy(wout_hbm.at[wout_at + (2 * m + net if packed else m)], wout_ref.at[m], sem.at[m])
+        pltpu.make_async_copy(wout_hbm.at[wout_at + m], wout_ref.at[m], sem.at[m])
         for m in range(members)
     ]
     for load in loads:
@@ -455,11 +455,20 @@
         shapes = (one((n, BASIS, D), bf16), one((n, BASIS, D), bf16), one((n, BASIS, BASIS), f32))
         return call(prepare_kernel, shapes, 0, *tables, jnp.stack([time_embed(t) for t in times]), shares, *w_in)
 
+    def pack(qkv, net):
+        return jnp.concatenate([columns(qkv), out2.reshape(4, 2, *student_out.shape)[:, net]], axis=0)
+
+    both = (pack(real_qkv, 0), pack(fake_qkv, 1))
+    mine = jnp.where(core == 0, both[0], both[1])
+    peer = jnp.where(core == 0, both[1], both[0])
+    peer, mine, shares = lax.optimization_barrier((peer, mine, shares))
+    peer = shift(peer, "core", 2, 1)
+    second = jnp.concatenate([jnp.where(core == 0, mine, peer), jnp.where(core == 0, peer, mine)], axis=1)
     high1, low1, gram1 = prepare(shares, (jnp.float32(1.0),), student_in)
     first, gram1 = lax.optimization_barrier((first, gram1))
-    real_qkv, fake_qkv, out2, first = lax.optimization_barrier((real_qkv, fake_qkv, out2, first))
-    second = gather(columns(real_qkv), columns(fake_qkv), out2)
-    proj1 = project(jnp.zeros((1,), jnp.int32), high1, first)
+    second, first = lax.optimization_barrier((second, first))
+    second = lax.all_gather(second, "y", axis=1, tiled=True)
+    proj1 = project(jnp.zeros((2,), jnp.int32), high1, first)
     peer1 = shift(proj1, "xl", 2, 1)
     place, proj1 = lax.optimization_barrier((place, proj1))
     x12, hidden = call(
@@ -485,13 +494,12 @@
         student_final.T,
         (gram, 2, 0),
     )
-    pick, second, unused = lax.optimization_barrier((core[None], second, message))
+    near = spread_to(message, TP, N_TP).reshape(N_TP * 8, 128)
+    pick, second, unused = lax.optimization_barrier((jnp.stack([core, core * 0]), second, message))
     proj2 = project(pick, high, second)
-    near = spread_to(message, TP, N_TP).reshape(N_TP * 8, 128)
-    near, proj2 = lax.optimization_barrier((near, proj2))
     proj2 = lax.all_gather(proj2, "zh", axis=0, tiled=False)
     everyone = spread_to(near, SEC, N_SEC).reshape(N_SEC * N_TP * 8, 128)
-    terms = attend(place, base, everyone, gram, (proj2,), 6, second)
+    terms = attend(place, base, everyone, gram, (proj2,), 3, second)
     x12, terms = lax.optimization_barrier((x12, terms))
     hidden = call(
         scores_own_kernel, one((2, OWN, D), f32), 1, place, x12, (high, 2, 0), (low, 2, 0)

time: 226 us -> 225 us (level)
  waiting for transfers between devices: 33 us -> 25.1 us
  blocking collectives: 64.5 us -> 71.7 us
    all_to_all x2 -> x3, blocking collectives: 27.3 us -> 37.5 us  [swap(): return lax.all_to_all(values, axes, 0, 0, tiled=False)]
    all_gather x2 -> x1, waiting for transfers between devices: 8.57 us -> 0.01 us  [gather(): lax.all_gather(jnp.concatenate(parts, axis=0), SEC, axis=1, tiled=True)]
    all_gather x1, blocking collectives: 19.1 us -> 16.1 us  [per_device(): proj2 = lax.all_gather(proj2, 'zh', axis=0, tiled=False)]
    all_to_all x6 -> x5, starting transfers between devices: 41.2 us -> 38.5 us  [swap(): return lax.all_to_all(values, axes, 0, 0, tiled=False)]
    ppermute x2 -> x3, starting transfers between devices: 7.01 us -> 8.87 us  [shift(): lax.ppermute(values, axis, [((i + step) % count, i) for i in range(count)])]
    unnamed x29 -> x33, local copies, waits for them, and re-layouts: 6.9 us -> 6.21 us
    all_to_all x6 -> x5, waiting for transfers between devices: 23.8 us -> 24.4 us  [swap(): return lax.all_to_all(values, axes, 0, 0, tiled=False)]
  transfers between devices with their start and end apart: 10 -> 10, of which waited for: 6 -> 5; matrix products, arithmetic and copies ran while one was open for 5% -> 6% of each run, Pallas kernels for 14% -> 15%
where the time goes in v4:
time: 225 us; the launch traced here: 224 us
  blocking collectives  71.7 us (32%)
  starting transfers between devices  47.5 us (21%)
  Pallas kernels  46.5 us (21%)
  waiting for transfers between devices  25.1 us (11%)
  between operations  15.1 us (7%)
  local copies, waits for them, and re-layouts  12.4 us (6%)
  other arithmetic  5.68 us (3%)
    all_to_all x5, starting transfers between devices, swap(): return lax.all_to_all(values, axes, 0, 0, tiled=False)  38.5 us
    all_to_all x3, blocking collectives, swap(): return lax.all_to_all(values, axes, 0, 0, tiled=False)  37.5 us
    all_to_all x5, waiting for transfers between devices, swap(): return lax.all_to_all(values, axes, 0, 0, tiled=False)  24.4 us
    pallas_call x2, Pallas kernels, attend(): pl.pallas_call(lambda *refs: attend_kernel(members, packed, wout_at, *ref...  19.9 us
    pallas_call x6, Pallas kernels, call(): pl.pallas_call(kernel, out_shape=shapes, grid=(1,), in_specs=[pl.BlockSpe...  19 us
    all_gather x1, blocking collectives, per_device(): out2 = lax.all_gather(out2, 'zh', axis=0, tiled=True)  18.1 us
    all_gather x1, blocking collectives, per_device(): proj2 = lax.all_gather(proj2, 'zh', axis=0, tiled=False)  16.1 us
    ppermute x3, starting transfers between devices, shift(): lax.ppermute(values, axis, [((i + step) % count, i) for i in range(count)])  8.87 us
  transfers between devices with their start and end apart: 10, of which 5 were waited for; matrix products, arithmetic and copies ran while one was open for 6% of the time, Pallas kernels for 15%

profile of v4, /device:TPU:1, one launch (start us, length us, event | category | flops | bytes accessed | tf_op | source)
XLA Modules:
  0.0 224.1 jit_solution(17463194173683161017)
XLA Ops:
  6.5 4.1 %collective-permute-start = (bf16[152,128]{1,0:T(8,128)(2,1)}, bf16[152,128]{1,0:T(8,128)(2,1)S(1)}, u32[]{:S(2)}, u32[]{:S(2)}) collective-permute-start(bf16[152,128]{1,0:T(8,128)(2,1)} %param.28), channel_id=1, source_target_pairs={{16,0},{0,16},{17,1},{1,17},{18,2},{2,18},{19,3},{3,19},{20,4},{4,... | collective-permute-start | bytes 116744 | tf_op jit(solution)/shard_map/ppermute | solution.py:370
  16.9 8.2 %all-to-all-start = ((bf16[16,144,128]{2,1,0:T(8,128)(2,1)}), bf16[16,144,128]{2,1,0:T(8,128)(2,1)S(1)}, u32[]{:S(2)}, u32[]{:S(2)}) async-start(bf16[16,144,128]{2,1,0:T(8,128)(2,1)} %broadcast_in_dim.23), calls=%async_computation | async-start | bytes 1179648 | tf_op jit(solution)/shard_map/all_to_all | solution.py:362
  25.2 18.1 %all_gather.15 = bf16[8,152,128]{2,1,0:T(8,128)(2,1)S(1)} all-gather(bf16[2,152,128]{2,1,0:T(8,128)(2,1)S(1)} %pad_maximum_fusion.4), channel_id=1, replica_groups=mesh['y'=8,'core'=2,'xl'=2,'zh'=4,'zp'=2,'rep'=2] {'zh'}, dimensions={0}, use_global_device_ids=true | all-gather | bytes 389120 | tf_op jit(solution)/shard_map/all_gather | solution.py:436
  45.9 11.9 %all-to-all-start.1 = ((f32[16,19,128]{2,1,0:T(8,128)}), f32[16,19,128]{2,1,0:T(8,128)S(1)}, u32[]{:S(2)}, u32[]{:S(2)}) async-start(f32[16,19,128]{2,1,0:T(8,128)} %broadcast_in_dim.24), calls=%async_computation.1 | async-start | bytes 393216 | tf_op jit(solution)/shard_map/all_to_all | solution.py:362
  58.0 7.8 %all-to-all-done.1.shares_ref = f32[16,19,128]{2,1,0:T(8,128)S(1)} async-done(((f32[16,19,128]{2,1,0:T(8,128)}), f32[16,19,128]{2,1,0:T(8,128)S(1)}, u32[]{:S(2)}, u32[]{:S(2)}) %all-to-all-start.1) | async-done | bytes 155680 | tf_op jit(solution)/shard_map/all_to_all | solution.py:362
  68.5 3.1 %prepare_kernel.2 = (bf16[1,192,2432]{2,1,0:T(8,128)(2,1)}, bf16[1,192,2432]{2,1,0:T(8,128)(2,1)}, f32[1,192,192]{2,1,0:T(8,128)}) custom-call(bf16[112,2432]{1,0:T(8,128)(2,1)} %constant.88.clone.high_ref, bf16[112,2432]{1,0:T(8,128)(2,1)} %constant.89.clone.low_ref, f32[1,2432]{1,0:T(1,128)} %stack.53.time_ref, f32[16,19,128]{2,1,0:T(8,128)} %copy-done.5, ...), custom_call_target="tpu_custom_call" | custom-call | flops 1000000000 | bytes 10000000 | tf_op jit(solution)/shard_map/prepare_kernel/pallas_call | solution.py:349
  73.2 3.8 %project.2.refs_3_ = bf16[3,192,128]{2,1,0:T(8,128)(2,1)} custom-call(s32[2]{0:T(128)} %broadcast_5_pick_ref.2.pick_ref, bf16[1,192,2432]{2,1,0:T(8,128)(2,1)} %get-tuple-element.47.hid_ref.high_ref, bf16[5,2432,128]{2,1,0:T(8,128)(2,1)} %all-gather.4.cloned.1.call-done.w_ref.refs_5_), custom_call_target="tpu_custom_call" | custom-call | flops 358612992 | bytes 3000000 | tf_op jit(solution)/shard_map/project/pallas_call | solution.py:95
  76.9 2.9 %collective-permute-start.2 = (bf16[3,192,128]{2,1,0:T(8,128)(2,1)}, bf16[3,192,128]{2,1,0:T(8,128)(2,1)S(1)}, u32[]{:S(2)}, u32[]{:S(2)}) collective-permute-start(bf16[3,192,128]{2,1,0:T(8,128)(2,1)} %project.2.refs_3_), channel_id=1, source_target_pairs={{16,0},{0,16},{17,1},{1,17},{18,2},{2,18},{19,3},{3,19},{20,4},{4,... | collective-permute-start | bytes 442376 | tf_op jit(solution)/shard_map/ppermute | solution.py:370
  80.5 2.9 %own_kernel.1 = (bf16[12,192]{1,0:T(8,128)(2,1)}, f32[12,2432]{1,0:T(8,128)}) custom-call(s32[5]{0:T(128)} %stack.52.place_ref.refs_0_.after_ref, bf16[144,128]{1,0:T(8,128)(2,1)} %copy-done.6, bf16[1,192,2432]{2,1,0:T(8,128)(2,1)} %get-tuple-element.47.hid_ref.high_ref, bf16[1,192,2432]{2,1,0:T(8,128)(2,1)} %get-tuple-element.56.low_ref), custom_call_target="tpu_custom_call" | custom-call | flops 1000000000 | bytes 10000000 | tf_op jit(solution)/shard_map/own_kernel/pallas_call | solution.py:349
  84.6 9.3 %attend.2 = bf16[8,48,608]{2,1,0:T(8,128)(2,1)} custom-call(s32[5]{0:T(128)} %stack.52.place_ref.refs_0_.after_ref, bf16[16,144,128]{2,1,0:T(8,128)(2,1)} %copy-done, f32[1,192,192]{2,1,0:T(8,128)} %get-tuple-element.59.refs_2_, bf16[3,192,128]{2,1,0:T(8,128)(2,1)} %project.2.refs_3_, bf16[3,192,128]{2,1,0:T(8,128)(2,1)} %copy-done.14, ...), custom_call_target="tpu_custom_call" | custom-call | flops 4000000000 | bytes 10000000 | tf_op jit(solution)/shard_map/attend/pallas_call | solution.py:245
  94.0 4.2 %all-to-all-start.2 = ((bf16[8,48,608]{2,1,0:T(8,128)(2,1)}), bf16[8,48,608]{2,1,0:T(8,128)(2,1)S(1)}, u32[]{:S(2)}, u32[]{:S(2)}) async-start(bf16[8,48,608]{2,1,0:T(8,128)(2,1)} %attend.2), calls=%async_computation.2 | async-start | bytes 983040 | tf_op jit(solution)/shard_map/all_to_all | solution.py:362
  100.4 4.0 %prepare_kernel.3 = (bf16[2,192,2432]{2,1,0:T(8,128)(2,1)}, bf16[2,192,2432]{2,1,0:T(8,128)(2,1)}, f32[2,192,192]{2,1,0:T(8,128)}) custom-call(bf16[112,2432]{1,0:T(8,128)(2,1)} %constant.88.clone.high_ref, bf16[112,2432]{1,0:T(8,128)(2,1)} %constant.89.clone.low_ref, f32[2,2432]{1,0:T(2,128)} %pad_maximum_fusion.6.time_ref, f32[16,19,128]{2,1,0:T(8,128)} %copy-done.5, ...), custom_call_target="tpu_custom_call" | custom-call | flops 1000000000 | bytes 10000000 | tf_op jit(solution)/shard_map/prepare_kernel/pallas_call | solution.py:349
  104.4 9.6 %all-to-all-done.2.recv_ref = bf16[8,48,608]{2,1,0:T(8,128)(2,1)S(1)} async-done(((bf16[8,48,608]{2,1,0:T(8,128)(2,1)}), bf16[8,48,608]{2,1,0:T(8,128)(2,1)S(1)}, u32[]{:S(2)}, u32[]{:S(2)}) %all-to-all-start.2) | async-done | bytes 466976 | tf_op jit(solution)/shard_map/all_to_all | solution.py:362
  114.9 2.9 %student_kernel.1 = (f32[12,64]{1,0:T(8,128)}, f32[12,64]{1,0:T(8,128)}, bf16[12,192]{1,0:T(8,128)(2,1)}, bf16[8,128]{1,0:T(8,128)(2,1)}) custom-call(s32[5]{0:T(128)} %stack.52.place_ref.refs_0_.after_ref, f32[1]{0:T(128)} %bitcast.1.time_ref, bf16[8,48,608]{2,1,0:T(8,128)(2,1)} %copy-done.2, f32[12,2432]{1,0:T(8,128)} %get-tuple-element.65.hidden_ref, ...), custom_call_target="tpu_custom_call" | custom-call | flops 1000000000 | bytes 10000000 | tf_op jit(solution)/shard_map/student_kernel/pallas_call | solution.py:349
  118.4 9.9 %all_to_all.40 = bf16[16,8,128]{2,1,0:T(8,128)(2,1)S(1)} all-to-all(bf16[16,8,128]{2,1,0:T(8,128)(2,1)S(1)} %broadcast_in_dim.26), channel_id=1, replica_groups=mesh['y'=8,'core'=2,'xl'=2,'zh'=4,'zp'=2,'rep'=2] {'xl','zh','zp'}, dimensions={0} | all-to-all | bytes 65536 | tf_op jit(solution)/shard_map/all_to_all | solution.py:362
  129.3 9.3 %all-to-all-start.4 = ((bf16[16,128,128]{2,1,0:T(8,128)(2,1)}), bf16[16,128,128]{2,1,0:T(8,128)(2,1)S(1)}, u32[]{:S(2)}, u32[]{:S(2)}) async-start(bf16[16,128,128]{2,1,0:T(8,128)(2,1)} %broadcast_in_dim.56), calls=%async_computation.4 | async-start | bytes 1048576 | tf_op jit(solution)/shard_map/all_to_all | solution.py:362
  139.2 3.8 %project.3 = bf16[3,192,128]{2,1,0:T(8,128)(2,1)} custom-call(s32[2]{0:T(128)} %pad_add_fusion.pick_ref, bf16[2,192,2432]{2,1,0:T(8,128)(2,1)} %get-tuple-element.72.hid_ref.high_ref, bf16[7,2432,128]{2,1,0:T(8,128)(2,1)} %all-gather.6.cloned.1.call-done.w_ref.refs_5_), custom_call_target="tpu_custom_call" | custom-call | flops 358612992 | bytes 3000000 | tf_op jit(solution)/shard_map/project/pallas_call | solution.py:95
  143.0 16.1 %all-gather = bf16[12,192,128]{2,1,0:T(8,128)(2,1)} all-gather(bf16[3,192,128]{2,1,0:T(8,128)(2,1)} %project.3), channel_id=2, replica_groups=mesh['y'=8,'core'=2,'xl'=2,'zh'=4,'zp'=2,'rep'=2] {'zh'}, dimensions={0}, use_global_device_ids=true | all-gather | bytes 737280 | tf_op jit(solution)/shard_map/all_gather | solution.py:500
  159.9 10.6 %attend.3 = bf16[8,48,608]{2,1,0:T(8,128)(2,1)} custom-call(s32[5]{0:T(128)} %stack.52.place_ref.refs_0_.after_ref, bf16[16,144,128]{2,1,0:T(8,128)(2,1)} %copy-done, bf16[2048,128]{1,0:T(8,128)(2,1)} %bitcast.53, f32[2,192,192]{2,1,0:T(8,128)} %get-tuple-element.67.gram_ref.refs_3_, bf16[4,3,192,128]{3,2,1,0:T(8,128)(2,1)} %bitcast.52, ...), custom_call_target="tpu_custom_call" | custom-call | flops 8000000000 | bytes 10000000 | tf_op jit(solution)/shard_map/attend/pallas_call | solution.py:245
  170.5 4.9 %all-to-all-start.5 = ((bf16[8,48,608]{2,1,0:T(8,128)(2,1)}), bf16[8,48,608]{2,1,0:T(8,128)(2,1)S(1)}, u32[]{:S(2)}, u32[]{:S(2)}) async-start(bf16[8,48,608]{2,1,0:T(8,128)(2,1)} %attend.3), calls=%async_computation.5 | async-start | bytes 983040 | tf_op jit(solution)/shard_map/all_to_all | solution.py:362
  175.3 3.4 %scores_own_kernel.1.hidden_ref = f32[2,12,2432]{2,1,0:T(8,128)} custom-call(s32[5]{0:T(128)} %stack.52.place_ref.refs_0_.after_ref, bf16[12,192]{1,0:T(8,128)(2,1)} %get-tuple-element.77.x12_ref, bf16[2,192,2432]{2,1,0:T(8,128)(2,1)} %get-tuple-element.72.hid_ref.high_ref, bf16[2,192,2432]{2,1,0:T(8,128)(2,1)} %get-tuple-element.78.low_ref), custom_call_target="tpu_custom_call" | custom-call | flops 1000000000 | bytes 10000000 | tf_op jit(solution)/shard_map/scores_own_kernel/pallas_call | solution.py:349
  178.8 5.3 %all-to-all-done.5.recv_ref = bf16[8,48,608]{2,1,0:T(8,128)(2,1)S(1)} async-done(((bf16[8,48,608]{2,1,0:T(8,128)(2,1)}), bf16[8,48,608]{2,1,0:T(8,128)(2,1)S(1)}, u32[]{:S(2)}, u32[]{:S(2)}) %all-to-all-start.5) | async-done | bytes 466976 | tf_op jit(solution)/shard_map/all_to_all | solution.py:362
  187.4 11.8 %all_to_all.41 = f32[16,8,128]{2,1,0:T(8,128)S(1)} all-to-all(f32[16,8,128]{2,1,0:T(8,128)} %score_kernel.1), channel_id=1, replica_groups=mesh['y'=8,'core'=2,'xl'=2,'zh'=4,'zp'=2,'rep'=2] {'xl','zh','zp'}, dimensions={0} | all-to-all | bytes 131072 | tf_op jit(solution)/shard_map/all_to_all | solution.py:362
  199.3 15.8 %all_to_all.42 = f32[16,1,128]{2,1,0:T(1,128)S(1)} all-to-all(f32[16,1,128]{2,1,0:T(1,128)S(1)} %broadcast_in_dim.57), channel_id=1, replica_groups=mesh['y'=8,'core'=2,'xl'=2,'zh'=4,'zp'=2,'rep'=2] {'y','core'}, dimensions={0} | all-to-all | bytes 16384 | tf_op jit(solution)/shard_map/all_to_all | solution.py:362
  (91 shorter events, 25.3 us)
Async XLA Ops:
  6.5 8.7 %copy-start.11 = (bf16[152,128]{1,0:T(8,128)(2,1)S(1)}, bf16[152,128]{1,0:T(8,128)(2,1)}, u32[]{:S(2)}) copy-start(bf16[152,128]{1,0:T(8,128)(2,1)} %param.28) | copy-start | bytes 116740
  6.5 8.7 %copy-start.7 = (bf16[152,3,128]{2,0,1:T(8,128)(2,1)S(1)}, bf16[152,3,128]{2,0,1:T(8,128)(2,1)}, u32[]{:S(2)}) copy-start(bf16[152,3,128]{2,0,1:T(8,128)(2,1)} %param.27) | copy-start | bytes 350212
  6.5 66.1 %all-gather.4.cloned.1.call-start = ((), (), s32[]{:S(2)}) async-start(), calls=%async_computation.8 | async-start | bytes 3307520 | tf_op jit(solution)/shard_map/all_gather | solution.py:446
  6.5 8.7 %collective-permute-start = (bf16[152,128]{1,0:T(8,128)(2,1)}, bf16[152,128]{1,0:T(8,128)(2,1)S(1)}, u32[]{:S(2)}, u32[]{:S(2)}) collective-permute-start(bf16[152,128]{1,0:T(8,128)(2,1)} %param.28), channel_id=1, source_target_pairs={{16,0},{0,16},{17,1},{1,17},{18,2},{2,18},{19,3},{3,19},{20,4},{4,... | collective-permute-start | bytes 116744 | tf_op jit(solution)/shard_map/ppermute | solution.py:370
  11.6 5.3 %copy-start.4 = (f32[1,192,64]{2,1,0:T(8,128)}, f32[1,192,64]{2,1,0:T(8,128)S(1)}, u32[]{:S(2)}) copy-start(f32[1,192,64]{2,1,0:T(8,128)S(1)} %copy.57) | copy-start | bytes 147460
  13.7 11.4 %copy-start.12 = (bf16[152,128]{1,0:T(8,128)(2,1)S(1)}, bf16[152,128]{1,0:T(8,128)(2,1)}, u32[]{:S(2)}) copy-start(bf16[152,128]{1,0:T(8,128)(2,1)} %param.36) | copy-start | bytes 116740
  13.7 11.4 %copy-start.13 = (bf16[152,128]{1,0:T(8,128)(2,1)S(1)}, bf16[152,128]{1,0:T(8,128)(2,1)}, u32[]{:S(2)}) copy-start(bf16[152,128]{1,0:T(8,128)(2,1)} %param.32) | copy-start | bytes 116740
  15.2 29.8 %copy-start.6 = (bf16[144,128]{1,0:T(8,128)(2,1)}, bf16[144,128]{1,0:T(8,128)(2,1)S(1)}, u32[]{:S(2)}) copy-start(bf16[144,128]{1,0:T(8,128)(2,1)S(1)} %concatenate.27.message_ref) | copy-start | bytes 110596
  16.9 28.1 %all-to-all-start = ((bf16[16,144,128]{2,1,0:T(8,128)(2,1)}), bf16[16,144,128]{2,1,0:T(8,128)(2,1)S(1)}, u32[]{:S(2)}, u32[]{:S(2)}) async-start(bf16[16,144,128]{2,1,0:T(8,128)(2,1)} %broadcast_in_dim.23), calls=%async_computation | async-start | bytes 1179648 | tf_op jit(solution)/shard_map/all_to_all | solution.py:362
  25.1 32.8 %copy-start.8 = (bf16[152,3,128]{2,0,1:T(8,128)(2,1)S(1)}, bf16[152,3,128]{2,0,1:T(8,128)(2,1)}, u32[]{:S(2)}) copy-start(bf16[152,3,128]{2,0,1:T(8,128)(2,1)} %param.31) | copy-start | bytes 350212
  25.1 32.8 %copy-start.9 = (bf16[152,3,128]{2,0,1:T(8,128)(2,1)S(1)}, bf16[152,3,128]{2,0,1:T(8,128)(2,1)}, u32[]{:S(2)}) copy-start(bf16[152,3,128]{2,0,1:T(8,128)(2,1)} %param.35) | copy-start | bytes 350212
  45.0 13.0 %copy-start = (bf16[16,144,128]{2,1,0:T(8,128)(2,1)}, bf16[16,144,128]{2,1,0:T(8,128)(2,1)S(1)}, u32[]{:S(2)}) copy-start(bf16[16,144,128]{2,1,0:T(8,128)(2,1)S(1)} %all-to-all-done.refs_1_) | copy-start | bytes 1769476
  45.9 19.9 %all-to-all-start.1 = ((f32[16,19,128]{2,1,0:T(8,128)}), f32[16,19,128]{2,1,0:T(8,128)S(1)}, u32[]{:S(2)}, u32[]{:S(2)}) async-start(f32[16,19,128]{2,1,0:T(8,128)} %broadcast_in_dim.24), calls=%async_computation.1 | async-start | bytes 393216 | tf_op jit(solution)/shard_map/all_to_all | solution.py:362
  57.8 81.4 %all-gather.6.cloned.1.call-start = ((), (), s32[]{:S(2)}) async-start(), calls=%async_computation.9 | async-start | bytes 4902912 | tf_op jit(solution)/shard_map/all_gather | solution.py:470
  65.8 2.7 %copy-start.5 = (f32[16,19,128]{2,1,0:T(8,128)}, f32[16,19,128]{2,1,0:T(8,128)S(1)}, u32[]{:S(2)}) copy-start(f32[16,19,128]{2,1,0:T(8,128)S(1)} %all-to-all-done.1.shares_ref) | copy-start | bytes 466948
  65.8 5.8 %collective-permute-start.1 = (bf16[7,152,128]{2,1,0:T(8,128)(2,1)S(1)}, bf16[7,152,128]{2,1,0:T(8,128)(2,1)S(1)}, u32[]{:S(2)}, u32[]{:S(2)}) collective-permute-start(bf16[7,152,128]{2,1,0:T(8,128)(2,1)S(1)} %get-tuple-element.49), channel_id=1, source_target_pairs={{32,0},{0,32},{33,1},{1,33},{34,2},{2,34},{35,3},{3,35},{36,4},{4,... | collective-permute-start | bytes 817160 | tf_op jit(solution)/shard_map/ppermute | solution.py:370
  76.9 7.0 %collective-permute-start.2 = (bf16[3,192,128]{2,1,0:T(8,128)(2,1)}, bf16[3,192,128]{2,1,0:T(8,128)(2,1)S(1)}, u32[]{:S(2)}, u32[]{:S(2)}) collective-permute-start(bf16[3,192,128]{2,1,0:T(8,128)(2,1)} %project.2.refs_3_), channel_id=1, source_target_pairs={{16,0},{0,16},{17,1},{1,17},{18,2},{2,18},{19,3},{3,19},{20,4},{4,... | collective-permute-start | bytes 442376 | tf_op jit(solution)/shard_map/ppermute | solution.py:370
  83.3 15.7 %copy-start.10 = (f32[1,192,64]{1,2,0:T(8,128)S(1)}, f32[1,192,64]{1,2,0:T(8,128)}, u32[]{:S(2)}) copy-start(f32[1,192,64]{1,2,0:T(8,128)} %param.21) | copy-start | bytes 147460
  94.0 20.1 %all-to-all-start.2 = ((bf16[8,48,608]{2,1,0:T(8,128)(2,1)}), bf16[8,48,608]{2,1,0:T(8,128)(2,1)S(1)}, u32[]{:S(2)}, u32[]{:S(2)}) async-start(bf16[8,48,608]{2,1,0:T(8,128)(2,1)} %attend.2), calls=%async_computation.2 | async-start | bytes 983040 | tf_op jit(solution)/shard_map/all_to_all | solution.py:362
  114.0 0.8 copy-start.2
  129.3 29.8 %all-to-all-start.4 = ((bf16[16,128,128]{2,1,0:T(8,128)(2,1)}), bf16[16,128,128]{2,1,0:T(8,128)(2,1)S(1)}, u32[]{:S(2)}, u32[]{:S(2)}) async-start(bf16[16,128,128]{2,1,0:T(8,128)(2,1)} %broadcast_in_dim.56), calls=%async_computation.4 | async-start | bytes 1048576 | tf_op jit(solution)/shard_map/all_to_all | solution.py:362
  159.0 0.8 copy-start.1
  170.5 13.6 %all-to-all-start.5 = ((bf16[8,48,608]{2,1,0:T(8,128)(2,1)}), bf16[8,48,608]{2,1,0:T(8,128)(2,1)S(1)}, u32[]{:S(2)}, u32[]{:S(2)}) async-start(bf16[8,48,608]{2,1,0:T(8,128)(2,1)} %attend.3), calls=%async_computation.5 | async-start | bytes 983040 | tf_op jit(solution)/shard_map/all_to_all | solution.py:362
  184.0 0.8 copy-start.3
  (1 other events, 0.7 us)
Sparse Core Ops, SparseCore 0:
  16.1 51.2 all-gather.3
  72.8 56.3 all-gather.5

commit v5 on v4

--- a/solution.py
+++ b/solution.py
@@ -460,14 +460,8 @@
 
     both = (pack(real_qkv, 0), pack(fake_qkv, 1))
     mine = jnp.where(core == 0, both[0], both[1])
-    peer = jnp.where(core == 0, both[1], both[0])
-    peer, mine, shares = lax.optimization_barrier((peer, mine, shares))
-    peer = shift(peer, "core", 2, 1)
-    second = jnp.concatenate([jnp.where(core == 0, mine, peer), jnp.where(core == 0, peer, mine)], axis=1)
     high1, low1, gram1 = prepare(shares, (jnp.float32(1.0),), student_in)
     first, gram1 = lax.optimization_barrier((first, gram1))
-    second, first = lax.optimization_barrier((second, first))
-    second = lax.all_gather(second, "y", axis=1, tiled=True)
     proj1 = project(jnp.zeros((2,), jnp.int32), high1, first)
     peer1 = shift(proj1, "xl", 2, 1)
     place, proj1 = lax.optimization_barrier((place, proj1))
@@ -475,6 +469,12 @@
         own_kernel, (one((OWN, BASIS), bf16), one((OWN, D), f32)), 1, place, own, (high1, 1, 0), (low1, 1, 0)
     )
     place, hidden = lax.optimization_barrier((place, hidden))
+    peer = jnp.where(core == 0, both[1], both[0])
+    peer, mine, hidden = lax.optimization_barrier((peer, mine, hidden))
+    peer = shift(peer, "core", 2, 1)
+    second = jnp.concatenate([jnp.where(core == 0, mine, peer), jnp.where(core == 0, peer, mine)], axis=1)
+    second, first = lax.optimization_barrier((second, first))
+    second = lax.all_gather(second, "y", axis=1, tiled=True)
     terms = attend(place, base, None, gram1, (proj1, peer1), 3, first)
     shares, terms = lax.optimization_barrier((shares, terms))
     high, low, gram = prepare(shares, (step_time, step_time), real_in, fake_in)

time: 225 us -> 232 us (1.031)
  waiting for transfers between devices: 25.1 us -> 29 us
    ppermute x3, waiting for transfers between devices: 0.64 us -> 5.8 us  [shift(): lax.ppermute(values, axis, [((i + step) % count, i) for i in range(count)])]
    unnamed x33 -> x35, local copies, waits for them, and re-layouts: 6.21 us -> 6.85 us
  transfers between devices with their start and end apart: 10 -> 10, of which waited for: 5 -> 6; matrix products, arithmetic and copies ran while one was open for 6% -> 5% of each run, Pallas kernels for 15% -> 11%
where the time goes in v5:
time: 232 us; the launch traced here: 230 us
  blocking collectives  72 us (31%)
  starting transfers between devices  48.9 us (21%)
  Pallas kernels  46.4 us (20%)
  waiting for transfers between devices  29 us (12%)
  between operations  15.1 us (7%)
  local copies, waits for them, and re-layouts  13 us (6%)
  other arithmetic  5.72 us (2%)
    all_to_all x5, starting transfers between devices, swap(): return lax.all_to_all(values, axes, 0, 0, tiled=False)  39.7 us
    all_to_all x3, blocking collectives, swap(): return lax.all_to_all(values, axes, 0, 0, tiled=False)  37.8 us
    all_to_all x5, waiting for transfers between devices, swap(): return lax.all_to_all(values, axes, 0, 0, tiled=False)  23.2 us
    pallas_call x2, Pallas kernels, attend(): pl.pallas_call(lambda *refs: attend_kernel(members, packed, wout_at, *ref...  19.9 us
    pallas_call x6, Pallas kernels, call(): pl.pallas_call(kernel, out_shape=shapes, grid=(1,), in_specs=[pl.BlockSpe...  18.9 us
    all_gather x1, blocking collectives, per_device(): out2 = lax.all_gather(out2, 'zh', axis=0, tiled=True)  18 us
    all_gather x1, blocking collectives, per_device(): proj2 = lax.all_gather(proj2, 'zh', axis=0, tiled=False)  16.2 us
    ppermute x3, starting transfers between devices, shift(): lax.ppermute(values, axis, [((i + step) % count, i) for i in range(count)])  9.15 us
  transfers between devices with their start and end apart: 10, of which 6 were waited for; matrix products, arithmetic and copies ran while one was open for 5% of the time, Pallas kernels for 11%

profile of v5, /device:TPU:1, one launch (start us, length us, event | category | flops | bytes accessed | tf_op | source)
XLA Modules:
  0.0 230.4 jit_solution(6840103195638703780)
XLA Ops:
  6.5 4.1 %collective-permute-start = (bf16[152,128]{1,0:T(8,128)(2,1)}, bf16[152,128]{1,0:T(8,128)(2,1)S(1)}, u32[]{:S(2)}, u32[]{:S(2)}) collective-permute-start(bf16[152,128]{1,0:T(8,128)(2,1)} %param.28), channel_id=1, source_target_pairs={{16,0},{0,16},{17,1},{1,17},{18,2},{2,18},{19,3},{3,19},{20,4},{4,... | collective-permute-start | bytes 116744 | tf_op jit(solution)/shard_map/ppermute | solution.py:370
  16.9 8.2 %all-to-all-start = ((bf16[16,144,128]{2,1,0:T(8,128)(2,1)}), bf16[16,144,128]{2,1,0:T(8,128)(2,1)S(1)}, u32[]{:S(2)}, u32[]{:S(2)}) async-start(bf16[16,144,128]{2,1,0:T(8,128)(2,1)} %broadcast_in_dim.23), calls=%async_computation | async-start | bytes 1179648 | tf_op jit(solution)/shard_map/all_to_all | solution.py:362
  26.5 18.0 %all_gather.15 = bf16[8,152,128]{2,1,0:T(8,128)(2,1)S(1)} all-gather(bf16[2,152,128]{2,1,0:T(8,128)(2,1)S(1)} %pad_maximum_fusion.4), channel_id=1, replica_groups=mesh['y'=8,'core'=2,'xl'=2,'zh'=4,'zp'=2,'rep'=2] {'zh'}, dimensions={0}, use_global_device_ids=true | all-gather | bytes 389120 | tf_op jit(solution)/shard_map/all_gather | solution.py:436
  46.0 11.9 %all-to-all-start.1 = ((f32[16,19,128]{2,1,0:T(8,128)}), f32[16,19,128]{2,1,0:T(8,128)S(1)}, u32[]{:S(2)}, u32[]{:S(2)}) async-start(f32[16,19,128]{2,1,0:T(8,128)} %broadcast_in_dim.24), calls=%async_computation.1 | async-start | bytes 393216 | tf_op jit(solution)/shard_map/all_to_all | solution.py:362
  58.2 7.8 %all-to-all-done.1.shares_ref = f32[16,19,128]{2,1,0:T(8,128)S(1)} async-done(((f32[16,19,128]{2,1,0:T(8,128)}), f32[16,19,128]{2,1,0:T(8,128)S(1)}, u32[]{:S(2)}, u32[]{:S(2)}) %all-to-all-start.1) | async-done | bytes 155680 | tf_op jit(solution)/shard_map/all_to_all | solution.py:362
  66.6 3.0 %prepare_kernel.2 = (bf16[1,192,2432]{2,1,0:T(8,128)(2,1)}, bf16[1,192,2432]{2,1,0:T(8,128)(2,1)}, f32[1,192,192]{2,1,0:T(8,128)}) custom-call(bf16[112,2432]{1,0:T(8,128)(2,1)} %constant.88.clone.high_ref, bf16[112,2432]{1,0:T(8,128)(2,1)} %constant.89.clone.low_ref, f32[1,2432]{1,0:T(1,128)} %stack.53.time_ref, f32[16,19,128]{2,1,0:T(8,128)} %copy-done.5, ...), custom_call_target="tpu_custom_call" | custom-call | flops 1000000000 | bytes 10000000 | tf_op jit(solution)/shard_map/prepare_kernel/pallas_call | solution.py:349
  70.2 3.8 %project.2.refs_3_ = bf16[3,192,128]{2,1,0:T(8,128)(2,1)} custom-call(s32[2]{0:T(128)} %broadcast_5_pick_ref.2.pick_ref, bf16[1,192,2432]{2,1,0:T(8,128)(2,1)} %get-tuple-element.45.hid_ref.high_ref, bf16[5,2432,128]{2,1,0:T(8,128)(2,1)} %all-gather.4.cloned.1.call-done.w_ref.refs_5_), custom_call_target="tpu_custom_call" | custom-call | flops 358612992 | bytes 3000000 | tf_op jit(solution)/shard_map/project/pallas_call | solution.py:95
  81.5 3.0 %collective-permute-start.1 = (bf16[3,192,128]{2,1,0:T(8,128)(2,1)S(1)}, bf16[3,192,128]{2,1,0:T(8,128)(2,1)S(1)}, u32[]{:S(2)}, u32[]{:S(2)}) collective-permute-start(bf16[3,192,128]{2,1,0:T(8,128)(2,1)S(1)} %copy-done.6), channel_id=1, source_target_pairs={{16,0},{0,16},{17,1},{1,17},{18,2},{2,18},{19,3},{3,19},{20,4},{4,... | collective-permute-start | bytes 442376 | tf_op jit(solution)/shard_map/ppermute | solution.py:370
  84.5 4.3 %collective-permute-done.1.refs_4_ = bf16[3,192,128]{2,1,0:T(8,128)(2,1)S(1)} collective-permute-done((bf16[3,192,128]{2,1,0:T(8,128)(2,1)S(1)}, bf16[3,192,128]{2,1,0:T(8,128)(2,1)S(1)}, u32[]{:S(2)}, u32[]{:S(2)}) %collective-permute-start.1) | collective-permute-done | bytes 147488 | tf_op jit(solution)/shard_map/ppermute | solution.py:370
  89.5 9.3 %attend.2 = bf16[8,48,608]{2,1,0:T(8,128)(2,1)} custom-call(s32[5]{0:T(128)} %stack.52.place_ref.refs_0_.after_ref, bf16[16,144,128]{2,1,0:T(8,128)(2,1)} %copy-done, f32[1,192,192]{2,1,0:T(8,128)} %get-tuple-element.54.refs_2_, bf16[3,192,128]{2,1,0:T(8,128)(2,1)} %project.2.refs_3_, bf16[3,192,128]{2,1,0:T(8,128)(2,1)} %copy-done.15, ...), custom_call_target="tpu_custom_call" | custom-call | flops 4000000000 | bytes 10000000 | tf_op jit(solution)/shard_map/attend/pallas_call | solution.py:245
  98.8 6.9 %all-to-all-start.2 = ((bf16[8,48,608]{2,1,0:T(8,128)(2,1)}), bf16[8,48,608]{2,1,0:T(8,128)(2,1)S(1)}, u32[]{:S(2)}, u32[]{:S(2)}) async-start(bf16[8,48,608]{2,1,0:T(8,128)(2,1)} %attend.2), calls=%async_computation.2 | async-start | bytes 983040 | tf_op jit(solution)/shard_map/all_to_all | solution.py:362
  107.9 4.0 %prepare_kernel.3 = (bf16[2,192,2432]{2,1,0:T(8,128)(2,1)}, bf16[2,192,2432]{2,1,0:T(8,128)(2,1)}, f32[2,192,192]{2,1,0:T(8,128)}) custom-call(bf16[112,2432]{1,0:T(8,128)(2,1)} %constant.88.clone.high_ref, bf16[112,2432]{1,0:T(8,128)(2,1)} %constant.89.clone.low_ref, f32[2,2432]{1,0:T(2,128)} %pad_maximum_fusion.6.time_ref, f32[16,19,128]{2,1,0:T(8,128)} %copy-done.5, ...), custom_call_target="tpu_custom_call" | custom-call | flops 1000000000 | bytes 10000000 | tf_op jit(solution)/shard_map/prepare_kernel/pallas_call | solution.py:349
  111.9 9.6 %all-to-all-done.2.recv_ref = bf16[8,48,608]{2,1,0:T(8,128)(2,1)S(1)} async-done(((bf16[8,48,608]{2,1,0:T(8,128)(2,1)}), bf16[8,48,608]{2,1,0:T(8,128)(2,1)S(1)}, u32[]{:S(2)}, u32[]{:S(2)}) %all-to-all-start.2) | async-done | bytes 466976 | tf_op jit(solution)/shard_map/all_to_all | solution.py:362
  122.3 2.9 %student_kernel.1 = (f32[12,64]{1,0:T(8,128)}, f32[12,64]{1,0:T(8,128)}, bf16[12,192]{1,0:T(8,128)(2,1)}, bf16[8,128]{1,0:T(8,128)(2,1)}) custom-call(s32[5]{0:T(128)} %stack.52.place_ref.refs_0_.after_ref, f32[1]{0:T(128)} %bitcast.1.time_ref, bf16[8,48,608]{2,1,0:T(8,128)(2,1)} %copy-done.2, f32[12,2432]{1,0:T(8,128)} %get-tuple-element.65.hidden_ref, ...), custom_call_target="tpu_custom_call" | custom-call | flops 1000000000 | bytes 10000000 | tf_op jit(solution)/shard_map/student_kernel/pallas_call | solution.py:349
  125.8 9.9 %all_to_all.40 = bf16[16,8,128]{2,1,0:T(8,128)(2,1)S(1)} all-to-all(bf16[16,8,128]{2,1,0:T(8,128)(2,1)S(1)} %broadcast_in_dim.26), channel_id=1, replica_groups=mesh['y'=8,'core'=2,'xl'=2,'zh'=4,'zp'=2,'rep'=2] {'xl','zh','zp'}, dimensions={0} | all-to-all | bytes 65536 | tf_op jit(solution)/shard_map/all_to_all | solution.py:362
  136.7 8.1 %all-to-all-start.4 = ((bf16[16,128,128]{2,1,0:T(8,128)(2,1)}), bf16[16,128,128]{2,1,0:T(8,128)(2,1)S(1)}, u32[]{:S(2)}, u32[]{:S(2)}) async-start(bf16[16,128,128]{2,1,0:T(8,128)(2,1)} %broadcast_in_dim.56), calls=%async_computation.4 | async-start | bytes 1048576 | tf_op jit(solution)/shard_map/all_to_all | solution.py:362
  145.3 3.8 %project.3 = bf16[3,192,128]{2,1,0:T(8,128)(2,1)} custom-call(s32[2]{0:T(128)} %pad_add_fusion.pick_ref, bf16[2,192,2432]{2,1,0:T(8,128)(2,1)} %get-tuple-element.72.hid_ref.high_ref, bf16[7,2432,128]{2,1,0:T(8,128)(2,1)} %all-gather.6.cloned.1.call-done.w_ref.refs_5_), custom_call_target="tpu_custom_call" | custom-call | flops 358612992 | bytes 3000000 | tf_op jit(solution)/shard_map/project/pallas_call | solution.py:95
  149.1 16.2 %all-gather = bf16[12,192,128]{2,1,0:T(8,128)(2,1)} all-gather(bf16[3,192,128]{2,1,0:T(8,128)(2,1)} %project.3), channel_id=2, replica_groups=mesh['y'=8,'core'=2,'xl'=2,'zh'=4,'zp'=2,'rep'=2] {'zh'}, dimensions={0}, use_global_device_ids=true | all-gather | bytes 737280 | tf_op jit(solution)/shard_map/all_gather | solution.py:500
  166.1 10.6 %attend.3 = bf16[8,48,608]{2,1,0:T(8,128)(2,1)} custom-call(s32[5]{0:T(128)} %stack.52.place_ref.refs_0_.after_ref, bf16[16,144,128]{2,1,0:T(8,128)(2,1)} %copy-done, bf16[2048,128]{1,0:T(8,128)(2,1)} %bitcast.53, f32[2,192,192]{2,1,0:T(8,128)} %get-tuple-element.67.gram_ref.refs_3_, bf16[4,3,192,128]{3,2,1,0:T(8,128)(2,1)} %bitcast.52, ...), custom_call_target="tpu_custom_call" | custom-call | flops 8000000000 | bytes 10000000 | tf_op jit(solution)/shard_map/attend/pallas_call | solution.py:245
  176.7 4.6 %all-to-all-start.5 = ((bf16[8,48,608]{2,1,0:T(8,128)(2,1)}), bf16[8,48,608]{2,1,0:T(8,128)(2,1)S(1)}, u32[]{:S(2)}, u32[]{:S(2)}) async-start(bf16[8,48,608]{2,1,0:T(8,128)(2,1)} %attend.3), calls=%async_computation.5 | async-start | bytes 983040 | tf_op jit(solution)/shard_map/all_to_all | solution.py:362
  181.3 3.5 %scores_own_kernel.1.hidden_ref = f32[2,12,2432]{2,1,0:T(8,128)} custom-call(s32[5]{0:T(128)} %stack.52.place_ref.refs_0_.after_ref, bf16[12,192]{1,0:T(8,128)(2,1)} %get-tuple-element.77.x12_ref, bf16[2,192,2432]{2,1,0:T(8,128)(2,1)} %get-tuple-element.72.hid_ref.high_ref, bf16[2,192,2432]{2,1,0:T(8,128)(2,1)} %get-tuple-element.78.low_ref), custom_call_target="tpu_custom_call" | custom-call | flops 1000000000 | bytes 10000000 | tf_op jit(solution)/shard_map/scores_own_kernel/pallas_call | solution.py:349
  184.8 5.3 %all-to-all-done.5.recv_ref = bf16[8,48,608]{2,1,0:T(8,128)(2,1)S(1)} async-done(((bf16[8,48,608]{2,1,0:T(8,128)(2,1)}), bf16[8,48,608]{2,1,0:T(8,128)(2,1)S(1)}, u32[]{:S(2)}, u32[]{:S(2)}) %all-to-all-start.5) | async-done | bytes 466976 | tf_op jit(solution)/shard_map/all_to_all | solution.py:362
  193.4 11.9 %all_to_all.41 = f32[16,8,128]{2,1,0:T(8,128)S(1)} all-to-all(f32[16,8,128]{2,1,0:T(8,128)} %score_kernel.1), channel_id=1, replica_groups=mesh['y'=8,'core'=2,'xl'=2,'zh'=4,'zp'=2,'rep'=2] {'xl','zh','zp'}, dimensions={0} | all-to-all | bytes 131072 | tf_op jit(solution)/shard_map/all_to_all | solution.py:362
  205.3 16.0 %all_to_all.42 = f32[16,1,128]{2,1,0:T(1,128)S(1)} all-to-all(f32[16,1,128]{2,1,0:T(1,128)S(1)} %broadcast_in_dim.57), channel_id=1, replica_groups=mesh['y'=8,'core'=2,'xl'=2,'zh'=4,'zp'=2,'rep'=2] {'y','core'}, dimensions={0} | all-to-all | bytes 16384 | tf_op jit(solution)/shard_map/all_to_all | solution.py:362
  (93 shorter events, 28.6 us)
Async XLA Ops:
  6.5 8.7 %copy-start.12 = (bf16[152,128]{1,0:T(8,128)(2,1)S(1)}, bf16[152,128]{1,0:T(8,128)(2,1)}, u32[]{:S(2)}) copy-start(bf16[152,128]{1,0:T(8,128)(2,1)} %param.28) | copy-start | bytes 116740
  6.5 8.7 %copy-start.8 = (bf16[152,3,128]{2,0,1:T(8,128)(2,1)S(1)}, bf16[152,3,128]{2,0,1:T(8,128)(2,1)}, u32[]{:S(2)}) copy-start(bf16[152,3,128]{2,0,1:T(8,128)(2,1)} %param.27) | copy-start | bytes 350212
  6.5 63.1 %all-gather.4.cloned.1.call-start = ((), (), s32[]{:S(2)}) async-start(), calls=%async_computation.8 | async-start | bytes 3307520 | tf_op jit(solution)/shard_map/all_gather | solution.py:446
  6.5 8.7 %collective-permute-start = (bf16[152,128]{1,0:T(8,128)(2,1)}, bf16[152,128]{1,0:T(8,128)(2,1)S(1)}, u32[]{:S(2)}, u32[]{:S(2)}) collective-permute-start(bf16[152,128]{1,0:T(8,128)(2,1)} %param.28), channel_id=1, source_target_pairs={{16,0},{0,16},{17,1},{1,17},{18,2},{2,18},{19,3},{3,19},{20,4},{4,... | collective-permute-start | bytes 116744 | tf_op jit(solution)/shard_map/ppermute | solution.py:370
  11.6 5.4 %copy-start.4 = (f32[1,192,64]{2,1,0:T(8,128)}, f32[1,192,64]{2,1,0:T(8,128)S(1)}, u32[]{:S(2)}) copy-start(f32[1,192,64]{2,1,0:T(8,128)S(1)} %copy.57) | copy-start | bytes 147460
  13.8 12.8 %copy-start.13 = (bf16[152,128]{1,0:T(8,128)(2,1)S(1)}, bf16[152,128]{1,0:T(8,128)(2,1)}, u32[]{:S(2)}) copy-start(bf16[152,128]{1,0:T(8,128)(2,1)} %param.36) | copy-start | bytes 116740
  13.8 12.8 %copy-start.14 = (bf16[152,128]{1,0:T(8,128)(2,1)S(1)}, bf16[152,128]{1,0:T(8,128)(2,1)}, u32[]{:S(2)}) copy-start(bf16[152,128]{1,0:T(8,128)(2,1)} %param.32) | copy-start | bytes 116740
  15.3 29.9 %copy-start.7 = (bf16[144,128]{1,0:T(8,128)(2,1)}, bf16[144,128]{1,0:T(8,128)(2,1)S(1)}, u32[]{:S(2)}) copy-start(bf16[144,128]{1,0:T(8,128)(2,1)S(1)} %concatenate.27.message_ref) | copy-start | bytes 110596
  16.9 28.1 %all-to-all-start = ((bf16[16,144,128]{2,1,0:T(8,128)(2,1)}), bf16[16,144,128]{2,1,0:T(8,128)(2,1)S(1)}, u32[]{:S(2)}, u32[]{:S(2)}) async-start(bf16[16,144,128]{2,1,0:T(8,128)(2,1)} %broadcast_in_dim.23), calls=%async_computation | async-start | bytes 1179648 | tf_op jit(solution)/shard_map/all_to_all | solution.py:362
  25.2 32.8 %copy-start.9 = (bf16[152,3,128]{2,0,1:T(8,128)(2,1)S(1)}, bf16[152,3,128]{2,0,1:T(8,128)(2,1)}, u32[]{:S(2)}) copy-start(bf16[152,3,128]{2,0,1:T(8,128)(2,1)} %param.31) | copy-start | bytes 350212
  25.2 32.8 %copy-start.10 = (bf16[152,3,128]{2,0,1:T(8,128)(2,1)S(1)}, bf16[152,3,128]{2,0,1:T(8,128)(2,1)}, u32[]{:S(2)}) copy-start(bf16[152,3,128]{2,0,1:T(8,128)(2,1)} %param.35) | copy-start | bytes 350212
  45.0 13.1 %copy-start = (bf16[16,144,128]{2,1,0:T(8,128)(2,1)}, bf16[16,144,128]{2,1,0:T(8,128)(2,1)S(1)}, u32[]{:S(2)}) copy-start(bf16[16,144,128]{2,1,0:T(8,128)(2,1)S(1)} %all-to-all-done.refs_1_) | copy-start | bytes 1769476
  46.0 19.9 %all-to-all-start.1 = ((f32[16,19,128]{2,1,0:T(8,128)}), f32[16,19,128]{2,1,0:T(8,128)S(1)}, u32[]{:S(2)}, u32[]{:S(2)}) async-start(f32[16,19,128]{2,1,0:T(8,128)} %broadcast_in_dim.24), calls=%async_computation.1 | async-start | bytes 393216 | tf_op jit(solution)/shard_map/all_to_all | solution.py:362
  57.9 87.4 %all-gather.6.cloned.1.call-start = ((), (), s32[]{:S(2)}) async-start(), calls=%async_computation.9 | async-start | bytes 4902912 | tf_op jit(solution)/shard_map/all_gather | solution.py:477
  76.9 4.6 %copy-start.6 = (bf16[3,192,128]{2,1,0:T(8,128)(2,1)S(1)}, bf16[3,192,128]{2,1,0:T(8,128)(2,1)}, u32[]{:S(2)}) copy-start(bf16[3,192,128]{2,1,0:T(8,128)(2,1)} %project.2.refs_3_) | copy-start | bytes 442372
  76.9 3.6 %collective-permute-start.2 = (bf16[7,152,128]{2,1,0:T(8,128)(2,1)S(1)}, bf16[7,152,128]{2,1,0:T(8,128)(2,1)S(1)}, u32[]{:S(2)}, u32[]{:S(2)}) collective-permute-start(bf16[7,152,128]{2,1,0:T(8,128)(2,1)S(1)} %get-tuple-element.59), channel_id=1, source_target_pairs={{32,0},{0,32},{33,1},{1,33},{34,2},{2,34},{35,3},{3,35},{36,4},{4,... | collective-permute-start | bytes 817160 | tf_op jit(solution)/shard_map/ppermute | solution.py:370
  81.5 25.0 %copy-start.11 = (f32[1,192,64]{1,2,0:T(8,128)S(1)}, f32[1,192,64]{1,2,0:T(8,128)}, u32[]{:S(2)}) copy-start(f32[1,192,64]{1,2,0:T(8,128)} %param.21) | copy-start | bytes 147460
  81.5 7.3 %collective-permute-start.1 = (bf16[3,192,128]{2,1,0:T(8,128)(2,1)S(1)}, bf16[3,192,128]{2,1,0:T(8,128)(2,1)S(1)}, u32[]{:S(2)}, u32[]{:S(2)}) collective-permute-start(bf16[3,192,128]{2,1,0:T(8,128)(2,1)S(1)} %copy-done.6), channel_id=1, source_target_pairs={{16,0},{0,16},{17,1},{1,17},{18,2},{2,18},{19,3},{3,19},{20,4},{4,... | collective-permute-start | bytes 442376 | tf_op jit(solution)/shard_map/ppermute | solution.py:370
  98.8 22.8 %all-to-all-start.2 = ((bf16[8,48,608]{2,1,0:T(8,128)(2,1)}), bf16[8,48,608]{2,1,0:T(8,128)(2,1)S(1)}, u32[]{:S(2)}, u32[]{:S(2)}) async-start(bf16[8,48,608]{2,1,0:T(8,128)(2,1)} %attend.2), calls=%async_computation.2 | async-start | bytes 983040 | tf_op jit(solution)/shard_map/all_to_all | solution.py:362
  121.6 0.8 copy-start.2
  136.7 28.6 %all-to-all-start.4 = ((bf16[16,128,128]{2,1,0:T(8,128)(2,1)}), bf16[16,128,128]{2,1,0:T(8,128)(2,1)S(1)}, u32[]{:S(2)}, u32[]{:S(2)}) async-start(bf16[16,128,128]{2,1,0:T(8,128)(2,1)} %broadcast_in_dim.56), calls=%async_computation.4 | async-start | bytes 1048576 | tf_op jit(solution)/shard_map/all_to_all | solution.py:362
  165.3 0.8 copy-start.1
  176.7 13.3 %all-to-all-start.5 = ((bf16[8,48,608]{2,1,0:T(8,128)(2,1)}), bf16[8,48,608]{2,1,0:T(8,128)(2,1)S(1)}, u32[]{:S(2)}, u32[]{:S(2)}) async-start(bf16[8,48,608]{2,1,0:T(8,128)(2,1)} %attend.3), calls=%async_computation.5 | async-start | bytes 983040 | tf_op jit(solution)/shard_map/all_to_all | solution.py:362
  190.0 0.8 copy-start.3
  (2 other events, 1.3 us)
Sparse Core Ops, SparseCore 0:
  16.2 51.2 all-gather.3
  81.6 57.3 all-gather.5
